TPU v7x, 32 devices: a whole 2x2x4 slice. The times are simulated.
32 devices in a mesh: grid: 4 (over x, core), mark: 8 (over z, y).
Axes of the slice: x: 2, y: 2, z: 4, core: 2. Of those that a mesh axis runs over, the one named last changes fastest.
Arguments:
- velocity: float32 [3, 128, 128, 256], P(None, 'grid', 'mark'), may hold values from -6 to 6
- pressure: float32 [128, 128, 256], P('grid', 'mark'), may hold values from -6 to 6
- cell_visc: float32 [128, 128, 256], P('grid', 'mark'), may hold values from 0.2 to 5
- cell_dens: float32 [128, 128, 256], P('grid', 'mark'), may hold values from 0.5 to 1.5
- block_brick: int32 [256, 48], P(('grid', 'mark')), may hold values from 0 to 1023
- block_counts: int32 [32, 8], P(('grid', 'mark')), may hold values from 0 to 48, as said below
- positions: float32 [256, 3, 48, 256], P(('grid', 'mark')), may hold values from 0 to 1
- start_visc: float32 [256, 48, 256], P(('grid', 'mark')), may hold values from 0.2 to 5
- marker_dens: float32 [256, 48, 256], P(('grid', 'mark')), may hold values from 0.5 to 1.5
Outputs:
- velocity_next: float32 [3, 128, 128, 256], P(None, 'grid', 'mark')
- pressure_next: float32 [128, 128, 256], P('grid', 'mark')
- visc_next: float32 [128, 128, 256], P('grid', 'mark')
- dens_next: float32 [128, 128, 256], P('grid', 'mark')
- marker_visc: float32 [256, 48, 256], P(('grid', 'mark'))
Inputs may be any that keep to these rules, and one draw needn't show every extreme that they name: `block_counts`: entry q of a marker device's row counts its live slots toward the grid device of mark index q in its group; in every group some grid device gets exactly 48 live slots from every marker device. `block_brick`: dead slots name bricks too.
All inputs are finite; a program needn't handle non-finite values.
Results may differ from a plain program's by a relative error of at most 0.0003.
Values sent between devices are 32-bit elements; how exact they have to be, the bound alone decides.
No kernel may reach another device: no remote copies, remote signals or barrier semaphores. Data moves between devices by JAX's collectives and lax.ppermute only.
A program may use at most 128 MiB of HBM per device.

v0:
```python
import functools

import jax
import jax.numpy as jnp
import numpy as np
from jax import lax
from jax.experimental import pallas as pl
from jax.experimental.pallas import tpu as pltpu
from jax.sharding import PartitionSpec as P

SWEEPS = 4
RELAX = 0.6
PRESSURE_RATE = 0.25
GRAVITY = 1.0
STRAIN_SCALE = 0.5

BX, BY, BZ = 4, 4, 8
PLANE = BX * BY
ROWS = 3 * PLANE
LANES = 128
GROUP = LANES // BZ
HALF = 8
SUBLANES = 8

f32, bf16 = jnp.float32, jnp.bfloat16


def vmem_limit(mib):
    return pltpu.CompilerParams(vmem_limit_bytes=mib * 1024 * 1024)


def cost(microseconds):
    return pl.CostEstimate(
        flops=int(microseconds * 1.15e9), bytes_accessed=0, transcendentals=0
    )


def place_of(brick):
    return lax.shift_right_logical(brick, GROUP.bit_length() - 1), (brick & (GROUP - 1)) * BZ


def pick_body(asked, vel, out, table):
    size_x, size_y, size_z = vel.shape[1:]
    bricks_y, halves = size_y // BY, size_z // LANES

    def repack(block_x, carry):
        for block_y in range(bricks_y):
            for half in range(halves):
                place = (block_x * bricks_y + block_y) * halves + half
                for c in range(3):
                    for i in range(BX):
                        row = (c * BX + i) * BY
                        table[place, row : row + BY, :] = vel[
                            c,
                            block_x * BX + i,
                            block_y * BY : (block_y + 1) * BY,
                            half * LANES : (half + 1) * LANES,
                        ]
        return carry

    lax.fori_loop(0, size_x // BX, repack, 0)
    groups = out.shape[1]
    lane_slot = lax.broadcasted_iota(jnp.int32, (ROWS, LANES), 1) // BZ

    def one_group(step, carry):
        device, group = step // groups, step % groups
        packed = jnp.zeros((ROWS, LANES), f32)
        for slot in range(GROUP):
            place, lane = place_of(asked[device, group * GROUP + slot])
            rolled = pltpu.roll(table[place], (BZ * slot - lane) & (LANES - 1), 1)
            packed = jnp.where(lane_slot == slot, rolled, packed)
        out[device, group] = packed
        return carry

    lax.fori_loop(0, out.shape[0] * groups, one_group, 0)


def pick_bricks(asked, velocity):
    devices, slots = asked.shape
    size_x, size_y, size_z = velocity.shape[1:]
    places = (size_x // BX) * (size_y // BY) * (size_z // LANES)
    return pl.pallas_call(
        pick_body,
        out_shape=jax.ShapeDtypeStruct((devices, slots // GROUP, ROWS, LANES), f32),
        in_specs=[
            pl.BlockSpec(memory_space=pltpu.SMEM),
            pl.BlockSpec(memory_space=pltpu.VMEM),
        ],
        out_specs=pl.BlockSpec(memory_space=pltpu.VMEM),
        scratch_shapes=[pltpu.VMEM((places, ROWS, LANES), f32)],
        compiler_params=vmem_limit(24),
        cost_estimate=cost(25),
        name="pick_bricks",
    )(asked, velocity)


def permutations():
    inside = BZ * HALF
    spread = np.zeros((2, 2, LANES, 4 * inside), np.float32)
    gather = np.zeros((2 * BY * inside, BY * LANES), np.float32)
    for half in range(2):
        for slot in range(HALF):
            for z in range(BZ):
                outer, inner = (half * HALF + slot) * BZ + z, z * HALF + slot
                for part in range(4):
                    spread[half, part // 2, outer, part * inside + inner] = 1
                for j in range(BY):
                    gather[(half * BY + j) * inside + inner, j * LANES + outer] = 1
    return jnp.asarray(spread, bf16), jnp.asarray(gather, bf16)


def split(value):
    high = value.astype(bf16)
    return high, (value - high.astype(f32)).astype(bf16)


def add_all(values):
    return functools.reduce(jnp.add, values)


def axis_weights(fraction, cells):
    middle = (cells - 1) / 2
    base = jnp.exp(fraction * (2.0 * cells) - float(cells))
    powers = [None, base]
    for i in range(2, cells):
        powers.append(powers[i // 2] * powers[i - i // 2])
    factors = [float(np.exp(middle**2 - (i - middle) ** 2)) for i in range(cells)]
    bells = [None] + [powers[i] * factors[i] for i in range(1, cells)]
    scale = 1.0 / (add_all(bells[1:]) + factors[0])
    weights = [scale * factors[0]] + [bell * scale for bell in bells[1:]]
    mean = add_all(
        [
            (weights[cells - 1 - i] - weights[i]) * (2.0 * (middle - i))
            for i in range(cells // 2)
        ]
    )
    slopes = [w * (2.0 * (i - middle) - mean) for i, w in enumerate(weights)]
    return weights, slopes


def dot(a, b):
    return jnp.dot(a, b, preferred_element_type=f32)


def gradients(products, weights, markers):
    weight_x, slope_x, weight_y, slope_y = ([weights[4 * n + i] for i in range(4)] for n in range(4))
    grads = []
    for c in range(3):
        lines = [[], [], []]
        for i in range(BX):
            rows = [((c * BX + i) * BY + j) * HALF for j in range(BY)]
            still = [products[row : row + HALF, :markers] for row in rows]
            rising = [products[row : row + HALF, markers:] for row in rows]
            lines[0].append(slope_x[i] * add_all([w * t for w, t in zip(weight_y, still)]))
            lines[1].append(weight_x[i] * add_all([w * t for w, t in zip(slope_y, still)]))
            lines[2].append(weight_x[i] * add_all([w * t for w, t in zip(weight_y, rising)]))
        grads.append([add_all(line) for line in lines])
    return grads


def own_lanes():
    shape = (HALF, 4 * BZ * HALF)
    lane = lax.broadcasted_iota(jnp.int32, shape, 1)
    return (lane % HALF == lax.broadcasted_iota(jnp.int32, shape, 0)).astype(f32)


def marker_groups(groups, counts, ins, outs, buffers, sums):
    spread, gather, places, start, dens, brick = ins
    visc_out, moments_out = outs
    permuted, left, right, products, weights, factors, planes_high, planes_low = buffers
    markers = places.shape[-1]
    inside = BZ * HALF
    own = own_lanes()
    halves = [
        (owner, 2 * group + half, half, 2 * n + half)
        for n, (owner, group) in enumerate(groups)
        for half in range(2)
    ]
    parts = [split(brick[owner, group]) for owner, group in groups]
    for _, _, half, n in halves:
        high, low = parts[n // 2]
        permuted[n][...] = dot(high, spread[half, 0]) + dot(low, spread[half, 1])
    heights = []
    for owner, part, _, n in halves:
        weight_z, slope_z = axis_weights(places[owner, 2, part], BZ)
        heights.append(weight_z)
        for z in range(0, BZ, 2):
            for column, values in ((0, weight_z), (1, slope_z)):
                high, low = split(jnp.concatenate(values[z : z + 2], axis=0))
                columns = slice(column * markers, (column + 1) * markers)
                for k in range(4):
                    begin = k * inside + z * HALF
                    right[n][begin : begin + 2 * HALF, columns] = low if k % 2 else high
    for _, _, _, n in halves:
        for row in range(0, ROWS, 2):
            pair = [
                jnp.broadcast_to(permuted[n][r : r + 1, :], own.shape) * own for r in (row, row + 1)
            ]
            left[n][row * HALF : (row + 2) * HALF, :] = jnp.concatenate(pair, axis=0).astype(bf16)
    for _, _, _, n in halves:
        products[n][...] = dot(left[n][...], right[n][...])
    for owner, part, _, n in halves:
        weights_x = axis_weights(places[owner, 0, part], BX)
        weights_y = axis_weights(places[owner, 1, part], BY)
        for k, values in enumerate((*weights_x, *weights_y)):
            for i, value in enumerate(values):
                weights[n][4 * k + i] = value
        for j in range(BY):
            for z in range(0, BZ, 2):
                pair = [weights_y[0][j] * heights[n][z + k] for k in range(2)]
                rows = slice((j * BZ + z) * HALF, (j * BZ + z + 2) * HALF)
                high, low = split(jnp.concatenate(pair, axis=0))
                planes_high[n][rows, :] = high
                planes_low[n][rows, :] = low

    count = 3 * BX * HALF
    for owner, part, _, n in halves:
        grads = gradients(products[n], weights[n], markers)
        normal = grads[0][0] ** 2 + grads[1][1] ** 2 + grads[2][2] ** 2
        shear_xy = 0.5 * (grads[0][1] + grads[1][0])
        shear_xz = 0.5 * (grads[0][2] + grads[2][0])
        shear_yz = 0.5 * (grads[1][2] + grads[2][1])
        invariant = 0.5 * normal + shear_xy**2 + shear_xz**2 + shear_yz**2
        scaled = invariant * (1.0 / (STRAIN_SCALE * STRAIN_SCALE))
        third = jnp.log(1.0 + scaled) * (1.0 / 3.0)
        first = start[owner, part]
        slot = lax.broadcasted_iota(jnp.int32, first.shape, 0) + part * HALF
        live = slot < counts[0, owner]
        visc_out[owner, part] = jnp.where(live, first * jnp.exp(-third), 0.0)
        carried = (
            live.astype(f32),
            jnp.where(live, jnp.log(first) - third, 0.0),
            jnp.where(live, dens[owner, part], 0.0),
        )
        for c in range(3):
            for i in range(0, BX, 2):
                pair = [carried[c] * weights[n][i + k] for k in range(2)]
                row = (c * BX + i) * HALF
                high, low = split(jnp.concatenate(pair, axis=0))
                factors[n][row : row + 2 * HALF, :] = high
                factors[n][count + row : count + row + 2 * HALF, :] = low

    contract = (((1,), (1,)), ((), ()))
    found = []
    for _, _, _, n in halves:
        both = lax.dot_general(
            factors[n][...], planes_high[n][...], contract, preferred_element_type=f32
        )
        rest = lax.dot_general(
            factors[n][:count], planes_low[n][...], contract, preferred_element_type=f32
        )
        found.append((both, rest))
    for _, _, half, n in halves:
        both, rest = found[n]
        total = both[:count] + both[count:] + rest
        chosen = total.reshape(3 * BX, HALF, BY * inside) * own[None]
        high, low = split(jnp.sum(chosen, axis=1))
        columns = slice(half * BY * inside, (half + 1) * BY * inside)
        row = (n // 2) * 32
        sums[row : row + 3 * BX, columns] = high.astype(f32)
        sums[row + 16 : row + 16 + 3 * BX, columns] = low.astype(f32)
    moved = dot(sums[...].astype(bf16), gather[...])
    for n, (owner, group) in enumerate(groups):
        mine = moved[32 * n : 32 * n + 3 * BX] + moved[32 * n + 16 : 32 * n + 16 + 3 * BX]
        for j in range(BY):
            rows = pl.ds(j, 3 * BX, stride=BY)
            moments_out[owner, group, rows, :] = mine[:, j * LANES : (j + 1) * LANES]


TOGETHER = 2


def marker_body(counts, *refs):
    ins, outs, scratch = refs[:6], refs[7:9], refs[9:]
    listed, sums, *flat = scratch
    held = 2 * TOGETHER
    buffers = [flat[n * held : (n + 1) * held] for n in range(len(flat) // held)]
    visc_out, moments_out = outs
    owners, groups = moments_out.shape[:2]
    visc_out[...] = jnp.zeros_like(visc_out)
    moments_out[...] = jnp.zeros_like(moments_out)
    sums[...] = jnp.zeros_like(sums)

    def list_groups(index, number):
        owner, group = index // groups, index % groups
        live = group * GROUP < counts[0, owner]

        @pl.when(live)
        def _():
            for n in range(TOGETHER):
                listed[2 * (number + n)] = owner
                listed[2 * (number + n) + 1] = group

        return jnp.where(live, number + 1, number)

    number = lax.fori_loop(0, owners * groups, list_groups, 0)

    def step(index, carry):
        first = TOGETHER * index
        taken = [
            (listed[2 * (first + n)], listed[2 * (first + n) + 1]) for n in range(TOGETHER)
        ]
        marker_groups(taken, counts, ins, outs, buffers, sums)
        return carry

    lax.fori_loop(0, (number + TOGETHER - 1) // TOGETHER, step, 0)


def marker_work(counts, positions, start_visc, marker_dens, bricks, after):
    owners, _, slots, markers = positions.shape
    groups, parts = slots // GROUP, slots // HALF
    spread, gather = permutations()
    width = 4 * BZ * HALF
    whole = pl.BlockSpec(memory_space=pltpu.VMEM)
    buffers = (
        pltpu.VMEM((ROWS, width), f32),
        pltpu.VMEM((ROWS * HALF, width), bf16),
        pltpu.VMEM((width, 2 * markers), bf16),
        pltpu.VMEM((ROWS * HALF, 2 * markers), f32),
        pltpu.VMEM((4 * 4, HALF, markers), f32),
        pltpu.VMEM((2 * 3 * BX * HALF, markers), bf16),
        pltpu.VMEM((BY * BZ * HALF, markers), bf16),
        pltpu.VMEM((BY * BZ * HALF, markers), bf16),
    )
    visc, moments = pl.pallas_call(
        marker_body,
        out_shape=(
            jax.ShapeDtypeStruct((owners, parts, HALF, markers), f32),
            jax.ShapeDtypeStruct((owners, groups, ROWS, LANES), f32),
        ),
        in_specs=[pl.BlockSpec(memory_space=pltpu.SMEM)]
        + [whole] * 6
        + [pl.BlockSpec(memory_space=pl.ANY)],
        out_specs=(whole, whole),
        scratch_shapes=[
            pltpu.SMEM((2 * (owners * groups + TOGETHER),), jnp.int32),
            pltpu.VMEM((32 * TOGETHER, 2 * BY * BZ * HALF), f32),
        ]
        + [buffer for buffer in buffers for _ in range(2 * TOGETHER)],
        compiler_params=vmem_limit(60),
        cost_estimate=cost(25),
        name="marker_work",
    )(
        counts,
        spread,
        gather,
        positions.reshape(owners, 3, parts, HALF, markers),
        start_visc.reshape(owners, parts, HALF, markers),
        marker_dens.reshape(owners, parts, HALF, markers),
        bricks,
        after,
    )
    return visc.reshape(owners, slots, markers), moments


def settle_body(asked, moments_in, visc_in, dens_in, visc_out, dens_out, *scratch):
    moments, visc, dens, done, *tables = scratch
    size_x, size_y, size_z = visc.shape
    copies = [
        pltpu.make_async_copy(there, here, done.at[n])
        for n, (there, here) in enumerate(
            ((moments_in, moments), (visc_in, visc), (dens_in, dens))
        )
    ]
    for copy in copies:
        copy.start()
    bricks_y, halves = size_y // BY, size_z // LANES
    for table in tables:
        table[...] = jnp.zeros_like(table)
    copies[0].wait()
    groups = moments.shape[1]
    lane_slot = lax.broadcasted_iota(jnp.int32, (ROWS, LANES), 1) // BZ

    def one_group(step, carry):
        device, group = step // groups, step % groups
        packed = moments[device, group]
        for slot in range(GROUP):
            table = tables[slot % len(tables)]
            place, lane = place_of(asked[device, group * GROUP + slot])
            piece = jnp.where(lane_slot == slot, packed, 0.0)
            piece = pltpu.roll(piece, (lane - BZ * slot) & (LANES - 1), 1)
            table[place] = table[place] + piece
        return carry

    lax.fori_loop(0, moments.shape[0] * groups, one_group, 0)
    copies[1].wait()
    copies[2].wait()

    def finish(block_x, carry):
        for block_y in range(0, bricks_y, 2):
            for half in range(halves):
                for i in range(BX):
                    here = (
                        block_x * BX + i,
                        slice(block_y * BY, (block_y + 2) * BY),
                        slice(half * LANES, (half + 1) * LANES),
                    )
                    sums = []
                    for c in range(3):
                        rows = slice((c * BX + i) * BY, (c * BX + i + 1) * BY)
                        places = [
                            (block_x * bricks_y + block_y + k) * halves + half for k in range(2)
                        ]
                        sums.append(
                            jnp.concatenate(
                                [add_all([t[place, rows, :] for t in tables]) for place in places]
                            )
                        )
                    scale = 1.0 / (sums[0] + 1.0)
                    visc_out[here] = jnp.exp((sums[1] + jnp.log(visc[here])) * scale)
                    dens_out[here] = (sums[2] + dens[here]) * scale
        return carry

    lax.fori_loop(0, size_x // BX, finish, 0)


def settle(asked, moments, cell_visc, cell_dens):
    size_x, size_y, size_z = cell_visc.shape
    places = (size_x // BX) * (size_y // BY) * (size_z // LANES)
    whole = pl.BlockSpec(memory_space=pltpu.VMEM)
    shape = jax.ShapeDtypeStruct(cell_visc.shape, f32)
    return pl.pallas_call(
        settle_body,
        out_shape=(shape, shape),
        in_specs=[pl.BlockSpec(memory_space=pltpu.SMEM)]
        + [pl.BlockSpec(memory_space=pl.ANY)] * 3,
        out_specs=(whole, whole),
        scratch_shapes=[
            pltpu.VMEM(moments.shape, f32),
            pltpu.VMEM(cell_visc.shape, f32),
            pltpu.VMEM(cell_visc.shape, f32),
            pltpu.SemaphoreType.DMA((3,)),
        ]
        + [pltpu.VMEM((places, ROWS, LANES), f32)] * 2,
        compiler_params=vmem_limit(24),
        cost_estimate=cost(7),
        name="settle",
    )(asked, moments, cell_visc, cell_dens)


def field_of(fields, index):
    return fields[0].at[index] if index < 3 else fields[index - 2]


def pack_x_body(*refs):
    ends, outs = refs[:8], refs[8:]
    for side in range(2):
        for f in range(6):
            outs[side][f] = field_of(ends[side::2], f)[...]


def pack_x(velocity, pressure, cell_visc, cell_dens):
    size_x, size_y, size_z = cell_visc.shape
    width = SWEEPS
    ends = (0, size_x // width - 1)
    vel = [
        pl.BlockSpec((3, width, size_y, size_z), lambda i, e=e: (0, e, 0, 0)) for e in ends
    ]
    block = [pl.BlockSpec((width, size_y, size_z), lambda i, e=e: (e, 0, 0)) for e in ends]
    whole = pl.BlockSpec((6, width, size_y, size_z), lambda i: (0, 0, 0, 0))
    shape = jax.ShapeDtypeStruct((6, width, size_y, size_z), f32)
    return pl.pallas_call(
        pack_x_body,
        grid=(1,),
        out_shape=(shape, shape),
        in_specs=vel + block * 3,
        out_specs=(whole, whole),
        compiler_params=vmem_limit(60),
        cost_estimate=cost(2),
        name="pack_x",
    )(velocity, velocity, pressure, pressure, cell_visc, cell_visc, cell_dens, cell_dens)


def corner_rows(upward, size_x):
    width = SWEEPS
    spare = (5 * width,) if upward else (4 * width - 1, 6 * width - 1)
    places = [(plane, row) for plane in range(size_x) for row in spare]
    found = []
    for field in range(6):
        for side in range(2):
            near = field == 5 or (field == 3 and side == 1 and not upward)
            reach = width - 1 if near else width
            for far_x in range(1, width):
                for far_y in range(1, reach - far_x + 1):
                    found.append((field, side, far_x, far_y))
    more = max(0, len(found) - len(places))
    places += [(size_x + n // (6 * width), n % (6 * width)) for n in range(more)]
    return [cell + at for cell, at in zip(found, places)], size_x + -(-more // (6 * width))


def pack_y_body(size_x, vel, pres, visc, dens, low_x, high_x, upward, downward):
    step_x, size_y, _ = pres.shape
    width = SWEEPS
    step = pl.program_id(0)
    planes = pl.ds(pl.multiple_of(step * step_x, step_x), step_x)
    for f in range(6):
        field = field_of((vel, pres, visc, dens), f)
        rows = slice(f * width, (f + 1) * width)
        upward[planes, rows, :] = field[:, size_y - width :, :]
        downward[planes, rows, :] = field[:, :width, :]

    @pl.when(step == pl.num_programs(0) - 1)
    def _():
        for up, face in ((True, upward), (False, downward)):
            for f, side, far_x, far_y, plane, row in corner_rows(up, size_x)[0]:
                halo, at = (high_x, far_x - 1) if side else (low_x, width - far_x)
                face[plane, row] = halo[f, at, size_y - far_y if up else far_y - 1]


def pack_y(velocity, pressure, cell_visc, cell_dens, low_x, high_x):
    size_x, size_y, size_z = cell_visc.shape
    step = 8
    block = pl.BlockSpec((step, size_y, size_z), lambda i: (i, 0, 0))
    halo = pl.BlockSpec(low_x.shape, lambda i: (0, 0, 0, 0))
    shapes = [(corner_rows(up, size_x)[1], 6 * SWEEPS, size_z) for up in (True, False)]
    return pl.pallas_call(
        functools.partial(pack_y_body, size_x),
        grid=(size_x // step,),
        out_shape=tuple(jax.ShapeDtypeStruct(shape, f32) for shape in shapes),
        in_specs=[
            pl.BlockSpec((3, step, size_y, size_z), lambda i: (0, i, 0, 0)),
            block,
            block,
            block,
            halo,
            halo,
        ],
        out_specs=tuple(pl.BlockSpec(shape, lambda i: (0, 0, 0)) for shape in shapes),
        compiler_params=vmem_limit(24),
        cost_estimate=cost(15),
        name="pack_y",
    )(velocity, pressure, cell_visc, cell_dens, low_x, high_x)


def place(per, x, y, rows):
    return x % per, pl.ds(y * SUBLANES + x // per, rows, stride=SUBLANES)


def put(target, x, y, rows, value):
    per, halves = target.shape[:2]
    plane, lines = place(per, x, y, rows)
    for half in range(halves):
        target[plane, half, lines, :] = value[:, half * LANES : (half + 1) * LANES]


def tile(y):
    if isinstance(y, int):
        return pl.ds(y * SUBLANES, SUBLANES)
    return pl.ds(pl.multiple_of(y * SUBLANES, SUBLANES), SUBLANES)


def row_work(cells, coefs, relax, forcing, rate):
    per, halves = cells.shape[1:3]
    lane = lax.broadcasted_iota(jnp.int32, (SUBLANES, LANES), 1)
    at_first, at_last = lane == 0, lane == LANES - 1

    def take(field, plane, y):
        return jnp.concatenate([field[plane, half, tile(y), :] for half in range(halves)], axis=1)

    def store(field, plane, y, value):
        for half in range(halves):
            field[plane, half, tile(y), :] = value[:, half * LANES : (half + 1) * LANES]

    def up_x(field, plane, y):
        if plane < per - 1:
            return take(field, plane + 1, y)
        return pltpu.roll(take(field, 0, y), SUBLANES - 1, 0)

    def down_x(field, plane, y):
        if plane > 0:
            return take(field, plane - 1, y)
        return pltpu.roll(take(field, per - 1, y), 1, 0)

    def rolled(a, shift):
        return [
            pltpu.roll(a[:, half * LANES : (half + 1) * LANES], shift, 1) for half in range(halves)
        ]

    def up_z(a):
        parts = rolled(a, LANES - 1)
        after = parts[1:] + [jnp.zeros_like(parts[0])]
        return jnp.concatenate([jnp.where(at_last, n, p) for p, n in zip(parts, after)], axis=1)

    def down_z(a):
        parts = rolled(a, 1)
        before = [jnp.zeros_like(parts[0])] + parts[:-1]
        return jnp.concatenate([jnp.where(at_first, b, p) for p, b in zip(parts, before)], axis=1)

    def prepare(y):
        visc, dens = cells.at[0], cells.at[1]
        for plane in range(per):
            here = take(visc, plane, y)
            near = [
                up_x(visc, plane, y),
                down_x(visc, plane, y),
                take(visc, plane, y + 1),
                take(visc, plane, y - 1),
                up_z(here),
                down_z(here),
            ]
            links = [0.5 * (here + other) for other in near]
            scale = jnp.where(here > 0.0, RELAX / add_all(links), 0.0)
            for n in range(6):
                coefs[n, plane, tile(y), :] = links[n] * scale
            relax[plane, tile(y), :] = scale
            forcing[plane, tile(y), :] = take(dens, plane, y) * (-GRAVITY * scale)
            rate[plane, tile(y), :] = PRESSURE_RATE * here

    def sweep(y, old, new):
        for plane in range(per):
            links = [coefs[n, plane, tile(y), :] for n in range(6)]
            scale = relax[plane, tile(y), :]
            pressure = take(old.at[3], plane, y)
            before = (
                down_x(old.at[3], plane, y),
                take(old.at[3], plane, y - 1),
                down_z(pressure),
            )
            changes = []
            for c in range(3):
                field = old.at[c]
                here = take(field, plane, y)
                near = [
                    up_x(field, plane, y),
                    down_x(field, plane, y),
                    take(field, plane, y + 1),
                    take(field, plane, y - 1),
                    up_z(here),
                    down_z(here),
                ]
                terms = [link * other for link, other in zip(links, near)]
                total = (terms[0] + terms[1]) + (terms[2] + terms[3])
                total = total + (terms[4] + terms[5])
                rest = (1.0 - RELAX) * here - scale * (pressure - before[c])
                if c == 2:
                    rest = rest + forcing[plane, tile(y), :]
                changes.append(near[2 * c] - here)
                store(new.at[c], plane, y, total + rest)
            pressed = pressure - rate[plane, tile(y), :] * add_all(changes)
            store(new.at[3], plane, y, pressed)

    return prepare, sweep


def kept_rows(size_y):
    width = SWEEPS
    return (
        ((width, size_y),),
        ((width + 1, width), (size_y - 1, width)),
        ((width, width + 1), (size_y - 1, width + 1)),
    )


def kept_copies(pairs, size_y, done):
    copies = []
    for (source, target), strips in zip(pairs, kept_rows(size_y)):
        for begin, rows in strips:
            span = (slice(None),) * 3 + (pl.ds(begin * SUBLANES, rows * SUBLANES),)
            copies.append(
                pltpu.make_async_copy(source.at[span], target.at[span], done.at[len(copies)])
            )
    return copies


def inner_body(vel, pres, visc, dens, low_x, high_x, _, even_out, odd_out, cells_out, *work):
    blocks, sides_x, even, odd, cells, coefs, relax, forcing, rate, done = work
    size_x, size_y, size_z = blocks.shape[1:]
    width = SWEEPS
    inputs = (
        (visc, blocks.at[4], (4,)),
        (vel, blocks.at[0:3], (0, 1, 2)),
        (pres, blocks.at[3], (3,)),
        (dens, blocks.at[5], (5,)),
        (low_x, sides_x.at[0], ()),
        (high_x, sides_x.at[1], ()),
    )
    copies = [
        pltpu.make_async_copy(there, here, done.at[n]) for n, (there, here, _) in enumerate(inputs)
    ]
    for copy in copies:
        copy.start()
    targets = [even.at[n] for n in range(4)] + [cells.at[n] for n in range(2)]
    for copy, (_, _, held) in zip(copies, inputs):
        copy.wait()
        for f in held:
            for i in range(size_x):
                for y in range(0, size_y, SUBLANES):
                    value = blocks[f, i, y : y + SUBLANES, :]
                    put(targets[f], i + width, y + width, SUBLANES, value)
    for side, begin in enumerate((0, width + size_x)):
        for f in range(6):
            for i in range(width):
                for y in range(0, size_y, SUBLANES):
                    value = sides_x[side, f, i, y : y + SUBLANES, :]
                    put(targets[f], begin + i, y + width, SUBLANES, value)

    prepare, sweep = row_work(cells, coefs, relax, forcing, rate)

    def prepare_row(y, carry):
        prepare(y)
        return carry

    first, last = width + 1, width + size_y - 1
    lax.fori_loop(first, last, prepare_row, 0, unroll=2)
    for step in range(SWEEPS):
        old, new = (odd, even) if step % 2 else (even, odd)

        def sweep_row(y, carry, old=old, new=new):
            sweep(y, old, new)
            return carry

        lax.fori_loop(first + step, last - step, sweep_row, 0, unroll=2)
    sends = kept_copies(((even, even_out), (odd, odd_out), (cells, cells_out)), size_y, done)
    for send in sends:
        send.start()
    for send in sends:
        send.wait()


def inner_sweeps(velocity, pressure, cell_visc, cell_dens, low_x, high_x, after):
    size_x, size_y, size_z = cell_visc.shape
    width = low_x.shape[1]
    per, rows = (size_x + 2 * width) // SUBLANES, (size_y + 2 * width) * SUBLANES
    block, cut = (per, rows, size_z), (per, size_z // LANES, rows, LANES)
    shapes = [(4,) + cut, (4,) + cut, (2,) + cut]
    anywhere = pl.BlockSpec(memory_space=pl.ANY)
    return pl.pallas_call(
        inner_body,
        out_shape=tuple(jax.ShapeDtypeStruct(shape, f32) for shape in shapes),
        in_specs=[anywhere] * 7,
        out_specs=(anywhere,) * 3,
        scratch_shapes=[
            pltpu.VMEM((6,) + cell_visc.shape, f32),
            pltpu.VMEM((2,) + low_x.shape, f32),
        ]
        + [pltpu.VMEM(shape, f32) for shape in shapes]
        + [
            pltpu.VMEM((6,) + block, f32),
            pltpu.VMEM(block, f32),
            pltpu.VMEM(block, f32),
            pltpu.VMEM(block, f32),
            pltpu.SemaphoreType.DMA((6,)),
        ],
        compiler_params=vmem_limit(40),
        cost_estimate=cost(25),
        name="inner_sweeps",
    )(velocity, pressure, cell_visc, cell_dens, low_x, high_x, after)


def edge_body(even_in, odd_in, cells_in, low_y, high_y, vel_out, pres_out, *work):
    from_low, from_high, results, even, odd, cells, coefs, relax, forcing, rate, done, more = work
    size_x, size_y, size_z = results.shape[1:]
    width = SWEEPS
    long_y = size_y + 2 * width
    halos = [
        pltpu.make_async_copy(low_y, from_low, more.at[0]),
        pltpu.make_async_copy(high_y, from_high, more.at[1]),
    ]
    kept = kept_copies(((even_in, even), (odd_in, odd), (cells_in, cells)), size_y, done)
    for copy in (*halos, *kept[3:], *kept[:3]):
        copy.start()
    targets = [even.at[n] for n in range(4)] + [cells.at[n] for n in range(2)]
    for target in targets:
        for x in (*range(width), *range(width + size_x, size_x + 2 * width)):
            for y in (0, width + size_y):
                put(target, x, y, width, jnp.zeros((width, size_z), f32))
    for up, halo, copy, begin in (
        (True, from_low, halos[0], 0),
        (False, from_high, halos[1], width + size_y),
    ):
        copy.wait()
        for f, target in enumerate(targets):
            rows = slice(f * width, (f + 1) * width)
            for i in range(size_x):
                put(target, i + width, begin, width, halo[i, rows, :])
        for f, side, far_x, far_y, plane, row in corner_rows(up, size_x)[0]:
            x = width + size_x - 1 + far_x if side else width - far_x
            y = width - far_y if up else width + size_y - 1 + far_y
            put(targets[f], x, y, 1, halo[plane, row : row + 1, :])
    for copy in kept:
        copy.wait()

    prepare, sweep = row_work(cells, coefs, relax, forcing, rate)

    def prepare_rows(n, carry):
        prepare(1 + n)
        prepare(long_y - 2 * width + n)
        return carry

    lax.fori_loop(0, 2 * width - 1, prepare_rows, 0)
    for step in range(SWEEPS):
        old, new = (odd, even) if step % 2 else (even, odd)

        def sweep_rows(n, carry, old=old, new=new, step=step):
            sweep(1 + step + n, old, new)
            sweep(width + size_y - 1 - step + n, old, new)
            return carry

        lax.fori_loop(0, width, sweep_rows, 0)

    final = odd if SWEEPS % 2 else even
    outs = [vel_out.at[0], vel_out.at[1], vel_out.at[2], pres_out]
    sends = [pltpu.make_async_copy(results.at[n], out, done.at[n]) for n, out in enumerate(outs)]
    per, halves = even.shape[1:3]
    for field, send in enumerate(sends):
        for i in range(size_x):
            for y in range(0, size_y, SUBLANES):
                plane, lines = place(per, i + width, y + width, SUBLANES)
                for half in range(halves):
                    columns = slice(half * LANES, (half + 1) * LANES)
                    results[field, i, y : y + SUBLANES, columns] = final[
                        field, plane, half, lines, :
                    ]
        send.start()
    for send in sends:
        send.wait()


def edge_sweeps(even, odd, cells, low_y, high_y, size_x, size_y):
    per, halves, rows = even.shape[1:4]
    size_z = halves * LANES
    block = (per, rows, size_z)
    anywhere = pl.BlockSpec(memory_space=pl.ANY)
    return pl.pallas_call(
        edge_body,
        out_shape=(
            jax.ShapeDtypeStruct((3, size_x, size_y, size_z), f32),
            jax.ShapeDtypeStruct((size_x, size_y, size_z), f32),
        ),
        in_specs=[anywhere] * 5,
        out_specs=(anywhere,) * 2,
        scratch_shapes=[
            pltpu.VMEM(low_y.shape, f32),
            pltpu.VMEM(high_y.shape, f32),
            pltpu.VMEM((4, size_x, size_y, size_z), f32),
            pltpu.VMEM(even.shape, f32),
            pltpu.VMEM(odd.shape, f32),
            pltpu.VMEM(cells.shape, f32),
            pltpu.VMEM((6,) + block, f32),
            pltpu.VMEM(block, f32),
            pltpu.VMEM(block, f32),
            pltpu.VMEM(block, f32),
            pltpu.SemaphoreType.DMA((5,)),
            pltpu.SemaphoreType.DMA((2,)),
        ],
        compiler_params=vmem_limit(40),
        cost_estimate=cost(1),
        name="edge_sweeps",
    )(even, odd, cells, low_y, high_y)


def shift(value, axis, step):
    size = lax.axis_size(axis)
    pairs = [(i, i + step) for i in range(size) if 0 <= i + step < size]
    return lax.ppermute(value, axis, pairs)


def per_device(
    velocity,
    pressure,
    cell_visc,
    cell_dens,
    block_brick,
    block_counts,
    positions,
    start_visc,
    marker_dens,
):
    asked = lax.all_to_all(block_brick, "mark", 0, 0, tiled=True)
    fields = (velocity, pressure, cell_visc, cell_dens)
    to_low, to_high = pack_x(*fields)
    low_x, high_x = shift(to_high, "grid", 1), shift(to_low, "grid", -1)
    upward, downward = pack_y(*fields, low_x, high_x)
    low_y, high_y = shift(upward, "mark", 1), shift(downward, "mark", -1)

    picked = pick_bricks(asked, velocity)
    bricks = lax.all_to_all(picked, "mark", 0, 0, tiled=True)
    marker_visc, moments = marker_work(
        block_counts, positions, start_visc, marker_dens, bricks, upward
    )
    gathered = lax.all_to_all(moments, "mark", 0, 0, tiled=True)
    state = inner_sweeps(*fields, low_x, high_x, moments)
    velocity_next, pressure_next = edge_sweeps(*state, low_y, high_y, *pressure.shape[:2])
    visc_next, dens_next = settle(asked, gathered, cell_visc, cell_dens)
    return velocity_next, pressure_next, visc_next, dens_next, marker_visc


def solution(mesh):
    in_specs = (
        P(None, "grid", "mark", None),
        P("grid", "mark", None),
        P("grid", "mark", None),
        P("grid", "mark", None),
        P(("grid", "mark"), None),
        P(("grid", "mark"), None),
        P(("grid", "mark"), None, None, None),
        P(("grid", "mark"), None, None),
        P(("grid", "mark"), None, None),
    )
    out_specs = (
        P(None, "grid", "mark", None),
        P("grid", "mark", None),
        P("grid", "mark", None),
        P("grid", "mark", None),
        P(("grid", "mark"), None, None),
    )
    return jax.shard_map(
        per_device, mesh=mesh, in_specs=in_specs, out_specs=out_specs, check_vma=False
    )
```

profile of v0, /device:TPU:18, one launch (start us, length us, event | category | flops | bytes accessed | tf_op | source)
XLA Modules:
  0.0 97.5 jit_solution(7549068179967700515)
XLA Ops:
  0.6 6.2 %all-to-all-start = ((s32[8,1,48]{2,1,0:T(1,128)}), s32[8,1,48]{2,1,0:T(1,128)S(1)}, u32[]{:S(2)}, u32[]{:S(2)}) async-start(s32[8,1,48]{2,1,0:T(1,128)} %bitcast.8), calls=%async_computation | async-start | bytes 8192 | tf_op jit(solution)/shard_map/all_to_all | solution.py:869
  6.8 2.2 %pack_x.1 = (f32[6,4,16,256]{3,2,1,0:T(8,128)}, f32[6,4,16,256]{3,2,1,0:T(8,128)}) custom-call(f32[3,32,16,256]{3,2,1,0:T(8,128)} %vel.5, f32[3,32,16,256]{3,2,1,0:T(8,128)} %vel.5, f32[32,16,256]{2,1,0:T(8,128)} %pres.3, f32[32,16,256]{2,1,0:T(8,128)} %pres.3, f32[32,16,256]{2,1,0:T(8,128)} %visc_in.1, f32[32,16,256]{2,1,0:T(8,128)} %visc_in.1, ...), custom_call_target="tpu_custom_call" | custom-call | flops 2300000000 | tf_op jit(solution)/shard_map/pack_x/pallas_call | solution.py:462
  9.0 1.9 %collective-permute-start = (f32[6,4,16,256]{3,2,1,0:T(8,128)}, f32[6,4,16,256]{3,2,1,0:T(8,128)S(1)}, u32[]{:S(2)}, u32[]{:S(2)}) collective-permute-start(f32[6,4,16,256]{3,2,1,0:T(8,128)} %get-tuple-element.18), channel_id=1, source_target_pairs={{0,8},{8,16},{16,24},{1,9},{9,17},{17,25},{2,10},{10,18},{18,26},{... | collective-permute-start | bytes 1179656 | tf_op jit(solution)/shard_map/ppermute | solution.py:855
  10.9 3.6 %collective-permute-start.1 = (f32[6,4,16,256]{3,2,1,0:T(8,128)}, f32[6,4,16,256]{3,2,1,0:T(8,128)S(1)}, u32[]{:S(2)}, u32[]{:S(2)}) collective-permute-start(f32[6,4,16,256]{3,2,1,0:T(8,128)} %get-tuple-element.19), channel_id=1, source_target_pairs={{8,0},{16,8},{24,16},{9,1},{17,9},{25,17},{10,2},{18,10},{26,18},{... | collective-permute-start | bytes 1179656 | tf_op jit(solution)/shard_map/ppermute | solution.py:855
  14.6 6.0 %pick_bricks.1 = f32[8,3,48,128]{3,2,1,0:T(8,128)} custom-call(s32[8,48]{1,0:T(8,128)S(1)} %bitcast.6, f32[3,32,16,256]{3,2,1,0:T(8,128)S(1)} %copy-done.1), custom_call_target="tpu_custom_call" | custom-call | flops 28750000128 | tf_op jit(solution)/shard_map/pick_bricks/pallas_call | solution.py:82
  20.5 6.0 %all-to-all-start.1 = ((f32[8,3,48,128]{3,2,1,0:T(8,128)}), f32[8,3,48,128]{3,2,1,0:T(8,128)}, u32[]{:S(2)}, u32[]{:S(2)}) async-start(f32[8,3,48,128]{3,2,1,0:T(8,128)} %pick_bricks.1), calls=%async_computation.1 | async-start | bytes 1179648 | tf_op jit(solution)/shard_map/all_to_all | solution.py:877
  27.3 1.0 %copy-done.6 = f32[32,16,256]{2,1,0:T(8,128)S(1)} copy-done((f32[32,16,256]{2,1,0:T(8,128)S(1)}, f32[32,16,256]{2,1,0:T(8,128)}, u32[]{:S(2)}) %copy-start.6) | copy-done | bytes 524312
  28.3 1.0 %copy-done.9 = f32[32,16,256]{2,1,0:T(8,128)S(1)} copy-done((f32[32,16,256]{2,1,0:T(8,128)S(1)}, f32[32,16,256]{2,1,0:T(8,128)}, u32[]{:S(2)}) %copy-start.9) | copy-done | bytes 524312
  29.4 1.0 %copy-done.13 = f32[6,4,16,256]{3,2,1,0:T(8,128)S(1)} copy-done((f32[6,4,16,256]{3,2,1,0:T(8,128)S(1)}, f32[6,4,16,256]{3,2,1,0:T(8,128)}, u32[]{:S(2)}) %copy-start.13) | copy-done | bytes 393240
  30.4 1.5 %pack_y.1 = (f32[34,24,256]{2,1,0:T(8,128)S(1)}, f32[32,24,256]{2,1,0:T(8,128)}) custom-call(f32[3,32,16,256]{3,2,1,0:T(8,128)S(1)} %copy-done.1, f32[32,16,256]{2,1,0:T(8,128)S(1)} %copy-done.4, f32[32,16,256]{2,1,0:T(8,128)S(1)} %copy-done.6, f32[32,16,256]{2,1,0:T(8,128)S(1)} %copy-done.9, f32[6,4,16,256]{3,2,1,0:T(8,128)S(1)} %collective-permute-done.low_x, ...), custom_call_target="tpu_custom_call" | custom-call | flops 17250000896 | tf_op jit(solution)/shard_map/pack_y/pallas_call | solution.py:516
  31.8 3.4 %collective-permute-start.2 = (f32[34,24,256]{2,1,0:T(8,128)S(1)}, f32[34,24,256]{2,1,0:T(8,128)S(1)}, u32[]{:S(2)}, u32[]{:S(2)}) collective-permute-start(f32[34,24,256]{2,1,0:T(8,128)S(1)} %get-tuple-element.20.refs_6_), channel_id=1, source_target_pairs={{0,1},{1,2},{2,3},{3,4},{4,5},{5,6},{6,7},{8,9},{9,10},{10,11},{11... | collective-permute-start | bytes 2506760 | tf_op jit(solution)/shard_map/ppermute | solution.py:855
  35.2 3.4 %collective-permute-start.3 = (f32[32,24,256]{2,1,0:T(8,128)}, f32[32,24,256]{2,1,0:T(8,128)S(1)}, u32[]{:S(2)}, u32[]{:S(2)}) collective-permute-start(f32[32,24,256]{2,1,0:T(8,128)} %get-tuple-element.25), channel_id=1, source_target_pairs={{1,0},{2,1},{3,2},{4,3},{5,4},{6,5},{7,6},{9,8},{10,9},{11,10},{12... | collective-permute-start | bytes 2359304 | tf_op jit(solution)/shard_map/ppermute | solution.py:855
  38.6 0.9 all-to-all-done.1.refs_5_
  39.5 12.6 %marker_work.1 = (f32[8,6,8,256]{3,2,1,0:T(8,128)}, f32[8,3,48,128]{3,2,1,0:T(8,128)}) custom-call(s32[1,8]{1,0:T(1,128)} %counts.1, bf16[2,2,128,256]{3,2,1,0:T(8,128)(2,1)} %constant.4.clone.refs_0_, bf16[512,512]{1,0:T(8,128)(2,1)} %constant.5.clone.refs_1_, f32[8,3,6,8,256]{4,3,2,1,0:T(8,128)} %bitcast.9, f32[8,6,8,256]{3,2,1,0:T(8,128)} %bitcast.10, ...), custom_call_target="tpu_custom_call" | custom-call | flops 28750000128 | tf_op jit(solution)/shard_map/marker_work/pallas_call | solution.py:325
  52.1 14.3 %all-to-all-start.2 = ((f32[8,3,48,128]{3,2,1,0:T(8,128)}), f32[8,3,48,128]{3,2,1,0:T(8,128)S(1)}, u32[]{:S(2)}, u32[]{:S(2)}) async-start(f32[8,3,48,128]{3,2,1,0:T(8,128)} %get-tuple-element.21._), calls=%async_computation.2 | async-start | bytes 1179648 | tf_op jit(solution)/shard_map/all_to_all | solution.py:881
  66.4 1.1 %copy-done = f32[8,3,48,128]{3,2,1,0:T(8,128)S(1)} copy-done((f32[8,3,48,128]{3,2,1,0:T(8,128)S(1)}, f32[8,3,48,128]{3,2,1,0:T(8,128)}, u32[]{:S(2)}) %copy-start) | copy-done | bytes 589848
  67.5 1.4 %copy-done.2 = f32[3,32,16,256]{3,2,1,0:T(8,128)S(1)} copy-done((f32[3,32,16,256]{3,2,1,0:T(8,128)S(1)}, f32[3,32,16,256]{3,2,1,0:T(8,128)}, u32[]{:S(2)}) %copy-start.2) | copy-done | bytes 1572888
  68.9 1.0 %copy-done.5 = f32[32,16,256]{2,1,0:T(8,128)S(1)} copy-done((f32[32,16,256]{2,1,0:T(8,128)S(1)}, f32[32,16,256]{2,1,0:T(8,128)}, u32[]{:S(2)}) %copy-start.5) | copy-done | bytes 524312
  70.0 1.0 %copy-done.7 = f32[32,16,256]{2,1,0:T(8,128)S(1)} copy-done((f32[32,16,256]{2,1,0:T(8,128)S(1)}, f32[32,16,256]{2,1,0:T(8,128)}, u32[]{:S(2)}) %copy-start.7) | copy-done | bytes 524312
  71.0 1.0 %copy-done.10 = f32[32,16,256]{2,1,0:T(8,128)S(1)} copy-done((f32[32,16,256]{2,1,0:T(8,128)S(1)}, f32[32,16,256]{2,1,0:T(8,128)}, u32[]{:S(2)}) %copy-start.10) | copy-done | bytes 524312
  72.0 1.0 %copy-done.14 = f32[6,4,16,256]{3,2,1,0:T(8,128)S(1)} copy-done((f32[6,4,16,256]{3,2,1,0:T(8,128)S(1)}, f32[6,4,16,256]{3,2,1,0:T(8,128)}, u32[]{:S(2)}) %copy-start.14) | copy-done | bytes 393240
  73.0 9.4 %inner_sweeps.1 = (f32[4,5,2,192,128]{4,3,2,1,0:T(8,128)S(1)}, f32[4,5,2,192,128]{4,3,2,1,0:T(8,128)S(1)}, f32[2,5,2,192,128]{4,3,2,1,0:T(8,128)S(1)}) custom-call(f32[3,32,16,256]{3,2,1,0:T(8,128)S(1)} %copy-done.2, f32[32,16,256]{2,1,0:T(8,128)S(1)} %copy-done.5, f32[32,16,256]{2,1,0:T(8,128)S(1)} %copy-done.7, f32[32,16,256]{2,1,0:T(8,128)S(1)} %copy-done.10, ...), custom_call_target="tpu_custom_call" | custom-call | flops 28750000128 | tf_op jit(solution)/shard_map/inner_sweeps/pallas_call | solution.py:727
  82.5 8.1 %edge_sweeps.1 = (f32[3,32,16,256]{3,2,1,0:T(8,128)}, f32[32,16,256]{2,1,0:T(8,128)}) custom-call(f32[4,5,2,192,128]{4,3,2,1,0:T(8,128)S(1)} %get-tuple-element.22.even_in, f32[4,5,2,192,128]{4,3,2,1,0:T(8,128)S(1)} %get-tuple-element.23.odd_in, f32[2,5,2,192,128]{4,3,2,1,0:T(8,128)S(1)} %get-tuple-element.24.cells_in, ...), custom_call_target="tpu_custom_call" | custom-call | flops 1150000000 | tf_op jit(solution)/shard_map/edge_sweeps/pallas_call | solution.py:824
  90.6 6.8 %settle.1 = (f32[32,16,256]{2,1,0:T(8,128)}, f32[32,16,256]{2,1,0:T(8,128)}) custom-call(s32[8,48]{1,0:T(8,128)S(1)} %bitcast.7, f32[8,3,48,128]{3,2,1,0:T(8,128)S(1)} %all-to-all-done.2.moments_in, f32[32,16,256]{2,1,0:T(8,128)S(1)} %copy-done.8, f32[32,16,256]{2,1,0:T(8,128)S(1)} %copy-done.11), custom_call_target="tpu_custom_call" | custom-call | flops 8049999872 | tf_op jit(solution)/shard_map/settle/pallas_call | solution.py:422
  (27 shorter events, 0.8 us)
Async XLA Ops:
  0.6 13.9 %all-to-all-start = ((s32[8,1,48]{2,1,0:T(1,128)}), s32[8,1,48]{2,1,0:T(1,128)S(1)}, u32[]{:S(2)}, u32[]{:S(2)}) async-start(s32[8,1,48]{2,1,0:T(1,128)} %bitcast.8), calls=%async_computation | async-start | bytes 8192 | tf_op jit(solution)/shard_map/all_to_all | solution.py:869
  6.8 7.8 %copy-start.1 = (f32[3,32,16,256]{3,2,1,0:T(8,128)S(1)}, f32[3,32,16,256]{3,2,1,0:T(8,128)}, u32[]{:S(2)}) copy-start(f32[3,32,16,256]{3,2,1,0:T(8,128)} %vel.5) | copy-start | bytes 4718596
  9.0 17.6 %collective-permute-start = (f32[6,4,16,256]{3,2,1,0:T(8,128)}, f32[6,4,16,256]{3,2,1,0:T(8,128)S(1)}, u32[]{:S(2)}, u32[]{:S(2)}) collective-permute-start(f32[6,4,16,256]{3,2,1,0:T(8,128)} %get-tuple-element.18), channel_id=1, source_target_pairs={{0,8},{8,16},{16,24},{1,9},{9,17},{17,25},{2,10},{10,18},{18,26},{... | collective-permute-start | bytes 1179656 | tf_op jit(solution)/shard_map/ppermute | solution.py:855
  10.9 15.6 %collective-permute-start.1 = (f32[6,4,16,256]{3,2,1,0:T(8,128)}, f32[6,4,16,256]{3,2,1,0:T(8,128)S(1)}, u32[]{:S(2)}, u32[]{:S(2)}) collective-permute-start(f32[6,4,16,256]{3,2,1,0:T(8,128)} %get-tuple-element.19), channel_id=1, source_target_pairs={{8,0},{16,8},{24,16},{9,1},{17,9},{25,17},{10,2},{18,10},{26,18},{... | collective-permute-start | bytes 1179656 | tf_op jit(solution)/shard_map/ppermute | solution.py:855
  14.6 12.7 %copy-start.4 = (f32[32,16,256]{2,1,0:T(8,128)S(1)}, f32[32,16,256]{2,1,0:T(8,128)}, u32[]{:S(2)}) copy-start(f32[32,16,256]{2,1,0:T(8,128)} %pres.3) | copy-start | bytes 1572868
  20.5 18.9 %all-to-all-start.1 = ((f32[8,3,48,128]{3,2,1,0:T(8,128)}), f32[8,3,48,128]{3,2,1,0:T(8,128)}, u32[]{:S(2)}, u32[]{:S(2)}) async-start(f32[8,3,48,128]{3,2,1,0:T(8,128)} %pick_bricks.1), calls=%async_computation.1 | async-start | bytes 1179648 | tf_op jit(solution)/shard_map/all_to_all | solution.py:877
  26.5 0.7 copy-start.12
  27.3 1.0 %copy-start.6 = (f32[32,16,256]{2,1,0:T(8,128)S(1)}, f32[32,16,256]{2,1,0:T(8,128)}, u32[]{:S(2)}) copy-start(f32[32,16,256]{2,1,0:T(8,128)} %visc_in.1) | copy-start | bytes 1572868
  28.3 1.0 %copy-start.9 = (f32[32,16,256]{2,1,0:T(8,128)S(1)}, f32[32,16,256]{2,1,0:T(8,128)}, u32[]{:S(2)}) copy-start(f32[32,16,256]{2,1,0:T(8,128)} %dens_in.1) | copy-start | bytes 1572868
  29.4 1.0 %copy-start.13 = (f32[6,4,16,256]{3,2,1,0:T(8,128)S(1)}, f32[6,4,16,256]{3,2,1,0:T(8,128)}, u32[]{:S(2)}) copy-start(f32[6,4,16,256]{3,2,1,0:T(8,128)} %copy-done.12) | copy-start | bytes 1179652
  31.8 7.6 %copy-start.3 = (f32[34,24,256]{2,1,0:T(8,128)}, f32[34,24,256]{2,1,0:T(8,128)S(1)}, u32[]{:S(2)}) copy-start(f32[34,24,256]{2,1,0:T(8,128)S(1)} %get-tuple-element.20.refs_6_) | copy-start | bytes 2506756
  31.8 50.6 %collective-permute-start.2 = (f32[34,24,256]{2,1,0:T(8,128)S(1)}, f32[34,24,256]{2,1,0:T(8,128)S(1)}, u32[]{:S(2)}, u32[]{:S(2)}) collective-permute-start(f32[34,24,256]{2,1,0:T(8,128)S(1)} %get-tuple-element.20.refs_6_), channel_id=1, source_target_pairs={{0,1},{1,2},{2,3},{3,4},{4,5},{5,6},{6,7},{8,9},{9,10},{10,11},{11... | collective-permute-start | bytes 2506760 | tf_op jit(solution)/shard_map/ppermute | solution.py:855
  35.2 47.3 %collective-permute-start.3 = (f32[32,24,256]{2,1,0:T(8,128)}, f32[32,24,256]{2,1,0:T(8,128)S(1)}, u32[]{:S(2)}, u32[]{:S(2)}) collective-permute-start(f32[32,24,256]{2,1,0:T(8,128)} %get-tuple-element.25), channel_id=1, source_target_pairs={{1,0},{2,1},{3,2},{4,3},{5,4},{6,5},{7,6},{9,8},{10,9},{11,10},{12... | collective-permute-start | bytes 2359304 | tf_op jit(solution)/shard_map/ppermute | solution.py:855
  52.1 38.6 %all-to-all-start.2 = ((f32[8,3,48,128]{3,2,1,0:T(8,128)}), f32[8,3,48,128]{3,2,1,0:T(8,128)S(1)}, u32[]{:S(2)}, u32[]{:S(2)}) async-start(f32[8,3,48,128]{3,2,1,0:T(8,128)} %get-tuple-element.21._), calls=%async_computation.2 | async-start | bytes 1179648 | tf_op jit(solution)/shard_map/all_to_all | solution.py:881
  66.4 1.1 %copy-start = (f32[8,3,48,128]{3,2,1,0:T(8,128)S(1)}, f32[8,3,48,128]{3,2,1,0:T(8,128)}, u32[]{:S(2)}) copy-start(f32[8,3,48,128]{3,2,1,0:T(8,128)} %get-tuple-element.21._) | copy-start | bytes 1769476
  67.5 1.4 %copy-start.2 = (f32[3,32,16,256]{3,2,1,0:T(8,128)S(1)}, f32[3,32,16,256]{3,2,1,0:T(8,128)}, u32[]{:S(2)}) copy-start(f32[3,32,16,256]{3,2,1,0:T(8,128)} %vel.5) | copy-start | bytes 4718596
  68.9 1.0 %copy-start.5 = (f32[32,16,256]{2,1,0:T(8,128)S(1)}, f32[32,16,256]{2,1,0:T(8,128)}, u32[]{:S(2)}) copy-start(f32[32,16,256]{2,1,0:T(8,128)} %pres.3) | copy-start | bytes 1572868
  70.0 1.0 %copy-start.7 = (f32[32,16,256]{2,1,0:T(8,128)S(1)}, f32[32,16,256]{2,1,0:T(8,128)}, u32[]{:S(2)}) copy-start(f32[32,16,256]{2,1,0:T(8,128)} %visc_in.1) | copy-start | bytes 1572868
  71.0 1.0 %copy-start.10 = (f32[32,16,256]{2,1,0:T(8,128)S(1)}, f32[32,16,256]{2,1,0:T(8,128)}, u32[]{:S(2)}) copy-start(f32[32,16,256]{2,1,0:T(8,128)} %dens_in.1) | copy-start | bytes 1572868
  72.0 1.0 %copy-start.14 = (f32[6,4,16,256]{3,2,1,0:T(8,128)S(1)}, f32[6,4,16,256]{3,2,1,0:T(8,128)}, u32[]{:S(2)}) copy-start(f32[6,4,16,256]{3,2,1,0:T(8,128)} %copy-done.12) | copy-start | bytes 1179652
  82.5 8.1 %copy-start.8 = (f32[32,16,256]{2,1,0:T(8,128)S(1)}, f32[32,16,256]{2,1,0:T(8,128)}, u32[]{:S(2)}) copy-start(f32[32,16,256]{2,1,0:T(8,128)} %visc_in.1) | copy-start | bytes 1572868
  82.5 8.1 %copy-start.11 = (f32[32,16,256]{2,1,0:T(8,128)S(1)}, f32[32,16,256]{2,1,0:T(8,128)}, u32[]{:S(2)}) copy-start(f32[32,16,256]{2,1,0:T(8,128)} %dens_in.1) | copy-start | bytes 1572868
where the time goes:
time: 98.6 us; the launch traced here: 97.5 us
  Pallas kernels  46.5 us (47%)
  starting transfers between devices  38.8 us (39%)
  local copies, waits for them, and re-layouts  10.5 us (11%)
    all_to_all x1, starting transfers between devices, per_device(): gathered = lax.all_to_all(moments, 'mark', 0, 0, tiled=True)  14.3 us
    pallas_call x1, Pallas kernels, marker_work(): pl.pallas_call(marker_body, out_shape=(jax.ShapeDtypeStruct((owners, part...  12.6 us
    ppermute x4, starting transfers between devices, shift(): return lax.ppermute(value, axis, pairs)  12.3 us
    unnamed x30, local copies, waits for them, and re-layouts  10.5 us
    pallas_call x1, Pallas kernels, inner_sweeps(): pl.pallas_call(inner_body, out_shape=tuple((jax.ShapeDtypeStruct(shape, f...  9.43 us
    pallas_call x1, Pallas kernels, edge_sweeps(): pl.pallas_call(edge_body, out_shape=(jax.ShapeDtypeStruct((3, size_x, siz...  8.08 us
    pallas_call x1, Pallas kernels, settle(): pl.pallas_call(settle_body, out_shape=(shape, shape), in_specs=[pl.BlockS...  6.82 us
    all_to_all x1, starting transfers between devices, per_device(): asked = lax.all_to_all(block_brick, 'mark', 0, 0, tiled=True)  6.18 us
  transfers between devices with their start and end apart: 7, of which 1 were waited for; matrix products, arithmetic and copies ran while one was open for 0% of the time, Pallas kernels for 41%

commit v1 on v0

--- a/solution.py
+++ b/solution.py
@@ -27,6 +27,10 @@
 
 def vmem_limit(mib):
     return pltpu.CompilerParams(vmem_limit_bytes=mib * 1024 * 1024)
+
+
+def in_hbm(*arrays):
+    return [pltpu.with_memory_space_constraint(array, pltpu.HBM) for array in arrays]
 
 
 def cost(microseconds):
@@ -337,17 +341,19 @@
             pltpu.VMEM((32 * TOGETHER, 2 * BY * BZ * HALF), f32),
         ]
         + [buffer for buffer in buffers for _ in range(2 * TOGETHER)],
-        compiler_params=vmem_limit(60),
+        compiler_params=vmem_limit(40),
         cost_estimate=cost(25),
         name="marker_work",
     )(
         counts,
-        spread,
-        gather,
-        positions.reshape(owners, 3, parts, HALF, markers),
-        start_visc.reshape(owners, parts, HALF, markers),
-        marker_dens.reshape(owners, parts, HALF, markers),
-        bricks,
+        *in_hbm(
+            spread,
+            gather,
+            positions.reshape(owners, 3, parts, HALF, markers),
+            start_visc.reshape(owners, parts, HALF, markers),
+            marker_dens.reshape(owners, parts, HALF, markers),
+            bricks,
+        ),
         after,
     )
     return visc.reshape(owners, slots, markers), moments
@@ -435,7 +441,7 @@
         compiler_params=vmem_limit(24),
         cost_estimate=cost(7),
         name="settle",
-    )(asked, moments, cell_visc, cell_dens)
+    )(asked, *in_hbm(moments, cell_visc, cell_dens))
 
 
 def field_of(fields, index):
@@ -529,7 +535,7 @@
         compiler_params=vmem_limit(24),
         cost_estimate=cost(15),
         name="pack_y",
-    )(velocity, pressure, cell_visc, cell_dens, low_x, high_x)
+    )(*in_hbm(velocity, pressure, cell_visc, cell_dens), low_x, high_x)
 
 
 def place(per, x, y, rows):
@@ -744,7 +750,7 @@
         compiler_params=vmem_limit(40),
         cost_estimate=cost(25),
         name="inner_sweeps",
-    )(velocity, pressure, cell_visc, cell_dens, low_x, high_x, after)
+    )(*in_hbm(velocity, pressure, cell_visc, cell_dens), low_x, high_x, after)
 
 
 def edge_body(even_in, odd_in, cells_in, low_y, high_y, vel_out, pres_out, *work):

time: 98.6 us -> 94.9 us (0.962)
  the two profiles are of different devices: /device:TPU:18 before, /device:TPU:10 now
where the time goes in v1:
time: 94.9 us; the launch traced here: 93.2 us
  Pallas kernels  57.2 us (60%)
  starting transfers between devices  28.7 us (30%)
  waiting for transfers between devices  4.51 us (5%)
  local copies, waits for them, and re-layouts  2.01 us (2%)
    pallas_call x1, Pallas kernels, marker_work(): pl.pallas_call(marker_body, out_shape=(jax.ShapeDtypeStruct((owners, part...  20.2 us
    ppermute x4, starting transfers between devices, shift(): return lax.ppermute(value, axis, pairs)  12.3 us
    pallas_call x1, Pallas kernels, inner_sweeps(): pl.pallas_call(inner_body, out_shape=tuple((jax.ShapeDtypeStruct(shape, f...  10.3 us
    pallas_call x1, Pallas kernels, edge_sweeps(): pl.pallas_call(edge_body, out_shape=(jax.ShapeDtypeStruct((3, size_x, siz...  8.07 us
    pallas_call x1, Pallas kernels, settle(): pl.pallas_call(settle_body, out_shape=(shape, shape), in_specs=[pl.BlockS...  7.48 us
    all_to_all x1, starting transfers between devices, per_device(): asked = lax.all_to_all(block_brick, 'mark', 0, 0, tiled=True)  6.29 us
    all_to_all x1, starting transfers between devices, per_device(): bricks = lax.all_to_all(picked, 'mark', 0, 0, tiled=True)  6 us
    pallas_call x1, Pallas kernels, pick_bricks(): pl.pallas_call(pick_body, out_shape=jax.ShapeDtypeStruct((devices, slots...  5.94 us
  transfers between devices with their start and end apart: 7, of which 1 were waited for; matrix products, arithmetic and copies ran while one was open for 0% of the time, Pallas kernels for 53%

profile of v1, /device:TPU:10, one launch (start us, length us, event | category | flops | bytes accessed | tf_op | source)
XLA Modules:
  0.0 93.2 jit_solution(7341394526837958659)
XLA Ops:
  0.6 6.3 %all-to-all-start = ((s32[8,1,48]{2,1,0:T(1,128)}), s32[8,1,48]{2,1,0:T(1,128)S(1)}, u32[]{:S(2)}, u32[]{:S(2)}) async-start(s32[8,1,48]{2,1,0:T(1,128)} %bitcast.8), calls=%async_computation | async-start | bytes 8192 | tf_op jit(solution)/shard_map/all_to_all | solution.py:875
  6.9 2.2 %pack_x.1 = (f32[6,4,16,256]{3,2,1,0:T(8,128)}, f32[6,4,16,256]{3,2,1,0:T(8,128)}) custom-call(f32[3,32,16,256]{3,2,1,0:T(8,128)} %vel.5, f32[3,32,16,256]{3,2,1,0:T(8,128)} %vel.5, f32[32,16,256]{2,1,0:T(8,128)} %pres.3, f32[32,16,256]{2,1,0:T(8,128)} %pres.3, f32[32,16,256]{2,1,0:T(8,128)} %visc_in.1, f32[32,16,256]{2,1,0:T(8,128)} %visc_in.1, ...), custom_call_target="tpu_custom_call" | custom-call | flops 2300000000 | tf_op jit(solution)/shard_map/pack_x/pallas_call | solution.py:468
  9.1 1.9 %collective-permute-start = (f32[6,4,16,256]{3,2,1,0:T(8,128)}, f32[6,4,16,256]{3,2,1,0:T(8,128)S(1)}, u32[]{:S(2)}, u32[]{:S(2)}) collective-permute-start(f32[6,4,16,256]{3,2,1,0:T(8,128)} %get-tuple-element.18), channel_id=1, source_target_pairs={{0,8},{8,16},{16,24},{1,9},{9,17},{17,25},{2,10},{10,18},{18,26},{... | collective-permute-start | bytes 1179656 | tf_op jit(solution)/shard_map/ppermute | solution.py:861
  11.0 3.6 %collective-permute-start.1 = (f32[6,4,16,256]{3,2,1,0:T(8,128)}, f32[6,4,16,256]{3,2,1,0:T(8,128)S(1)}, u32[]{:S(2)}, u32[]{:S(2)}) collective-permute-start(f32[6,4,16,256]{3,2,1,0:T(8,128)} %get-tuple-element.19), channel_id=1, source_target_pairs={{8,0},{16,8},{24,16},{9,1},{17,9},{25,17},{10,2},{18,10},{26,18},{... | collective-permute-start | bytes 1179656 | tf_op jit(solution)/shard_map/ppermute | solution.py:861
  14.7 5.9 %pick_bricks.1 = f32[8,3,48,128]{3,2,1,0:T(8,128)} custom-call(s32[8,48]{1,0:T(8,128)S(1)} %bitcast.6, f32[3,32,16,256]{3,2,1,0:T(8,128)S(1)} %copy-done), custom_call_target="tpu_custom_call" | custom-call | flops 28750000128 | tf_op jit(solution)/shard_map/pick_bricks/pallas_call | solution.py:86
  20.6 6.0 %all-to-all-start.1 = ((f32[8,3,48,128]{3,2,1,0:T(8,128)}), f32[8,3,48,128]{3,2,1,0:T(8,128)}, u32[]{:S(2)}, u32[]{:S(2)}) async-start(f32[8,3,48,128]{3,2,1,0:T(8,128)} %pick_bricks.1), calls=%async_computation.1 | async-start | bytes 1179648 | tf_op jit(solution)/shard_map/all_to_all | solution.py:883
  26.6 0.0 copy-start.1
  26.6 0.0 collective-permute-done.1.high_x
  26.6 0.0 copy-start.3
  26.7 3.0 %pack_y.1 = (f32[34,24,256]{2,1,0:T(8,128)S(1)}, f32[32,24,256]{2,1,0:T(8,128)S(1)}) custom-call(f32[3,32,16,256]{3,2,1,0:T(8,128)} %vel.5, f32[32,16,256]{2,1,0:T(8,128)} %pres.3, f32[32,16,256]{2,1,0:T(8,128)} %visc_in.1, f32[32,16,256]{2,1,0:T(8,128)} %dens_in.1, f32[6,4,16,256]{3,2,1,0:T(8,128)S(1)} %collective-permute-done.low_x, ...), custom_call_target="tpu_custom_call" | custom-call | flops 17250000896 | tf_op jit(solution)/shard_map/pack_y/pallas_call | solution.py:522
  29.7 3.4 %collective-permute-start.2 = (f32[34,24,256]{2,1,0:T(8,128)S(1)}, f32[34,24,256]{2,1,0:T(8,128)S(1)}, u32[]{:S(2)}, u32[]{:S(2)}) collective-permute-start(f32[34,24,256]{2,1,0:T(8,128)S(1)} %get-tuple-element.20.refs_6_), channel_id=1, source_target_pairs={{0,1},{1,2},{2,3},{3,4},{4,5},{5,6},{6,7},{8,9},{9,10},{10,11},{11... | collective-permute-start | bytes 2506760 | tf_op jit(solution)/shard_map/ppermute | solution.py:861
  33.1 3.4 %collective-permute-start.3 = (f32[32,24,256]{2,1,0:T(8,128)S(1)}, f32[32,24,256]{2,1,0:T(8,128)S(1)}, u32[]{:S(2)}, u32[]{:S(2)}) collective-permute-start(f32[32,24,256]{2,1,0:T(8,128)S(1)} %get-tuple-element.25), channel_id=1, source_target_pairs={{1,0},{2,1},{3,2},{4,3},{5,4},{6,5},{7,6},{9,8},{10,9},{11,10},{12... | collective-permute-start | bytes 2359304 | tf_op jit(solution)/shard_map/ppermute | solution.py:861
  36.5 4.5 %all-to-all-done.1.refs_5_ = f32[8,3,48,128]{3,2,1,0:T(8,128)} async-done(((f32[8,3,48,128]{3,2,1,0:T(8,128)}), f32[8,3,48,128]{3,2,1,0:T(8,128)}, u32[]{:S(2)}, u32[]{:S(2)}) %all-to-all-start.1) | async-done | bytes 589856 | tf_op jit(solution)/shard_map/all_to_all | solution.py:883
  41.0 20.2 %marker_work.1 = (f32[8,6,8,256]{3,2,1,0:T(8,128)}, f32[8,3,48,128]{3,2,1,0:T(8,128)}) custom-call(s32[1,8]{1,0:T(1,128)S(1)} %copy-done.5, bf16[2,2,128,256]{3,2,1,0:T(8,128)(2,1)} %constant.4.clone.refs_0_, bf16[512,512]{1,0:T(8,128)(2,1)} %constant.5.clone.refs_1_, f32[8,3,6,8,256]{4,3,2,1,0:T(8,128)} %bitcast.9, f32[8,6,8,256]{3,2,1,0:T(8,128)} %bitcast.10, ...), custom_call_target="tpu_custom_call" | custom-call | flops 28750000128 | tf_op jit(solution)/shard_map/marker_work/pallas_call | solution.py:329
  61.2 4.1 %all-to-all-start.2 = ((f32[8,3,48,128]{3,2,1,0:T(8,128)}), f32[8,3,48,128]{3,2,1,0:T(8,128)}, u32[]{:S(2)}, u32[]{:S(2)}) async-start(f32[8,3,48,128]{3,2,1,0:T(8,128)} %get-tuple-element.21._), calls=%async_computation.2 | async-start | bytes 1179648 | tf_op jit(solution)/shard_map/all_to_all | solution.py:887
  65.4 0.0 copy-start.2
  65.4 1.0 %copy-done.2 = f32[6,4,16,256]{3,2,1,0:T(8,128)S(1)} copy-done((f32[6,4,16,256]{3,2,1,0:T(8,128)S(1)}, f32[6,4,16,256]{3,2,1,0:T(8,128)}, u32[]{:S(2)}) %copy-start.2) | copy-done | bytes 393240
  66.4 1.0 %copy-done.4 = f32[6,4,16,256]{3,2,1,0:T(8,128)S(1)} copy-done((f32[6,4,16,256]{3,2,1,0:T(8,128)S(1)}, f32[6,4,16,256]{3,2,1,0:T(8,128)}, u32[]{:S(2)}) %copy-start.4) | copy-done | bytes 393240
  67.4 10.3 %inner_sweeps.1 = (f32[4,5,2,192,128]{4,3,2,1,0:T(8,128)S(1)}, f32[4,5,2,192,128]{4,3,2,1,0:T(8,128)S(1)}, f32[2,5,2,192,128]{4,3,2,1,0:T(8,128)S(1)}) custom-call(f32[3,32,16,256]{3,2,1,0:T(8,128)} %vel.5, f32[32,16,256]{2,1,0:T(8,128)} %pres.3, f32[32,16,256]{2,1,0:T(8,128)} %visc_in.1, f32[32,16,256]{2,1,0:T(8,128)} %dens_in.1, ...), custom_call_target="tpu_custom_call" | custom-call | flops 28750000128 | tf_op jit(solution)/shard_map/inner_sweeps/pallas_call | solution.py:733
  77.7 0.0 collective-permute-done.3.high_y
  77.7 0.0 collective-permute-done.2.low_y
  77.7 8.1 %edge_sweeps.1 = (f32[3,32,16,256]{3,2,1,0:T(8,128)}, f32[32,16,256]{2,1,0:T(8,128)}) custom-call(f32[4,5,2,192,128]{4,3,2,1,0:T(8,128)S(1)} %get-tuple-element.22.even_in, f32[4,5,2,192,128]{4,3,2,1,0:T(8,128)S(1)} %get-tuple-element.23.odd_in, f32[2,5,2,192,128]{4,3,2,1,0:T(8,128)S(1)} %get-tuple-element.24.cells_in, ...), custom_call_target="tpu_custom_call" | custom-call | flops 1150000000 | tf_op jit(solution)/shard_map/edge_sweeps/pallas_call | solution.py:830
  85.8 0.0 all-to-all-done.2.moments_in
  85.8 7.5 %settle.1 = (f32[32,16,256]{2,1,0:T(8,128)}, f32[32,16,256]{2,1,0:T(8,128)}) custom-call(s32[8,48]{1,0:T(8,128)S(1)} %bitcast.7, f32[8,3,48,128]{3,2,1,0:T(8,128)} %all-to-all-done.2.moments_in, f32[32,16,256]{2,1,0:T(8,128)} %visc_in.1, f32[32,16,256]{2,1,0:T(8,128)} %dens_in.1), custom_call_target="tpu_custom_call" | custom-call | flops 8049999872 | tf_op jit(solution)/shard_map/settle/pallas_call | solution.py:428
  (9 shorter events, 0.0 us)
Async XLA Ops:
  0.6 14.0 %all-to-all-start = ((s32[8,1,48]{2,1,0:T(1,128)}), s32[8,1,48]{2,1,0:T(1,128)S(1)}, u32[]{:S(2)}, u32[]{:S(2)}) async-start(s32[8,1,48]{2,1,0:T(1,128)} %bitcast.8), calls=%async_computation | async-start | bytes 8192 | tf_op jit(solution)/shard_map/all_to_all | solution.py:875
  6.9 7.8 %copy-start = (f32[3,32,16,256]{3,2,1,0:T(8,128)S(1)}, f32[3,32,16,256]{3,2,1,0:T(8,128)}, u32[]{:S(2)}) copy-start(f32[3,32,16,256]{3,2,1,0:T(8,128)} %vel.5) | copy-start | bytes 4718596
  9.1 17.5 %collective-permute-start = (f32[6,4,16,256]{3,2,1,0:T(8,128)}, f32[6,4,16,256]{3,2,1,0:T(8,128)S(1)}, u32[]{:S(2)}, u32[]{:S(2)}) collective-permute-start(f32[6,4,16,256]{3,2,1,0:T(8,128)} %get-tuple-element.18), channel_id=1, source_target_pairs={{0,8},{8,16},{16,24},{1,9},{9,17},{17,25},{2,10},{10,18},{18,26},{... | collective-permute-start | bytes 1179656 | tf_op jit(solution)/shard_map/ppermute | solution.py:861
  11.0 15.6 %collective-permute-start.1 = (f32[6,4,16,256]{3,2,1,0:T(8,128)}, f32[6,4,16,256]{3,2,1,0:T(8,128)S(1)}, u32[]{:S(2)}, u32[]{:S(2)}) collective-permute-start(f32[6,4,16,256]{3,2,1,0:T(8,128)} %get-tuple-element.19), channel_id=1, source_target_pairs={{8,0},{16,8},{24,16},{9,1},{17,9},{25,17},{10,2},{18,10},{26,18},{... | collective-permute-start | bytes 1179656 | tf_op jit(solution)/shard_map/ppermute | solution.py:861
  20.6 20.4 %all-to-all-start.1 = ((f32[8,3,48,128]{3,2,1,0:T(8,128)}), f32[8,3,48,128]{3,2,1,0:T(8,128)}, u32[]{:S(2)}, u32[]{:S(2)}) async-start(f32[8,3,48,128]{3,2,1,0:T(8,128)} %pick_bricks.1), calls=%async_computation.1 | async-start | bytes 1179648 | tf_op jit(solution)/shard_map/all_to_all | solution.py:883
  26.6 14.4 %copy-start.5 = (s32[1,8]{1,0:T(1,128)S(1)}, s32[1,8]{1,0:T(1,128)}, u32[]{:S(2)}) copy-start(s32[1,8]{1,0:T(1,128)} %counts.1) | copy-start | bytes 100
  26.6 3.1 %copy-start.1 = (f32[6,4,16,256]{3,2,1,0:T(8,128)}, f32[6,4,16,256]{3,2,1,0:T(8,128)S(1)}, u32[]{:S(2)}) copy-start(f32[6,4,16,256]{3,2,1,0:T(8,128)S(1)} %collective-permute-done.low_x) | copy-start | bytes 1179652
  26.6 3.1 %copy-start.3 = (f32[6,4,16,256]{3,2,1,0:T(8,128)}, f32[6,4,16,256]{3,2,1,0:T(8,128)S(1)}, u32[]{:S(2)}) copy-start(f32[6,4,16,256]{3,2,1,0:T(8,128)S(1)} %collective-permute-done.1.high_x) | copy-start | bytes 1179652
  29.7 47.9 %collective-permute-start.2 = (f32[34,24,256]{2,1,0:T(8,128)S(1)}, f32[34,24,256]{2,1,0:T(8,128)S(1)}, u32[]{:S(2)}, u32[]{:S(2)}) collective-permute-start(f32[34,24,256]{2,1,0:T(8,128)S(1)} %get-tuple-element.20.refs_6_), channel_id=1, source_target_pairs={{0,1},{1,2},{2,3},{3,4},{4,5},{5,6},{6,7},{8,9},{9,10},{10,11},{11... | collective-permute-start | bytes 2506760 | tf_op jit(solution)/shard_map/ppermute | solution.py:861
  33.1 44.6 %collective-permute-start.3 = (f32[32,24,256]{2,1,0:T(8,128)S(1)}, f32[32,24,256]{2,1,0:T(8,128)S(1)}, u32[]{:S(2)}, u32[]{:S(2)}) collective-permute-start(f32[32,24,256]{2,1,0:T(8,128)S(1)} %get-tuple-element.25), channel_id=1, source_target_pairs={{1,0},{2,1},{3,2},{4,3},{5,4},{6,5},{7,6},{9,8},{10,9},{11,10},{12... | collective-permute-start | bytes 2359304 | tf_op jit(solution)/shard_map/ppermute | solution.py:861
  61.2 24.5 %all-to-all-start.2 = ((f32[8,3,48,128]{3,2,1,0:T(8,128)}), f32[8,3,48,128]{3,2,1,0:T(8,128)}, u32[]{:S(2)}, u32[]{:S(2)}) async-start(f32[8,3,48,128]{3,2,1,0:T(8,128)} %get-tuple-element.21._), calls=%async_computation.2 | async-start | bytes 1179648 | tf_op jit(solution)/shard_map/all_to_all | solution.py:887
  65.4 1.0 %copy-start.2 = (f32[6,4,16,256]{3,2,1,0:T(8,128)S(1)}, f32[6,4,16,256]{3,2,1,0:T(8,128)}, u32[]{:S(2)}) copy-start(f32[6,4,16,256]{3,2,1,0:T(8,128)} %copy-done.1) | copy-start | bytes 1179652
  66.4 1.0 %copy-start.4 = (f32[6,4,16,256]{3,2,1,0:T(8,128)S(1)}, f32[6,4,16,256]{3,2,1,0:T(8,128)}, u32[]{:S(2)}) copy-start(f32[6,4,16,256]{3,2,1,0:T(8,128)} %copy-done.3) | copy-start | bytes 1179652

commit v2 on v1

--- a/solution.py
+++ b/solution.py
@@ -171,7 +171,7 @@
 def marker_groups(groups, counts, ins, outs, buffers, sums):
     spread, gather, places, start, dens, brick = ins
     visc_out, moments_out = outs
-    permuted, left, right, products, weights, factors, planes_high, planes_low = buffers
+    permuted, left, right, products, weights, factors, planes = buffers
     markers = places.shape[-1]
     inside = BZ * HALF
     own = own_lanes()
@@ -184,10 +184,8 @@
     for _, _, half, n in halves:
         high, low = parts[n // 2]
         permuted[n][...] = dot(high, spread[half, 0]) + dot(low, spread[half, 1])
-    heights = []
     for owner, part, _, n in halves:
         weight_z, slope_z = axis_weights(places[owner, 2, part], BZ)
-        heights.append(weight_z)
         for z in range(0, BZ, 2):
             for column, values in ((0, weight_z), (1, slope_z)):
                 high, low = split(jnp.concatenate(values[z : z + 2], axis=0))
@@ -195,15 +193,12 @@
                 for k in range(4):
                     begin = k * inside + z * HALF
                     right[n][begin : begin + 2 * HALF, columns] = low if k % 2 else high
-    for _, _, _, n in halves:
         for row in range(0, ROWS, 2):
             pair = [
                 jnp.broadcast_to(permuted[n][r : r + 1, :], own.shape) * own for r in (row, row + 1)
             ]
             left[n][row * HALF : (row + 2) * HALF, :] = jnp.concatenate(pair, axis=0).astype(bf16)
-    for _, _, _, n in halves:
         products[n][...] = dot(left[n][...], right[n][...])
-    for owner, part, _, n in halves:
         weights_x = axis_weights(places[owner, 0, part], BX)
         weights_y = axis_weights(places[owner, 1, part], BY)
         for k, values in enumerate((*weights_x, *weights_y)):
@@ -211,13 +206,14 @@
                 weights[n][4 * k + i] = value
         for j in range(BY):
             for z in range(0, BZ, 2):
-                pair = [weights_y[0][j] * heights[n][z + k] for k in range(2)]
+                pair = [weights_y[0][j] * weight_z[z + k] for k in range(2)]
                 rows = slice((j * BZ + z) * HALF, (j * BZ + z + 2) * HALF)
                 high, low = split(jnp.concatenate(pair, axis=0))
-                planes_high[n][rows, :] = high
-                planes_low[n][rows, :] = low
-
-    count = 3 * BX * HALF
+                planes[n][rows, :markers] = high
+                planes[n][rows, markers:] = low
+
+    contract = (((1,), (1,)), ((), ()))
+    found = []
     for owner, part, _, n in halves:
         grads = gradients(products[n], weights[n], markers)
         normal = grads[0][0] ** 2 + grads[1][1] ** 2 + grads[2][2] ** 2
@@ -241,23 +237,23 @@
                 pair = [carried[c] * weights[n][i + k] for k in range(2)]
                 row = (c * BX + i) * HALF
                 high, low = split(jnp.concatenate(pair, axis=0))
-                factors[n][row : row + 2 * HALF, :] = high
-                factors[n][count + row : count + row + 2 * HALF, :] = low
-
-    contract = (((1,), (1,)), ((), ()))
-    found = []
-    for _, _, _, n in halves:
+                rows = slice(row, row + 2 * HALF)
+                factors[n][rows, :markers] = high
+                factors[n][rows, markers : 2 * markers] = high
+                factors[n][rows, 2 * markers :] = low
+
         both = lax.dot_general(
-            factors[n][...], planes_high[n][...], contract, preferred_element_type=f32
+            factors[n][:, : 2 * markers], planes[n][...], contract, preferred_element_type=f32
         )
         rest = lax.dot_general(
-            factors[n][:count], planes_low[n][...], contract, preferred_element_type=f32
+            factors[n][:, 2 * markers :],
+            planes[n][:, :markers],
+            contract,
+            preferred_element_type=f32,
         )
-        found.append((both, rest))
+        found.append(both + rest)
     for _, _, half, n in halves:
-        both, rest = found[n]
-        total = both[:count] + both[count:] + rest
-        chosen = total.reshape(3 * BX, HALF, BY * inside) * own[None]
+        chosen = found[n].reshape(3 * BX, HALF, BY * inside) * own[None]
         high, low = split(jnp.sum(chosen, axis=1))
         columns = slice(half * BY * inside, (half + 1) * BY * inside)
         row = (n // 2) * 32
@@ -322,9 +318,8 @@
         pltpu.VMEM((width, 2 * markers), bf16),
         pltpu.VMEM((ROWS * HALF, 2 * markers), f32),
         pltpu.VMEM((4 * 4, HALF, markers), f32),
-        pltpu.VMEM((2 * 3 * BX * HALF, markers), bf16),
-        pltpu.VMEM((BY * BZ * HALF, markers), bf16),
-        pltpu.VMEM((BY * BZ * HALF, markers), bf16),
+        pltpu.VMEM((3 * BX * HALF, 3 * markers), bf16),
+        pltpu.VMEM((BY * BZ * HALF, 2 * markers), bf16),
     )
     visc, moments = pl.pallas_call(
         marker_body,
@@ -535,7 +530,7 @@
         compiler_params=vmem_limit(24),
         cost_estimate=cost(15),
         name="pack_y",
-    )(*in_hbm(velocity, pressure, cell_visc, cell_dens), low_x, high_x)
+    )(*in_hbm(velocity, pressure, cell_visc, cell_dens, low_x, high_x))
 
 
 def place(per, x, y, rows):
@@ -612,7 +607,17 @@
             forcing[plane, tile(y), :] = take(dens, plane, y) * (-GRAVITY * scale)
             rate[plane, tile(y), :] = PRESSURE_RATE * here
 
-    def sweep(y, old, new):
+    def sweep(y, old, new, results=None):
+        def keep(field, plane, value):
+            if results is None:
+                store(new.at[field], plane, y, value)
+                return
+            size_y = results.shape[2] // (per * SUBLANES)
+            begin = plane * size_y + y - SWEEPS
+            rows = pl.ds(begin, SUBLANES, stride=per * size_y)
+            for half in range(halves):
+                results[field, half, rows, :] = value[:, half * LANES : (half + 1) * LANES]
+
         for plane in range(per):
             links = [coefs[n, plane, tile(y), :] for n in range(6)]
             scale = relax[plane, tile(y), :]
@@ -641,9 +646,9 @@
                 if c == 2:
                     rest = rest + forcing[plane, tile(y), :]
                 changes.append(near[2 * c] - here)
-                store(new.at[c], plane, y, total + rest)
+                keep(c, plane, total + rest)
             pressed = pressure - rate[plane, tile(y), :] * add_all(changes)
-            store(new.at[3], plane, y, pressed)
+            keep(3, plane, pressed)
 
     return prepare, sweep
 
@@ -651,7 +656,7 @@
 def kept_rows(size_y):
     width = SWEEPS
     return (
-        ((width, size_y),),
+        ((width, width), (size_y, width)),
         ((width + 1, width), (size_y - 1, width)),
         ((width, width + 1), (size_y - 1, width + 1)),
     )
@@ -668,8 +673,9 @@
     return copies
 
 
-def inner_body(vel, pres, visc, dens, low_x, high_x, _, even_out, odd_out, cells_out, *work):
-    blocks, sides_x, even, odd, cells, coefs, relax, forcing, rate, done = work
+def inner_body(vel, pres, visc, dens, low_x, high_x, _, *refs):
+    even_out, odd_out, cells_out, results_out, *work = refs
+    blocks, sides_x, even, odd, cells, results, coefs, relax, forcing, rate, done = work
     size_x, size_y, size_z = blocks.shape[1:]
     width = SWEEPS
     inputs = (
@@ -711,12 +717,15 @@
     for step in range(SWEEPS):
         old, new = (odd, even) if step % 2 else (even, odd)
 
-        def sweep_row(y, carry, old=old, new=new):
-            sweep(y, old, new)
+        last_one = results if step == SWEEPS - 1 else None
+
+        def sweep_row(y, carry, old=old, new=new, results=last_one):
+            sweep(y, old, new, results)
             return carry
 
         lax.fori_loop(first + step, last - step, sweep_row, 0, unroll=2)
     sends = kept_copies(((even, even_out), (odd, odd_out), (cells, cells_out)), size_y, done)
+    sends.append(pltpu.make_async_copy(results, results_out, done.at[len(sends)]))
     for send in sends:
         send.start()
     for send in sends:
@@ -729,12 +738,13 @@
     per, rows = (size_x + 2 * width) // SUBLANES, (size_y + 2 * width) * SUBLANES
     block, cut = (per, rows, size_z), (per, size_z // LANES, rows, LANES)
     shapes = [(4,) + cut, (4,) + cut, (2,) + cut]
+    shapes.append((4, size_z // LANES, (size_x + 2 * width) * size_y, LANES))
     anywhere = pl.BlockSpec(memory_space=pl.ANY)
     return pl.pallas_call(
         inner_body,
         out_shape=tuple(jax.ShapeDtypeStruct(shape, f32) for shape in shapes),
         in_specs=[anywhere] * 7,
-        out_specs=(anywhere,) * 3,
+        out_specs=(anywhere,) * 4,
         scratch_shapes=[
             pltpu.VMEM((6,) + cell_visc.shape, f32),
             pltpu.VMEM((2,) + low_x.shape, f32),
@@ -745,25 +755,26 @@
             pltpu.VMEM(block, f32),
             pltpu.VMEM(block, f32),
             pltpu.VMEM(block, f32),
-            pltpu.SemaphoreType.DMA((6,)),
+            pltpu.SemaphoreType.DMA((7,)),
         ],
         compiler_params=vmem_limit(40),
         cost_estimate=cost(25),
         name="inner_sweeps",
-    )(*in_hbm(velocity, pressure, cell_visc, cell_dens), low_x, high_x, after)
-
-
-def edge_body(even_in, odd_in, cells_in, low_y, high_y, vel_out, pres_out, *work):
+    )(*in_hbm(velocity, pressure, cell_visc, cell_dens, low_x, high_x), after)
+
+
+def edge_body(size_x, even_in, odd_in, cells_in, results_in, low_y, high_y, vel_out, pres_out, *work):
     from_low, from_high, results, even, odd, cells, coefs, relax, forcing, rate, done, more = work
-    size_x, size_y, size_z = results.shape[1:]
     width = SWEEPS
-    long_y = size_y + 2 * width
+    halves, long_y = even.shape[2], even.shape[3] // SUBLANES
+    size_y, size_z = long_y - 2 * width, halves * LANES
     halos = [
         pltpu.make_async_copy(low_y, from_low, more.at[0]),
         pltpu.make_async_copy(high_y, from_high, more.at[1]),
     ]
     kept = kept_copies(((even_in, even), (odd_in, odd), (cells_in, cells)), size_y, done)
-    for copy in (*halos, *kept[3:], *kept[:3]):
+    inner = pltpu.make_async_copy(results_in, results, more.at[2])
+    for copy in (*halos, *kept, inner):
         copy.start()
     targets = [even.at[n] for n in range(4)] + [cells.at[n] for n in range(2)]
     for target in targets:
@@ -797,48 +808,50 @@
     for step in range(SWEEPS):
         old, new = (odd, even) if step % 2 else (even, odd)
 
-        def sweep_rows(n, carry, old=old, new=new, step=step):
-            sweep(1 + step + n, old, new)
-            sweep(width + size_y - 1 - step + n, old, new)
+        last_one = None
+        if step == SWEEPS - 1:
+            last_one = results
+            inner.wait()
+
+        def sweep_rows(n, carry, old=old, new=new, step=step, results=last_one):
+            sweep(1 + step + n, old, new, results)
+            sweep(width + size_y - 1 - step + n, old, new, results)
             return carry
 
         lax.fori_loop(0, width, sweep_rows, 0)
 
-    final = odd if SWEEPS % 2 else even
-    outs = [vel_out.at[0], vel_out.at[1], vel_out.at[2], pres_out]
-    sends = [pltpu.make_async_copy(results.at[n], out, done.at[n]) for n, out in enumerate(outs)]
-    per, halves = even.shape[1:3]
-    for field, send in enumerate(sends):
-        for i in range(size_x):
-            for y in range(0, size_y, SUBLANES):
-                plane, lines = place(per, i + width, y + width, SUBLANES)
-                for half in range(halves):
-                    columns = slice(half * LANES, (half + 1) * LANES)
-                    results[field, i, y : y + SUBLANES, columns] = final[
-                        field, plane, half, lines, :
-                    ]
+    own = pl.ds(width * size_y, size_x * size_y)
+    sends = []
+    for field, out in enumerate([vel_out.at[0], vel_out.at[1], vel_out.at[2], pres_out]):
+        for half in range(halves):
+            columns = pl.ds(half * LANES, LANES)
+            done_one = done.at[len(sends)]
+            sends.append(
+                pltpu.make_async_copy(results.at[field, half, own], out.at[:, columns], done_one)
+            )
+    for send in sends:
         send.start()
     for send in sends:
         send.wait()
 
 
-def edge_sweeps(even, odd, cells, low_y, high_y, size_x, size_y):
+def edge_sweeps(even, odd, cells, results, low_y, high_y, size_x, size_y):
     per, halves, rows = even.shape[1:4]
     size_z = halves * LANES
     block = (per, rows, size_z)
     anywhere = pl.BlockSpec(memory_space=pl.ANY)
-    return pl.pallas_call(
-        edge_body,
+    velocity, pressure = pl.pallas_call(
+        functools.partial(edge_body, size_x),
         out_shape=(
-            jax.ShapeDtypeStruct((3, size_x, size_y, size_z), f32),
-            jax.ShapeDtypeStruct((size_x, size_y, size_z), f32),
+            jax.ShapeDtypeStruct((3, size_x * size_y, size_z), f32),
+            jax.ShapeDtypeStruct((size_x * size_y, size_z), f32),
         ),
-        in_specs=[anywhere] * 5,
+        in_specs=[anywhere] * 6,
         out_specs=(anywhere,) * 2,
         scratch_shapes=[
             pltpu.VMEM(low_y.shape, f32),
             pltpu.VMEM(high_y.shape, f32),
-            pltpu.VMEM((4, size_x, size_y, size_z), f32),
+            pltpu.VMEM(results.shape, f32),
             pltpu.VMEM(even.shape, f32),
             pltpu.VMEM(odd.shape, f32),
             pltpu.VMEM(cells.shape, f32),
@@ -846,13 +859,17 @@
             pltpu.VMEM(block, f32),
             pltpu.VMEM(block, f32),
             pltpu.VMEM(block, f32),
-            pltpu.SemaphoreType.DMA((5,)),
-            pltpu.SemaphoreType.DMA((2,)),
+            pltpu.SemaphoreType.DMA((8,)),
+            pltpu.SemaphoreType.DMA((3,)),
         ],
         compiler_params=vmem_limit(40),
         cost_estimate=cost(1),
         name="edge_sweeps",
-    )(even, odd, cells, low_y, high_y)
+    )(even, odd, cells, results, low_y, high_y)
+    return (
+        velocity.reshape(3, size_x, size_y, size_z),
+        pressure.reshape(size_x, size_y, size_z),
+    )
 
 
 def shift(value, axis, step):

time: 94.9 us -> 95.4 us (level)
  the two profiles are of different devices: /device:TPU:10 before, /device:TPU:18 now
where the time goes in v2:
time: 95.4 us; the launch traced here: 94.7 us
  Pallas kernels  49.6 us (52%)
  starting transfers between devices  35.4 us (37%)
  waiting for transfers between devices  8.1 us (8%)
    ppermute x4, starting transfers between devices, shift(): return lax.ppermute(value, axis, pairs)  12.3 us
    pallas_call x1, Pallas kernels, marker_work(): pl.pallas_call(marker_body, out_shape=(jax.ShapeDtypeStruct((owners, part...  11.8 us
    all_to_all x1, starting transfers between devices, per_device(): gathered = lax.all_to_all(moments, 'mark', 0, 0, tiled=True)  11 us
    pallas_call x1, Pallas kernels, inner_sweeps(): pl.pallas_call(inner_body, out_shape=tuple((jax.ShapeDtypeStruct(shape, f...  10.7 us
    pallas_call x1, Pallas kernels, edge_sweeps(): pl.pallas_call(functools.partial(edge_body, size_x), out_shape=(jax.Shape...  8.49 us
    pallas_call x1, Pallas kernels, settle(): pl.pallas_call(settle_body, out_shape=(shape, shape), in_specs=[pl.BlockS...  7.48 us
    all_to_all x1, starting transfers between devices, per_device(): asked = lax.all_to_all(block_brick, 'mark', 0, 0, tiled=True)  6.18 us
    all_to_all x1, starting transfers between devices, per_device(): bricks = lax.all_to_all(picked, 'mark', 0, 0, tiled=True)  6 us
  transfers between devices with their start and end apart: 7, of which 2 were waited for; matrix products, arithmetic and copies ran while one was open for 0% of the time, Pallas kernels for 45%

profile of v2, /device:TPU:18, one launch (start us, length us, event | category | flops | bytes accessed | tf_op | source)
XLA Modules:
  0.0 94.7 jit_solution(11868745765396238492)
XLA Ops:
  0.6 6.2 %all-to-all-start = ((s32[8,1,48]{2,1,0:T(1,128)}), s32[8,1,48]{2,1,0:T(1,128)S(1)}, u32[]{:S(2)}, u32[]{:S(2)}) async-start(s32[8,1,48]{2,1,0:T(1,128)} %bitcast.10), calls=%async_computation | async-start | bytes 8192 | tf_op jit(solution)/shard_map/all_to_all | solution.py:892
  6.8 2.2 %pack_x.1 = (f32[6,4,16,256]{3,2,1,0:T(8,128)}, f32[6,4,16,256]{3,2,1,0:T(8,128)}) custom-call(f32[3,32,16,256]{3,2,1,0:T(8,128)} %vel.5, f32[3,32,16,256]{3,2,1,0:T(8,128)} %vel.5, f32[32,16,256]{2,1,0:T(8,128)} %pres.3, f32[32,16,256]{2,1,0:T(8,128)} %pres.3, f32[32,16,256]{2,1,0:T(8,128)} %visc_in.1, f32[32,16,256]{2,1,0:T(8,128)} %visc_in.1, ...), custom_call_target="tpu_custom_call" | custom-call | flops 2300000000 | tf_op jit(solution)/shard_map/pack_x/pallas_call | solution.py:463
  9.0 1.9 %collective-permute-start = (f32[6,4,16,256]{3,2,1,0:T(8,128)}, f32[6,4,16,256]{3,2,1,0:T(8,128)S(1)}, u32[]{:S(2)}, u32[]{:S(2)}) collective-permute-start(f32[6,4,16,256]{3,2,1,0:T(8,128)} %get-tuple-element.19), channel_id=1, source_target_pairs={{0,8},{8,16},{16,24},{1,9},{9,17},{17,25},{2,10},{10,18},{18,26},{... | collective-permute-start | bytes 1179656 | tf_op jit(solution)/shard_map/ppermute | solution.py:878
  10.9 3.6 %collective-permute-start.1 = (f32[6,4,16,256]{3,2,1,0:T(8,128)}, f32[6,4,16,256]{3,2,1,0:T(8,128)}, u32[]{:S(2)}, u32[]{:S(2)}) collective-permute-start(f32[6,4,16,256]{3,2,1,0:T(8,128)} %get-tuple-element.20), channel_id=1, source_target_pairs={{8,0},{16,8},{24,16},{9,1},{17,9},{25,17},{10,2},{18,10},{26,18},{... | collective-permute-start | bytes 1179656 | tf_op jit(solution)/shard_map/ppermute | solution.py:878
  14.6 0.0 all-to-all-done
  14.6 5.9 %pick_bricks.1 = f32[8,3,48,128]{3,2,1,0:T(8,128)} custom-call(s32[8,48]{1,0:T(8,128)S(1)} %bitcast.8, f32[3,32,16,256]{3,2,1,0:T(8,128)S(1)} %copy-done), custom_call_target="tpu_custom_call" | custom-call | flops 28750000128 | tf_op jit(solution)/shard_map/pick_bricks/pallas_call | solution.py:86
  20.5 6.0 %all-to-all-start.1 = ((f32[8,3,48,128]{3,2,1,0:T(8,128)}), f32[8,3,48,128]{3,2,1,0:T(8,128)}, u32[]{:S(2)}, u32[]{:S(2)}) async-start(f32[8,3,48,128]{3,2,1,0:T(8,128)} %pick_bricks.1), calls=%async_computation.1 | async-start | bytes 1179648 | tf_op jit(solution)/shard_map/all_to_all | solution.py:900
  26.5 0.0 collective-permute-done.low_x
  26.5 0.0 copy-start.2
  26.5 0.7 copy-done.2
  27.3 0.0 collective-permute-done.1.high_x
  27.3 3.0 %pack_y.1 = (f32[34,24,256]{2,1,0:T(8,128)S(1)}, f32[32,24,256]{2,1,0:T(8,128)S(1)}) custom-call(f32[3,32,16,256]{3,2,1,0:T(8,128)} %vel.5, f32[32,16,256]{2,1,0:T(8,128)} %pres.3, f32[32,16,256]{2,1,0:T(8,128)} %visc_in.1, f32[32,16,256]{2,1,0:T(8,128)} %dens_in.1, f32[6,4,16,256]{3,2,1,0:T(8,128)} %copy-done.2, f32[6,4,16,256]{3,2,1,0:T(8,128)} %collective-permute-done.1.high_x), custom_call_target="tpu_custom_call" | custom-call | flops 17250000896 | tf_op jit(solution)/shard_map/pack_y/pallas_call | solution.py:517
  30.3 3.4 %collective-permute-start.2 = (f32[34,24,256]{2,1,0:T(8,128)S(1)}, f32[34,24,256]{2,1,0:T(8,128)S(1)}, u32[]{:S(2)}, u32[]{:S(2)}) collective-permute-start(f32[34,24,256]{2,1,0:T(8,128)S(1)} %get-tuple-element.21.refs_6_), channel_id=1, source_target_pairs={{0,1},{1,2},{2,3},{3,4},{4,5},{5,6},{6,7},{8,9},{9,10},{10,11},{11... | collective-permute-start | bytes 2506760 | tf_op jit(solution)/shard_map/ppermute | solution.py:878
  33.7 3.4 %collective-permute-start.3 = (f32[32,24,256]{2,1,0:T(8,128)S(1)}, f32[32,24,256]{2,1,0:T(8,128)S(1)}, u32[]{:S(2)}, u32[]{:S(2)}) collective-permute-start(f32[32,24,256]{2,1,0:T(8,128)S(1)} %get-tuple-element.27), channel_id=1, source_target_pairs={{1,0},{2,1},{3,2},{4,3},{5,4},{6,5},{7,6},{9,8},{10,9},{11,10},{12... | collective-permute-start | bytes 2359304 | tf_op jit(solution)/shard_map/ppermute | solution.py:878
  37.1 3.6 %all-to-all-done.1.refs_5_ = f32[8,3,48,128]{3,2,1,0:T(8,128)} async-done(((f32[8,3,48,128]{3,2,1,0:T(8,128)}), f32[8,3,48,128]{3,2,1,0:T(8,128)}, u32[]{:S(2)}, u32[]{:S(2)}) %all-to-all-start.1) | async-done | bytes 589856 | tf_op jit(solution)/shard_map/all_to_all | solution.py:900
  40.6 0.0 copy-done.1
  40.6 11.8 %marker_work.1 = (f32[8,6,8,256]{3,2,1,0:T(8,128)}, f32[8,3,48,128]{3,2,1,0:T(8,128)}) custom-call(s32[1,8]{1,0:T(1,128)S(1)} %copy-done.1, bf16[2,2,128,256]{3,2,1,0:T(8,128)(2,1)} %constant.4.clone.refs_0_, bf16[512,512]{1,0:T(8,128)(2,1)} %constant.5.clone.refs_1_, f32[8,3,6,8,256]{4,3,2,1,0:T(8,128)} %bitcast.12, f32[8,6,8,256]{3,2,1,0:T(8,128)} %bitcast.14, ...), custom_call_target="tpu_custom_call" | custom-call | flops 28750000128 | tf_op jit(solution)/shard_map/marker_work/pallas_call | solution.py:324
  52.4 11.0 %all-to-all-start.2 = ((f32[8,3,48,128]{3,2,1,0:T(8,128)}), f32[8,3,48,128]{3,2,1,0:T(8,128)}, u32[]{:S(2)}, u32[]{:S(2)}) async-start(f32[8,3,48,128]{3,2,1,0:T(8,128)} %get-tuple-element.22._), calls=%async_computation.2 | async-start | bytes 1179648 | tf_op jit(solution)/shard_map/all_to_all | solution.py:904
  63.4 10.7 %inner_sweeps.1 = (f32[4,5,2,192,128]{4,3,2,1,0:T(8,128)S(1)}, f32[4,5,2,192,128]{4,3,2,1,0:T(8,128)S(1)}, f32[2,5,2,192,128]{4,3,2,1,0:T(8,128)S(1)}, f32[4,2,640,128]{3,2,1,0:T(8,128)S(1)}) custom-call(f32[3,32,16,256]{3,2,1,0:T(8,128)} %vel.5, f32[32,16,256]{2,1,0:T(8,128)} %pres.3, f32[32,16,256]{2,1,0:T(8,128)} %visc_in.1, f32[32,16,256]{2,1,0:T(8,128)} %dens_in.1, ...), custom_call_target="tpu_custom_call" | custom-call | flops 28750000128 | tf_op jit(solution)/shard_map/inner_sweeps/pallas_call | solution.py:743
  74.2 4.5 %collective-permute-done.3.high_y = f32[32,24,256]{2,1,0:T(8,128)S(1)} collective-permute-done((f32[32,24,256]{2,1,0:T(8,128)S(1)}, f32[32,24,256]{2,1,0:T(8,128)S(1)}, u32[]{:S(2)}, u32[]{:S(2)}) %collective-permute-start.3) | collective-permute-done | bytes 786464 | tf_op jit(solution)/shard_map/ppermute | solution.py:878
  78.7 0.0 collective-permute-done.2.low_y
  78.7 8.5 %edge_sweeps.1 = (f32[3,512,256]{2,1,0:T(8,128)}, f32[512,256]{1,0:T(8,128)}) custom-call(f32[4,5,2,192,128]{4,3,2,1,0:T(8,128)S(1)} %get-tuple-element.23.even_in, f32[4,5,2,192,128]{4,3,2,1,0:T(8,128)S(1)} %get-tuple-element.24.odd_in, f32[2,5,2,192,128]{4,3,2,1,0:T(8,128)S(1)} %get-tuple-element.25.cells_in, ...), custom_call_target="tpu_custom_call" | custom-call | flops 1150000000 | tf_op jit(solution)/shard_map/edge_sweeps/pallas_call | solution.py:843
  87.2 0.0 all-to-all-done.2.moments_in
  87.2 7.5 %settle.1 = (f32[32,16,256]{2,1,0:T(8,128)}, f32[32,16,256]{2,1,0:T(8,128)}) custom-call(s32[8,48]{1,0:T(8,128)S(1)} %bitcast.9, f32[8,3,48,128]{3,2,1,0:T(8,128)} %all-to-all-done.2.moments_in, f32[32,16,256]{2,1,0:T(8,128)} %visc_in.1, f32[32,16,256]{2,1,0:T(8,128)} %dens_in.1), custom_call_target="tpu_custom_call" | custom-call | flops 8049999872 | tf_op jit(solution)/shard_map/settle/pallas_call | solution.py:423
  (3 shorter events, 0.0 us)
Async XLA Ops:
  0.6 13.9 %all-to-all-start = ((s32[8,1,48]{2,1,0:T(1,128)}), s32[8,1,48]{2,1,0:T(1,128)S(1)}, u32[]{:S(2)}, u32[]{:S(2)}) async-start(s32[8,1,48]{2,1,0:T(1,128)} %bitcast.10), calls=%async_computation | async-start | bytes 8192 | tf_op jit(solution)/shard_map/all_to_all | solution.py:892
  6.8 7.8 %copy-start = (f32[3,32,16,256]{3,2,1,0:T(8,128)S(1)}, f32[3,32,16,256]{3,2,1,0:T(8,128)}, u32[]{:S(2)}) copy-start(f32[3,32,16,256]{3,2,1,0:T(8,128)} %vel.5) | copy-start | bytes 4718596
  9.0 17.5 %collective-permute-start = (f32[6,4,16,256]{3,2,1,0:T(8,128)}, f32[6,4,16,256]{3,2,1,0:T(8,128)S(1)}, u32[]{:S(2)}, u32[]{:S(2)}) collective-permute-start(f32[6,4,16,256]{3,2,1,0:T(8,128)} %get-tuple-element.19), channel_id=1, source_target_pairs={{0,8},{8,16},{16,24},{1,9},{9,17},{17,25},{2,10},{10,18},{18,26},{... | collective-permute-start | bytes 1179656 | tf_op jit(solution)/shard_map/ppermute | solution.py:878
  10.9 16.4 %collective-permute-start.1 = (f32[6,4,16,256]{3,2,1,0:T(8,128)}, f32[6,4,16,256]{3,2,1,0:T(8,128)}, u32[]{:S(2)}, u32[]{:S(2)}) collective-permute-start(f32[6,4,16,256]{3,2,1,0:T(8,128)} %get-tuple-element.20), channel_id=1, source_target_pairs={{8,0},{16,8},{24,16},{9,1},{17,9},{25,17},{10,2},{18,10},{26,18},{... | collective-permute-start | bytes 1179656 | tf_op jit(solution)/shard_map/ppermute | solution.py:878
  20.5 20.1 %all-to-all-start.1 = ((f32[8,3,48,128]{3,2,1,0:T(8,128)}), f32[8,3,48,128]{3,2,1,0:T(8,128)}, u32[]{:S(2)}, u32[]{:S(2)}) async-start(f32[8,3,48,128]{3,2,1,0:T(8,128)} %pick_bricks.1), calls=%async_computation.1 | async-start | bytes 1179648 | tf_op jit(solution)/shard_map/all_to_all | solution.py:900
  26.5 14.1 %copy-start.1 = (s32[1,8]{1,0:T(1,128)S(1)}, s32[1,8]{1,0:T(1,128)}, u32[]{:S(2)}) copy-start(s32[1,8]{1,0:T(1,128)} %counts.1) | copy-start | bytes 100
  26.5 0.7 copy-start.2
  30.3 48.4 %collective-permute-start.2 = (f32[34,24,256]{2,1,0:T(8,128)S(1)}, f32[34,24,256]{2,1,0:T(8,128)S(1)}, u32[]{:S(2)}, u32[]{:S(2)}) collective-permute-start(f32[34,24,256]{2,1,0:T(8,128)S(1)} %get-tuple-element.21.refs_6_), channel_id=1, source_target_pairs={{0,1},{1,2},{2,3},{3,4},{4,5},{5,6},{6,7},{8,9},{9,10},{10,11},{11... | collective-permute-start | bytes 2506760 | tf_op jit(solution)/shard_map/ppermute | solution.py:878
  33.7 45.0 %collective-permute-start.3 = (f32[32,24,256]{2,1,0:T(8,128)S(1)}, f32[32,24,256]{2,1,0:T(8,128)S(1)}, u32[]{:S(2)}, u32[]{:S(2)}) collective-permute-start(f32[32,24,256]{2,1,0:T(8,128)S(1)} %get-tuple-element.27), channel_id=1, source_target_pairs={{1,0},{2,1},{3,2},{4,3},{5,4},{6,5},{7,6},{9,8},{10,9},{11,10},{12... | collective-permute-start | bytes 2359304 | tf_op jit(solution)/shard_map/ppermute | solution.py:878
  52.4 34.7 %all-to-all-start.2 = ((f32[8,3,48,128]{3,2,1,0:T(8,128)}), f32[8,3,48,128]{3,2,1,0:T(8,128)}, u32[]{:S(2)}, u32[]{:S(2)}) async-start(f32[8,3,48,128]{3,2,1,0:T(8,128)} %get-tuple-element.22._), calls=%async_computation.2 | async-start | bytes 1179648 | tf_op jit(solution)/shard_map/all_to_all | solution.py:904

commit v3 on v1

--- a/solution.py
+++ b/solution.py
@@ -275,7 +275,7 @@
 
 
 def marker_body(counts, *refs):
-    ins, outs, scratch = refs[:6], refs[7:9], refs[9:]
+    ins, outs, scratch = refs[:6], refs[6:8], refs[8:]
     listed, sums, *flat = scratch
     held = 2 * TOGETHER
     buffers = [flat[n * held : (n + 1) * held] for n in range(len(flat) // held)]
@@ -310,9 +310,20 @@
     lax.fori_loop(0, (number + TOGETHER - 1) // TOGETHER, step, 0)
 
 
-def marker_work(counts, positions, start_visc, marker_dens, bricks, after):
+def by_halves(positions, start_visc, marker_dens):
     owners, _, slots, markers = positions.shape
-    groups, parts = slots // GROUP, slots // HALF
+    parts = slots // HALF
+    return (
+        positions.reshape(owners, 3, parts, HALF, markers),
+        start_visc.reshape(owners, parts, HALF, markers),
+        marker_dens.reshape(owners, parts, HALF, markers),
+    )
+
+
+def marker_work(counts, positions, start_visc, marker_dens, bricks):
+    owners, _, parts, _, markers = positions.shape
+    slots = parts * HALF
+    groups = slots // GROUP
     spread, gather = permutations()
     width = 4 * BZ * HALF
     whole = pl.BlockSpec(memory_space=pltpu.VMEM)
@@ -333,8 +344,7 @@
             jax.ShapeDtypeStruct((owners, groups, ROWS, LANES), f32),
         ),
         in_specs=[pl.BlockSpec(memory_space=pltpu.SMEM)]
-        + [whole] * 6
-        + [pl.BlockSpec(memory_space=pl.ANY)],
+        + [whole] * 6,
         out_specs=(whole, whole),
         scratch_shapes=[
             pltpu.SMEM((2 * (owners * groups + TOGETHER),), jnp.int32),
@@ -346,15 +356,12 @@
         name="marker_work",
     )(
         counts,
-        *in_hbm(
-            spread,
-            gather,
-            positions.reshape(owners, 3, parts, HALF, markers),
-            start_visc.reshape(owners, parts, HALF, markers),
-            marker_dens.reshape(owners, parts, HALF, markers),
-            bricks,
-        ),
-        after,
+        *in_hbm(spread, gather),
+        *[
+            pltpu.with_memory_space_constraint(array, pltpu.VMEM)
+            for array in (positions, start_visc, marker_dens)
+        ],
+        *in_hbm(bricks),
     )
     return visc.reshape(owners, slots, markers), moments
 
@@ -494,7 +501,18 @@
     return [cell + at for cell, at in zip(found, places)], size_x + -(-more // (6 * width))
 
 
-def pack_y_body(size_x, vel, pres, visc, dens, low_x, high_x, upward, downward):
+def pack_y_body(size_x, vel, pres, visc, dens, low_x, high_x, *refs):
+    sources, (upward, downward), targets, done = refs[:3], refs[3:5], refs[5:8], refs[8]
+    fetches = [
+        pltpu.make_async_copy(source, target, done.at[n])
+        for n, (source, target) in enumerate(zip(sources, targets))
+    ]
+
+    @pl.when(pl.program_id(0) == 0)
+    def _():
+        for fetch in fetches:
+            fetch.start()
+
     step_x, size_y, _ = pres.shape
     width = SWEEPS
     step = pl.program_id(0)
@@ -511,18 +529,22 @@
             for f, side, far_x, far_y, plane, row in corner_rows(up, size_x)[0]:
                 halo, at = (high_x, far_x - 1) if side else (low_x, width - far_x)
                 face[plane, row] = halo[f, at, size_y - far_y if up else far_y - 1]
-
-
-def pack_y(velocity, pressure, cell_visc, cell_dens, low_x, high_x):
+        for fetch in fetches:
+            fetch.wait()
+
+
+def pack_y(velocity, pressure, cell_visc, cell_dens, low_x, high_x, *fetched):
     size_x, size_y, size_z = cell_visc.shape
     step = 8
     block = pl.BlockSpec((step, size_y, size_z), lambda i: (i, 0, 0))
     halo = pl.BlockSpec(low_x.shape, lambda i: (0, 0, 0, 0))
+    anywhere = pl.BlockSpec(memory_space=pl.ANY)
     shapes = [(corner_rows(up, size_x)[1], 6 * SWEEPS, size_z) for up in (True, False)]
     return pl.pallas_call(
         functools.partial(pack_y_body, size_x),
         grid=(size_x // step,),
-        out_shape=tuple(jax.ShapeDtypeStruct(shape, f32) for shape in shapes),
+        out_shape=tuple(jax.ShapeDtypeStruct(shape, f32) for shape in shapes)
+        + tuple(pltpu.VMEM(array.shape, f32) for array in fetched),
         in_specs=[
             pl.BlockSpec((3, step, size_y, size_z), lambda i: (0, i, 0, 0)),
             block,
@@ -530,12 +552,15 @@
             block,
             halo,
             halo,
-        ],
-        out_specs=tuple(pl.BlockSpec(shape, lambda i: (0, 0, 0)) for shape in shapes),
+        ]
+        + [anywhere] * len(fetched),
+        out_specs=tuple(pl.BlockSpec(shape, lambda i: (0, 0, 0)) for shape in shapes)
+        + (anywhere,) * len(fetched),
+        scratch_shapes=[pltpu.SemaphoreType.DMA((3,))],
         compiler_params=vmem_limit(24),
         cost_estimate=cost(15),
         name="pack_y",
-    )(*in_hbm(velocity, pressure, cell_visc, cell_dens), low_x, high_x)
+    )(*in_hbm(velocity, pressure, cell_visc, cell_dens, low_x, high_x, *fetched))
 
 
 def place(per, x, y, rows):
@@ -750,7 +775,7 @@
         compiler_params=vmem_limit(40),
         cost_estimate=cost(25),
         name="inner_sweeps",
-    )(*in_hbm(velocity, pressure, cell_visc, cell_dens), low_x, high_x, after)
+    )(*in_hbm(velocity, pressure, cell_visc, cell_dens, low_x, high_x), after)
 
 
 def edge_body(even_in, odd_in, cells_in, low_y, high_y, vel_out, pres_out, *work):
@@ -876,14 +901,13 @@
     fields = (velocity, pressure, cell_visc, cell_dens)
     to_low, to_high = pack_x(*fields)
     low_x, high_x = shift(to_high, "grid", 1), shift(to_low, "grid", -1)
-    upward, downward = pack_y(*fields, low_x, high_x)
+    marker_data = by_halves(positions, start_visc, marker_dens)
+    upward, downward, *marker_data = pack_y(*fields, low_x, high_x, *marker_data)
     low_y, high_y = shift(upward, "mark", 1), shift(downward, "mark", -1)
 
     picked = pick_bricks(asked, velocity)
     bricks = lax.all_to_all(picked, "mark", 0, 0, tiled=True)
-    marker_visc, moments = marker_work(
-        block_counts, positions, start_visc, marker_dens, bricks, upward
-    )
+    marker_visc, moments = marker_work(block_counts, *marker_data, bricks)
     gathered = lax.all_to_all(moments, "mark", 0, 0, tiled=True)
     state = inner_sweeps(*fields, low_x, high_x, moments)
     velocity_next, pressure_next = edge_sweeps(*state, low_y, high_y, *pressure.shape[:2])

time: 94.9 us -> 96.2 us (1.014)
  the two profiles are of different devices: /device:TPU:10 before, /device:TPU:18 now
where the time goes in v3:
time: 96.2 us; the launch traced here: 95.1 us
  Pallas kernels  55.8 us (58%)
  starting transfers between devices  31.8 us (33%)
  local copies, waits for them, and re-layouts  6.61 us (7%)
    pallas_call x1, Pallas kernels, marker_work(): pl.pallas_call(marker_body, out_shape=(jax.ShapeDtypeStruct((owners, part...  18.2 us
    ppermute x4, starting transfers between devices, shift(): return lax.ppermute(value, axis, pairs)  12.3 us
    pallas_call x1, Pallas kernels, inner_sweeps(): pl.pallas_call(inner_body, out_shape=tuple((jax.ShapeDtypeStruct(shape, f...  10.3 us
    pallas_call x1, Pallas kernels, edge_sweeps(): pl.pallas_call(edge_body, out_shape=(jax.ShapeDtypeStruct((3, size_x, siz...  8.12 us
    pallas_call x1, Pallas kernels, settle(): pl.pallas_call(settle_body, out_shape=(shape, shape), in_specs=[pl.BlockS...  7.48 us
    all_to_all x1, starting transfers between devices, per_device(): gathered = lax.all_to_all(moments, 'mark', 0, 0, tiled=True)  7.34 us
    unnamed x20, local copies, waits for them, and re-layouts  6.61 us
    all_to_all x1, starting transfers between devices, per_device(): asked = lax.all_to_all(block_brick, 'mark', 0, 0, tiled=True)  6.18 us
  transfers between devices with their start and end apart: 7, of which 1 were waited for; matrix products, arithmetic and copies ran while one was open for 0% of the time, Pallas kernels for 51%

profile of v3, /device:TPU:18, one launch (start us, length us, event | category | flops | bytes accessed | tf_op | source)
XLA Modules:
  0.0 95.1 jit_solution(12769699909821877532)
XLA Ops:
  0.6 6.2 %all-to-all-start = ((s32[8,1,48]{2,1,0:T(1,128)}), s32[8,1,48]{2,1,0:T(1,128)S(1)}, u32[]{:S(2)}, u32[]{:S(2)}) async-start(s32[8,1,48]{2,1,0:T(1,128)} %bitcast.8), calls=%async_computation | async-start | bytes 8192 | tf_op jit(solution)/shard_map/all_to_all | solution.py:900
  6.8 2.2 %pack_x.1 = (f32[6,4,16,256]{3,2,1,0:T(8,128)}, f32[6,4,16,256]{3,2,1,0:T(8,128)}) custom-call(f32[3,32,16,256]{3,2,1,0:T(8,128)} %vel.5, f32[3,32,16,256]{3,2,1,0:T(8,128)} %vel.5, f32[32,16,256]{2,1,0:T(8,128)} %pres.3, f32[32,16,256]{2,1,0:T(8,128)} %pres.3, f32[32,16,256]{2,1,0:T(8,128)} %visc_in.1, f32[32,16,256]{2,1,0:T(8,128)} %visc_in.1, ...), custom_call_target="tpu_custom_call" | custom-call | flops 2300000000 | tf_op jit(solution)/shard_map/pack_x/pallas_call | solution.py:475
  9.0 1.9 %collective-permute-start = (f32[6,4,16,256]{3,2,1,0:T(8,128)}, f32[6,4,16,256]{3,2,1,0:T(8,128)S(1)}, u32[]{:S(2)}, u32[]{:S(2)}) collective-permute-start(f32[6,4,16,256]{3,2,1,0:T(8,128)} %get-tuple-element.21), channel_id=1, source_target_pairs={{0,8},{8,16},{16,24},{1,9},{9,17},{17,25},{2,10},{10,18},{18,26},{... | collective-permute-start | bytes 1179656 | tf_op jit(solution)/shard_map/ppermute | solution.py:886
  10.9 3.6 %collective-permute-start.1 = (f32[6,4,16,256]{3,2,1,0:T(8,128)}, f32[6,4,16,256]{3,2,1,0:T(8,128)S(1)}, u32[]{:S(2)}, u32[]{:S(2)}) collective-permute-start(f32[6,4,16,256]{3,2,1,0:T(8,128)} %get-tuple-element.22), channel_id=1, source_target_pairs={{8,0},{16,8},{24,16},{9,1},{17,9},{25,17},{10,2},{18,10},{26,18},{... | collective-permute-start | bytes 1179656 | tf_op jit(solution)/shard_map/ppermute | solution.py:886
  14.6 6.0 %pick_bricks.1 = f32[8,3,48,128]{3,2,1,0:T(8,128)} custom-call(s32[8,48]{1,0:T(8,128)S(1)} %bitcast.6, f32[3,32,16,256]{3,2,1,0:T(8,128)S(1)} %copy-done), custom_call_target="tpu_custom_call" | custom-call | flops 28750000128 | tf_op jit(solution)/shard_map/pick_bricks/pallas_call | solution.py:86
  20.5 6.0 %all-to-all-start.1 = ((f32[8,3,48,128]{3,2,1,0:T(8,128)}), f32[8,3,48,128]{3,2,1,0:T(8,128)}, u32[]{:S(2)}, u32[]{:S(2)}) async-start(f32[8,3,48,128]{3,2,1,0:T(8,128)} %pick_bricks.1), calls=%async_computation.1 | async-start | bytes 1179648 | tf_op jit(solution)/shard_map/all_to_all | solution.py:909
  26.5 0.0 copy-start.9
  26.6 0.7 copy-done.8
  27.3 0.1 copy-done.9
  27.4 3.6 %pack_y.1 = (f32[34,24,256]{2,1,0:T(8,128)S(1)}, f32[32,24,256]{2,1,0:T(8,128)S(1)}, f32[8,3,6,8,256]{4,3,2,1,0:T(8,128)S(1)}, f32[8,6,8,256]{3,2,1,0:T(8,128)S(1)}, f32[8,6,8,256]{3,2,1,0:T(8,128)S(1)}) custom-call(f32[3,32,16,256]{3,2,1,0:T(8,128)} %vel.5, f32[32,16,256]{2,1,0:T(8,128)} %pres.3, f32[32,16,256]{2,1,0:T(8,128)} %visc_in.1, ...), custom_call_target="tpu_custom_call" | custom-call | flops 17250000896 | tf_op jit(solution)/shard_map/pack_y/pallas_call | solution.py:543
  31.0 1.0 %copy-done.2 = f32[8,3,6,8,256]{4,3,2,1,0:T(8,128)} copy-done((f32[8,3,6,8,256]{4,3,2,1,0:T(8,128)}, f32[8,3,6,8,256]{4,3,2,1,0:T(8,128)S(1)}, u32[]{:S(2)}) %copy-start.2) | copy-done | bytes 1179672
  32.0 0.7 copy-done.4
  32.7 0.7 copy-done.6
  33.5 3.4 %collective-permute-start.2 = (f32[34,24,256]{2,1,0:T(8,128)S(1)}, f32[34,24,256]{2,1,0:T(8,128)S(1)}, u32[]{:S(2)}, u32[]{:S(2)}) collective-permute-start(f32[34,24,256]{2,1,0:T(8,128)S(1)} %get-tuple-element.30), channel_id=1, source_target_pairs={{0,1},{1,2},{2,3},{3,4},{4,5},{5,6},{6,7},{8,9},{9,10},{10,11},{11... | collective-permute-start | bytes 2506760 | tf_op jit(solution)/shard_map/ppermute | solution.py:886
  36.9 3.4 %collective-permute-start.3 = (f32[32,24,256]{2,1,0:T(8,128)S(1)}, f32[32,24,256]{2,1,0:T(8,128)S(1)}, u32[]{:S(2)}, u32[]{:S(2)}) collective-permute-start(f32[32,24,256]{2,1,0:T(8,128)S(1)} %get-tuple-element.31), channel_id=1, source_target_pairs={{1,0},{2,1},{3,2},{4,3},{5,4},{6,5},{7,6},{9,8},{10,9},{11,10},{12... | collective-permute-start | bytes 2359304 | tf_op jit(solution)/shard_map/ppermute | solution.py:886
  40.3 1.3 %copy-done.3 = f32[8,3,6,8,256]{4,3,2,1,0:T(8,128)S(1)} copy-done((f32[8,3,6,8,256]{4,3,2,1,0:T(8,128)S(1)}, f32[8,3,6,8,256]{4,3,2,1,0:T(8,128)}, u32[]{:S(2)}) %copy-start.3) | copy-done | bytes 1179672
  41.5 1.0 %copy-done.5 = f32[8,6,8,256]{3,2,1,0:T(8,128)S(1)} copy-done((f32[8,6,8,256]{3,2,1,0:T(8,128)S(1)}, f32[8,6,8,256]{3,2,1,0:T(8,128)}, u32[]{:S(2)}) %copy-start.5) | copy-done | bytes 393240
  42.5 1.0 %copy-done.7 = f32[8,6,8,256]{3,2,1,0:T(8,128)S(1)} copy-done((f32[8,6,8,256]{3,2,1,0:T(8,128)S(1)}, f32[8,6,8,256]{3,2,1,0:T(8,128)}, u32[]{:S(2)}) %copy-start.7) | copy-done | bytes 393240
  43.5 18.2 %marker_work.1 = (f32[8,6,8,256]{3,2,1,0:T(8,128)}, f32[8,3,48,128]{3,2,1,0:T(8,128)}) custom-call(s32[1,8]{1,0:T(1,128)S(1)} %copy-done.1, bf16[2,2,128,256]{3,2,1,0:T(8,128)(2,1)} %constant.4.clone.refs_0_, bf16[512,512]{1,0:T(8,128)(2,1)} %constant.5.clone.refs_1_, f32[8,3,6,8,256]{4,3,2,1,0:T(8,128)S(1)} %copy-done.3, f32[8,6,8,256]{3,2,1,0:T(8,128)S(1)} %copy-done.5, ...), custom_call_target="tpu_custom_call" | custom-call | flops 28750000128 | tf_op jit(solution)/shard_map/marker_work/pallas_call | solution.py:340
  61.7 7.3 %all-to-all-start.2 = ((f32[8,3,48,128]{3,2,1,0:T(8,128)}), f32[8,3,48,128]{3,2,1,0:T(8,128)}, u32[]{:S(2)}, u32[]{:S(2)}) async-start(f32[8,3,48,128]{3,2,1,0:T(8,128)} %get-tuple-element.26._), calls=%async_computation.2 | async-start | bytes 1179648 | tf_op jit(solution)/shard_map/all_to_all | solution.py:911
  69.0 10.3 %inner_sweeps.1 = (f32[4,5,2,192,128]{4,3,2,1,0:T(8,128)S(1)}, f32[4,5,2,192,128]{4,3,2,1,0:T(8,128)S(1)}, f32[2,5,2,192,128]{4,3,2,1,0:T(8,128)S(1)}) custom-call(f32[3,32,16,256]{3,2,1,0:T(8,128)} %vel.5, f32[32,16,256]{2,1,0:T(8,128)} %pres.3, f32[32,16,256]{2,1,0:T(8,128)} %visc_in.1, f32[32,16,256]{2,1,0:T(8,128)} %dens_in.1, ...), custom_call_target="tpu_custom_call" | custom-call | flops 28750000128 | tf_op jit(solution)/shard_map/inner_sweeps/pallas_call | solution.py:758
  79.4 0.1 collective-permute-done.3.high_y
  79.5 8.1 %edge_sweeps.1 = (f32[3,32,16,256]{3,2,1,0:T(8,128)}, f32[32,16,256]{2,1,0:T(8,128)}) custom-call(f32[4,5,2,192,128]{4,3,2,1,0:T(8,128)S(1)} %get-tuple-element.27.even_in, f32[4,5,2,192,128]{4,3,2,1,0:T(8,128)S(1)} %get-tuple-element.28.odd_in, f32[2,5,2,192,128]{4,3,2,1,0:T(8,128)S(1)} %get-tuple-element.29.cells_in, ...), custom_call_target="tpu_custom_call" | custom-call | flops 1150000000 | tf_op jit(solution)/shard_map/edge_sweeps/pallas_call | solution.py:855
  87.6 7.5 %settle.1 = (f32[32,16,256]{2,1,0:T(8,128)}, f32[32,16,256]{2,1,0:T(8,128)}) custom-call(s32[8,48]{1,0:T(8,128)S(1)} %bitcast.7, f32[8,3,48,128]{3,2,1,0:T(8,128)} %all-to-all-done.2.moments_in, f32[32,16,256]{2,1,0:T(8,128)} %visc_in.1, f32[32,16,256]{2,1,0:T(8,128)} %dens_in.1), custom_call_target="tpu_custom_call" | custom-call | flops 8049999872 | tf_op jit(solution)/shard_map/settle/pallas_call | solution.py:435
  (17 shorter events, 0.0 us)
Async XLA Ops:
  0.6 13.9 %all-to-all-start = ((s32[8,1,48]{2,1,0:T(1,128)}), s32[8,1,48]{2,1,0:T(1,128)S(1)}, u32[]{:S(2)}, u32[]{:S(2)}) async-start(s32[8,1,48]{2,1,0:T(1,128)} %bitcast.8), calls=%async_computation | async-start | bytes 8192 | tf_op jit(solution)/shard_map/all_to_all | solution.py:900
  6.8 7.8 %copy-start = (f32[3,32,16,256]{3,2,1,0:T(8,128)S(1)}, f32[3,32,16,256]{3,2,1,0:T(8,128)}, u32[]{:S(2)}) copy-start(f32[3,32,16,256]{3,2,1,0:T(8,128)} %vel.5) | copy-start | bytes 4718596
  9.0 17.5 %collective-permute-start = (f32[6,4,16,256]{3,2,1,0:T(8,128)}, f32[6,4,16,256]{3,2,1,0:T(8,128)S(1)}, u32[]{:S(2)}, u32[]{:S(2)}) collective-permute-start(f32[6,4,16,256]{3,2,1,0:T(8,128)} %get-tuple-element.21), channel_id=1, source_target_pairs={{0,8},{8,16},{16,24},{1,9},{9,17},{17,25},{2,10},{10,18},{18,26},{... | collective-permute-start | bytes 1179656 | tf_op jit(solution)/shard_map/ppermute | solution.py:886
  10.9 15.6 %collective-permute-start.1 = (f32[6,4,16,256]{3,2,1,0:T(8,128)}, f32[6,4,16,256]{3,2,1,0:T(8,128)S(1)}, u32[]{:S(2)}, u32[]{:S(2)}) collective-permute-start(f32[6,4,16,256]{3,2,1,0:T(8,128)} %get-tuple-element.22), channel_id=1, source_target_pairs={{8,0},{16,8},{24,16},{9,1},{17,9},{25,17},{10,2},{18,10},{26,18},{... | collective-permute-start | bytes 1179656 | tf_op jit(solution)/shard_map/ppermute | solution.py:886
  20.5 19.7 %all-to-all-start.1 = ((f32[8,3,48,128]{3,2,1,0:T(8,128)}), f32[8,3,48,128]{3,2,1,0:T(8,128)}, u32[]{:S(2)}, u32[]{:S(2)}) async-start(f32[8,3,48,128]{3,2,1,0:T(8,128)} %pick_bricks.1), calls=%async_computation.1 | async-start | bytes 1179648 | tf_op jit(solution)/shard_map/all_to_all | solution.py:909
  26.5 0.7 copy-start.8
  26.5 0.9 copy-start.9
  27.4 12.8 %copy-start.1 = (s32[1,8]{1,0:T(1,128)S(1)}, s32[1,8]{1,0:T(1,128)}, u32[]{:S(2)}) copy-start(s32[1,8]{1,0:T(1,128)} %counts.1) | copy-start | bytes 100
  31.0 1.0 %copy-start.2 = (f32[8,3,6,8,256]{4,3,2,1,0:T(8,128)}, f32[8,3,6,8,256]{4,3,2,1,0:T(8,128)S(1)}, u32[]{:S(2)}) copy-start(f32[8,3,6,8,256]{4,3,2,1,0:T(8,128)S(1)} %get-tuple-element.23.refs_2_) | copy-start | bytes 3538948
  32.0 0.7 copy-start.4
  32.7 0.7 copy-start.6
  33.5 46.0 %collective-permute-start.2 = (f32[34,24,256]{2,1,0:T(8,128)S(1)}, f32[34,24,256]{2,1,0:T(8,128)S(1)}, u32[]{:S(2)}, u32[]{:S(2)}) collective-permute-start(f32[34,24,256]{2,1,0:T(8,128)S(1)} %get-tuple-element.30), channel_id=1, source_target_pairs={{0,1},{1,2},{2,3},{3,4},{4,5},{5,6},{6,7},{8,9},{9,10},{10,11},{11... | collective-permute-start | bytes 2506760 | tf_op jit(solution)/shard_map/ppermute | solution.py:886
  36.9 42.6 %collective-permute-start.3 = (f32[32,24,256]{2,1,0:T(8,128)S(1)}, f32[32,24,256]{2,1,0:T(8,128)S(1)}, u32[]{:S(2)}, u32[]{:S(2)}) collective-permute-start(f32[32,24,256]{2,1,0:T(8,128)S(1)} %get-tuple-element.31), channel_id=1, source_target_pairs={{1,0},{2,1},{3,2},{4,3},{5,4},{6,5},{7,6},{9,8},{10,9},{11,10},{12... | collective-permute-start | bytes 2359304 | tf_op jit(solution)/shard_map/ppermute | solution.py:886
  40.3 1.3 %copy-start.3 = (f32[8,3,6,8,256]{4,3,2,1,0:T(8,128)S(1)}, f32[8,3,6,8,256]{4,3,2,1,0:T(8,128)}, u32[]{:S(2)}) copy-start(f32[8,3,6,8,256]{4,3,2,1,0:T(8,128)} %copy-done.2) | copy-start | bytes 3538948
  41.5 1.0 %copy-start.5 = (f32[8,6,8,256]{3,2,1,0:T(8,128)S(1)}, f32[8,6,8,256]{3,2,1,0:T(8,128)}, u32[]{:S(2)}) copy-start(f32[8,6,8,256]{3,2,1,0:T(8,128)} %copy-done.4) | copy-start | bytes 1179652
  42.5 1.0 %copy-start.7 = (f32[8,6,8,256]{3,2,1,0:T(8,128)S(1)}, f32[8,6,8,256]{3,2,1,0:T(8,128)}, u32[]{:S(2)}) copy-start(f32[8,6,8,256]{3,2,1,0:T(8,128)} %copy-done.6) | copy-start | bytes 1179652
  61.7 25.9 %all-to-all-start.2 = ((f32[8,3,48,128]{3,2,1,0:T(8,128)}), f32[8,3,48,128]{3,2,1,0:T(8,128)}, u32[]{:S(2)}, u32[]{:S(2)}) async-start(f32[8,3,48,128]{3,2,1,0:T(8,128)} %get-tuple-element.26._), calls=%async_computation.2 | async-start | bytes 1179648 | tf_op jit(solution)/shard_map/all_to_all | solution.py:911

commit v4 on v1

--- a/solution.py
+++ b/solution.py
@@ -271,7 +271,7 @@
             moments_out[owner, group, rows, :] = mine[:, j * LANES : (j + 1) * LANES]
 
 
-TOGETHER = 2
+TOGETHER = 3
 
 
 def marker_body(counts, *refs):
@@ -437,7 +437,7 @@
             pltpu.VMEM(cell_visc.shape, f32),
             pltpu.SemaphoreType.DMA((3,)),
         ]
-        + [pltpu.VMEM((places, ROWS, LANES), f32)] * 2,
+        + [pltpu.VMEM((places, ROWS, LANES), f32)],
         compiler_params=vmem_limit(24),
         cost_estimate=cost(7),
         name="settle",
@@ -535,7 +535,7 @@
         compiler_params=vmem_limit(24),
         cost_estimate=cost(15),
         name="pack_y",
-    )(*in_hbm(velocity, pressure, cell_visc, cell_dens), low_x, high_x)
+    )(*in_hbm(velocity, pressure, cell_visc, cell_dens, low_x, high_x))
 
 
 def place(per, x, y, rows):
@@ -750,7 +750,7 @@
         compiler_params=vmem_limit(40),
         cost_estimate=cost(25),
         name="inner_sweeps",
-    )(*in_hbm(velocity, pressure, cell_visc, cell_dens), low_x, high_x, after)
+    )(*in_hbm(velocity, pressure, cell_visc, cell_dens, low_x, high_x), after)
 
 
 def edge_body(even_in, odd_in, cells_in, low_y, high_y, vel_out, pres_out, *work):

time: 94.9 us -> 94.3 us (level)
  the two profiles are of different devices: /device:TPU:10 before, /device:TPU:18 now
where the time goes in v4:
time: 94.3 us; the launch traced here: 93.3 us
  Pallas kernels  48.9 us (52%)
  starting transfers between devices  39.3 us (42%)
  waiting for transfers between devices  2.96 us (3%)
  local copies, waits for them, and re-layouts  1.48 us (2%)
    all_to_all x1, starting transfers between devices, per_device(): gathered = lax.all_to_all(moments, 'mark', 0, 0, tiled=True)  14.8 us
    ppermute x4, starting transfers between devices, shift(): return lax.ppermute(value, axis, pairs)  12.3 us
    pallas_call x1, Pallas kernels, marker_work(): pl.pallas_call(marker_body, out_shape=(jax.ShapeDtypeStruct((owners, part...  12.1 us
    pallas_call x1, Pallas kernels, inner_sweeps(): pl.pallas_call(inner_body, out_shape=tuple((jax.ShapeDtypeStruct(shape, f...  10.3 us
    pallas_call x1, Pallas kernels, edge_sweeps(): pl.pallas_call(edge_body, out_shape=(jax.ShapeDtypeStruct((3, size_x, siz...  8.07 us
    pallas_call x1, Pallas kernels, settle(): pl.pallas_call(settle_body, out_shape=(shape, shape), in_specs=[pl.BlockS...  7.28 us
    all_to_all x1, starting transfers between devices, per_device(): asked = lax.all_to_all(block_brick, 'mark', 0, 0, tiled=True)  6.18 us
    all_to_all x1, starting transfers between devices, per_device(): bricks = lax.all_to_all(picked, 'mark', 0, 0, tiled=True)  6 us
  transfers between devices with their start and end apart: 7, of which 2 were waited for; matrix products, arithmetic and copies ran while one was open for 0% of the time, Pallas kernels for 45%

profile of v4, /device:TPU:18, one launch (start us, length us, event | category | flops | bytes accessed | tf_op | source)
XLA Modules:
  0.0 93.3 jit_solution(7709995440730189714)
XLA Ops:
  0.6 6.2 %all-to-all-start = ((s32[8,1,48]{2,1,0:T(1,128)}), s32[8,1,48]{2,1,0:T(1,128)S(1)}, u32[]{:S(2)}, u32[]{:S(2)}) async-start(s32[8,1,48]{2,1,0:T(1,128)} %bitcast.8), calls=%async_computation | async-start | bytes 8192 | tf_op jit(solution)/shard_map/all_to_all | solution.py:875
  6.8 2.2 %pack_x.1 = (f32[6,4,16,256]{3,2,1,0:T(8,128)}, f32[6,4,16,256]{3,2,1,0:T(8,128)}) custom-call(f32[3,32,16,256]{3,2,1,0:T(8,128)} %vel.5, f32[3,32,16,256]{3,2,1,0:T(8,128)} %vel.5, f32[32,16,256]{2,1,0:T(8,128)} %pres.3, f32[32,16,256]{2,1,0:T(8,128)} %pres.3, f32[32,16,256]{2,1,0:T(8,128)} %visc_in.1, f32[32,16,256]{2,1,0:T(8,128)} %visc_in.1, ...), custom_call_target="tpu_custom_call" | custom-call | flops 2300000000 | tf_op jit(solution)/shard_map/pack_x/pallas_call | solution.py:468
  9.0 1.9 %collective-permute-start = (f32[6,4,16,256]{3,2,1,0:T(8,128)}, f32[6,4,16,256]{3,2,1,0:T(8,128)S(1)}, u32[]{:S(2)}, u32[]{:S(2)}) collective-permute-start(f32[6,4,16,256]{3,2,1,0:T(8,128)} %get-tuple-element.18), channel_id=1, source_target_pairs={{0,8},{8,16},{16,24},{1,9},{9,17},{17,25},{2,10},{10,18},{18,26},{... | collective-permute-start | bytes 1179656 | tf_op jit(solution)/shard_map/ppermute | solution.py:861
  10.9 3.6 %collective-permute-start.1 = (f32[6,4,16,256]{3,2,1,0:T(8,128)}, f32[6,4,16,256]{3,2,1,0:T(8,128)S(1)}, u32[]{:S(2)}, u32[]{:S(2)}) collective-permute-start(f32[6,4,16,256]{3,2,1,0:T(8,128)} %get-tuple-element.19), channel_id=1, source_target_pairs={{8,0},{16,8},{24,16},{9,1},{17,9},{25,17},{10,2},{18,10},{26,18},{... | collective-permute-start | bytes 1179656 | tf_op jit(solution)/shard_map/ppermute | solution.py:861
  14.5 0.0 all-to-all-done
  14.6 5.9 %pick_bricks.1 = f32[8,3,48,128]{3,2,1,0:T(8,128)} custom-call(s32[8,48]{1,0:T(8,128)S(1)} %bitcast.6, f32[3,32,16,256]{3,2,1,0:T(8,128)S(1)} %copy-done), custom_call_target="tpu_custom_call" | custom-call | flops 28750000128 | tf_op jit(solution)/shard_map/pick_bricks/pallas_call | solution.py:86
  20.5 6.0 %all-to-all-start.1 = ((f32[8,3,48,128]{3,2,1,0:T(8,128)}), f32[8,3,48,128]{3,2,1,0:T(8,128)}, u32[]{:S(2)}, u32[]{:S(2)}) async-start(f32[8,3,48,128]{3,2,1,0:T(8,128)} %pick_bricks.1), calls=%async_computation.1 | async-start | bytes 1179648 | tf_op jit(solution)/shard_map/all_to_all | solution.py:883
  26.5 0.0 collective-permute-done.low_x
  26.5 0.0 copy-start.2
  26.5 0.0 collective-permute-done.1.high_x
  26.5 0.7 copy-done.2
  27.3 0.7 copy-done.3
  28.0 3.0 %pack_y.1 = (f32[34,24,256]{2,1,0:T(8,128)S(1)}, f32[32,24,256]{2,1,0:T(8,128)S(1)}) custom-call(f32[3,32,16,256]{3,2,1,0:T(8,128)} %vel.5, f32[32,16,256]{2,1,0:T(8,128)} %pres.3, f32[32,16,256]{2,1,0:T(8,128)} %visc_in.1, f32[32,16,256]{2,1,0:T(8,128)} %dens_in.1, f32[6,4,16,256]{3,2,1,0:T(8,128)} %copy-done.2, f32[6,4,16,256]{3,2,1,0:T(8,128)} %copy-done.3), custom_call_target="tpu_custom_call" | custom-call | flops 17250000896 | tf_op jit(solution)/shard_map/pack_y/pallas_call | solution.py:522
  31.0 3.4 %collective-permute-start.2 = (f32[34,24,256]{2,1,0:T(8,128)S(1)}, f32[34,24,256]{2,1,0:T(8,128)S(1)}, u32[]{:S(2)}, u32[]{:S(2)}) collective-permute-start(f32[34,24,256]{2,1,0:T(8,128)S(1)} %get-tuple-element.20.refs_6_), channel_id=1, source_target_pairs={{0,1},{1,2},{2,3},{3,4},{4,5},{5,6},{6,7},{8,9},{9,10},{10,11},{11... | collective-permute-start | bytes 2506760 | tf_op jit(solution)/shard_map/ppermute | solution.py:861
  34.4 3.4 %collective-permute-start.3 = (f32[32,24,256]{2,1,0:T(8,128)S(1)}, f32[32,24,256]{2,1,0:T(8,128)S(1)}, u32[]{:S(2)}, u32[]{:S(2)}) collective-permute-start(f32[32,24,256]{2,1,0:T(8,128)S(1)} %get-tuple-element.25), channel_id=1, source_target_pairs={{1,0},{2,1},{3,2},{4,3},{5,4},{6,5},{7,6},{9,8},{10,9},{11,10},{12... | collective-permute-start | bytes 2359304 | tf_op jit(solution)/shard_map/ppermute | solution.py:861
  37.8 2.2 %all-to-all-done.1.refs_5_ = f32[8,3,48,128]{3,2,1,0:T(8,128)} async-done(((f32[8,3,48,128]{3,2,1,0:T(8,128)}), f32[8,3,48,128]{3,2,1,0:T(8,128)}, u32[]{:S(2)}, u32[]{:S(2)}) %all-to-all-start.1) | async-done | bytes 589856 | tf_op jit(solution)/shard_map/all_to_all | solution.py:883
  40.0 12.1 %marker_work.1 = (f32[8,6,8,256]{3,2,1,0:T(8,128)}, f32[8,3,48,128]{3,2,1,0:T(8,128)}) custom-call(s32[1,8]{1,0:T(1,128)S(1)} %copy-done.1, bf16[2,2,128,256]{3,2,1,0:T(8,128)(2,1)} %constant.4.clone.refs_0_, bf16[512,512]{1,0:T(8,128)(2,1)} %constant.5.clone.refs_1_, f32[8,3,6,8,256]{4,3,2,1,0:T(8,128)} %bitcast.9, f32[8,6,8,256]{3,2,1,0:T(8,128)} %bitcast.10, ...), custom_call_target="tpu_custom_call" | custom-call | flops 28750000128 | tf_op jit(solution)/shard_map/marker_work/pallas_call | solution.py:329
  52.1 14.8 %all-to-all-start.2 = ((f32[8,3,48,128]{3,2,1,0:T(8,128)}), f32[8,3,48,128]{3,2,1,0:T(8,128)}, u32[]{:S(2)}, u32[]{:S(2)}) async-start(f32[8,3,48,128]{3,2,1,0:T(8,128)} %get-tuple-element.21._), calls=%async_computation.2 | async-start | bytes 1179648 | tf_op jit(solution)/shard_map/all_to_all | solution.py:887
  66.9 10.3 %inner_sweeps.1 = (f32[4,5,2,192,128]{4,3,2,1,0:T(8,128)S(1)}, f32[4,5,2,192,128]{4,3,2,1,0:T(8,128)S(1)}, f32[2,5,2,192,128]{4,3,2,1,0:T(8,128)S(1)}) custom-call(f32[3,32,16,256]{3,2,1,0:T(8,128)} %vel.5, f32[32,16,256]{2,1,0:T(8,128)} %pres.3, f32[32,16,256]{2,1,0:T(8,128)} %visc_in.1, f32[32,16,256]{2,1,0:T(8,128)} %dens_in.1, ...), custom_call_target="tpu_custom_call" | custom-call | flops 28750000128 | tf_op jit(solution)/shard_map/inner_sweeps/pallas_call | solution.py:733
  77.2 0.8 collective-permute-done.3.high_y
  77.9 0.0 collective-permute-done.2.low_y
  77.9 8.1 %edge_sweeps.1 = (f32[3,32,16,256]{3,2,1,0:T(8,128)}, f32[32,16,256]{2,1,0:T(8,128)}) custom-call(f32[4,5,2,192,128]{4,3,2,1,0:T(8,128)S(1)} %get-tuple-element.22.even_in, f32[4,5,2,192,128]{4,3,2,1,0:T(8,128)S(1)} %get-tuple-element.23.odd_in, f32[2,5,2,192,128]{4,3,2,1,0:T(8,128)S(1)} %get-tuple-element.24.cells_in, ...), custom_call_target="tpu_custom_call" | custom-call | flops 1150000000 | tf_op jit(solution)/shard_map/edge_sweeps/pallas_call | solution.py:830
  86.0 0.0 all-to-all-done.2.moments_in
  86.0 7.3 %settle.1 = (f32[32,16,256]{2,1,0:T(8,128)}, f32[32,16,256]{2,1,0:T(8,128)}) custom-call(s32[8,48]{1,0:T(8,128)S(1)} %bitcast.7, f32[8,3,48,128]{3,2,1,0:T(8,128)} %all-to-all-done.2.moments_in, f32[32,16,256]{2,1,0:T(8,128)} %visc_in.1, f32[32,16,256]{2,1,0:T(8,128)} %dens_in.1), custom_call_target="tpu_custom_call" | custom-call | flops 8049999872 | tf_op jit(solution)/shard_map/settle/pallas_call | solution.py:428
  (5 shorter events, 0.0 us)
Async XLA Ops:
  0.6 13.9 %all-to-all-start = ((s32[8,1,48]{2,1,0:T(1,128)}), s32[8,1,48]{2,1,0:T(1,128)S(1)}, u32[]{:S(2)}, u32[]{:S(2)}) async-start(s32[8,1,48]{2,1,0:T(1,128)} %bitcast.8), calls=%async_computation | async-start | bytes 8192 | tf_op jit(solution)/shard_map/all_to_all | solution.py:875
  6.8 7.8 %copy-start = (f32[3,32,16,256]{3,2,1,0:T(8,128)S(1)}, f32[3,32,16,256]{3,2,1,0:T(8,128)}, u32[]{:S(2)}) copy-start(f32[3,32,16,256]{3,2,1,0:T(8,128)} %vel.5) | copy-start | bytes 4718596
  9.0 17.5 %collective-permute-start = (f32[6,4,16,256]{3,2,1,0:T(8,128)}, f32[6,4,16,256]{3,2,1,0:T(8,128)S(1)}, u32[]{:S(2)}, u32[]{:S(2)}) collective-permute-start(f32[6,4,16,256]{3,2,1,0:T(8,128)} %get-tuple-element.18), channel_id=1, source_target_pairs={{0,8},{8,16},{16,24},{1,9},{9,17},{17,25},{2,10},{10,18},{18,26},{... | collective-permute-start | bytes 1179656 | tf_op jit(solution)/shard_map/ppermute | solution.py:861
  10.9 15.6 %collective-permute-start.1 = (f32[6,4,16,256]{3,2,1,0:T(8,128)}, f32[6,4,16,256]{3,2,1,0:T(8,128)S(1)}, u32[]{:S(2)}, u32[]{:S(2)}) collective-permute-start(f32[6,4,16,256]{3,2,1,0:T(8,128)} %get-tuple-element.19), channel_id=1, source_target_pairs={{8,0},{16,8},{24,16},{9,1},{17,9},{25,17},{10,2},{18,10},{26,18},{... | collective-permute-start | bytes 1179656 | tf_op jit(solution)/shard_map/ppermute | solution.py:861
  20.5 19.5 %all-to-all-start.1 = ((f32[8,3,48,128]{3,2,1,0:T(8,128)}), f32[8,3,48,128]{3,2,1,0:T(8,128)}, u32[]{:S(2)}, u32[]{:S(2)}) async-start(f32[8,3,48,128]{3,2,1,0:T(8,128)} %pick_bricks.1), calls=%async_computation.1 | async-start | bytes 1179648 | tf_op jit(solution)/shard_map/all_to_all | solution.py:883
  26.5 13.5 %copy-start.1 = (s32[1,8]{1,0:T(1,128)S(1)}, s32[1,8]{1,0:T(1,128)}, u32[]{:S(2)}) copy-start(s32[1,8]{1,0:T(1,128)} %counts.1) | copy-start | bytes 100
  26.5 0.7 copy-start.2
  27.3 0.7 copy-start.3
  31.0 46.9 %collective-permute-start.2 = (f32[34,24,256]{2,1,0:T(8,128)S(1)}, f32[34,24,256]{2,1,0:T(8,128)S(1)}, u32[]{:S(2)}, u32[]{:S(2)}) collective-permute-start(f32[34,24,256]{2,1,0:T(8,128)S(1)} %get-tuple-element.20.refs_6_), channel_id=1, source_target_pairs={{0,1},{1,2},{2,3},{3,4},{4,5},{5,6},{6,7},{8,9},{9,10},{10,11},{11... | collective-permute-start | bytes 2506760 | tf_op jit(solution)/shard_map/ppermute | solution.py:861
  34.4 43.5 %collective-permute-start.3 = (f32[32,24,256]{2,1,0:T(8,128)S(1)}, f32[32,24,256]{2,1,0:T(8,128)S(1)}, u32[]{:S(2)}, u32[]{:S(2)}) collective-permute-start(f32[32,24,256]{2,1,0:T(8,128)S(1)} %get-tuple-element.25), channel_id=1, source_target_pairs={{1,0},{2,1},{3,2},{4,3},{5,4},{6,5},{7,6},{9,8},{10,9},{11,10},{12... | collective-permute-start | bytes 2359304 | tf_op jit(solution)/shard_map/ppermute | solution.py:861
  52.1 33.9 %all-to-all-start.2 = ((f32[8,3,48,128]{3,2,1,0:T(8,128)}), f32[8,3,48,128]{3,2,1,0:T(8,128)}, u32[]{:S(2)}, u32[]{:S(2)}) async-start(f32[8,3,48,128]{3,2,1,0:T(8,128)} %get-tuple-element.21._), calls=%async_computation.2 | async-start | bytes 1179648 | tf_op jit(solution)/shard_map/all_to_all | solution.py:887

commit v5 on v4

--- a/solution.py
+++ b/solution.py
@@ -359,8 +359,8 @@
     return visc.reshape(owners, slots, markers), moments
 
 
-def settle_body(asked, moments_in, visc_in, dens_in, visc_out, dens_out, *scratch):
-    moments, visc, dens, done, *tables = scratch
+def settle_body(asked, moments_in, visc_in, dens_in, visc_far, dens_far, *scratch):
+    moments, visc, dens, visc_out, dens_out, done, sent, *tables = scratch
     size_x, size_y, size_z = visc.shape
     copies = [
         pltpu.make_async_copy(there, here, done.at[n])
@@ -391,6 +391,13 @@
     lax.fori_loop(0, moments.shape[0] * groups, one_group, 0)
     copies[1].wait()
     copies[2].wait()
+
+    def sends(block_x):
+        planes = pl.ds(block_x * BX, BX)
+        return [
+            pltpu.make_async_copy(here.at[planes], there.at[planes], sent.at[n, block_x])
+            for n, (here, there) in enumerate(((visc_out, visc_far), (dens_out, dens_far)))
+        ]
 
     def finish(block_x, carry):
         for block_y in range(0, bricks_y, 2):
@@ -415,27 +422,37 @@
                     scale = 1.0 / (sums[0] + 1.0)
                     visc_out[here] = jnp.exp((sums[1] + jnp.log(visc[here])) * scale)
                     dens_out[here] = (sums[2] + dens[here]) * scale
+        for send in sends(block_x):
+            send.start()
         return carry
 
+    def drain(block_x, carry):
+        for send in sends(block_x):
+            send.wait()
+        return carry
+
     lax.fori_loop(0, size_x // BX, finish, 0)
+    lax.fori_loop(0, size_x // BX, drain, 0)
 
 
 def settle(asked, moments, cell_visc, cell_dens):
     size_x, size_y, size_z = cell_visc.shape
     places = (size_x // BX) * (size_y // BY) * (size_z // LANES)
-    whole = pl.BlockSpec(memory_space=pltpu.VMEM)
     shape = jax.ShapeDtypeStruct(cell_visc.shape, f32)
     return pl.pallas_call(
         settle_body,
         out_shape=(shape, shape),
         in_specs=[pl.BlockSpec(memory_space=pltpu.SMEM)]
         + [pl.BlockSpec(memory_space=pl.ANY)] * 3,
-        out_specs=(whole, whole),
+        out_specs=(pl.BlockSpec(memory_space=pl.ANY),) * 2,
         scratch_shapes=[
             pltpu.VMEM(moments.shape, f32),
             pltpu.VMEM(cell_visc.shape, f32),
             pltpu.VMEM(cell_visc.shape, f32),
+            pltpu.VMEM(cell_visc.shape, f32),
+            pltpu.VMEM(cell_visc.shape, f32),
             pltpu.SemaphoreType.DMA((3,)),
+            pltpu.SemaphoreType.DMA((2, size_x // BX)),
         ]
         + [pltpu.VMEM((places, ROWS, LANES), f32)],
         compiler_params=vmem_limit(24),
@@ -669,37 +686,43 @@
 
 
 def inner_body(vel, pres, visc, dens, low_x, high_x, _, even_out, odd_out, cells_out, *work):
-    blocks, sides_x, even, odd, cells, coefs, relax, forcing, rate, done = work
+    blocks, sides_x, even, odd, cells, coefs, relax, forcing, rate, done, more = work
     size_x, size_y, size_z = blocks.shape[1:]
     width = SWEEPS
     inputs = (
-        (visc, blocks.at[4], (4,)),
-        (vel, blocks.at[0:3], (0, 1, 2)),
-        (pres, blocks.at[3], (3,)),
-        (dens, blocks.at[5], (5,)),
-        (low_x, sides_x.at[0], ()),
-        (high_x, sides_x.at[1], ()),
+        (visc, blocks.at[4]),
+        (dens, blocks.at[5]),
+        (low_x, sides_x.at[0]),
+        (high_x, sides_x.at[1]),
+        (vel, blocks.at[0:3]),
+        (pres, blocks.at[3]),
     )
     copies = [
-        pltpu.make_async_copy(there, here, done.at[n]) for n, (there, here, _) in enumerate(inputs)
+        pltpu.make_async_copy(there, here, done.at[n]) for n, (there, here) in enumerate(inputs)
     ]
     for copy in copies:
         copy.start()
     targets = [even.at[n] for n in range(4)] + [cells.at[n] for n in range(2)]
-    for copy, (_, _, held) in zip(copies, inputs):
-        copy.wait()
-        for f in held:
-            for i in range(size_x):
-                for y in range(0, size_y, SUBLANES):
-                    value = blocks[f, i, y : y + SUBLANES, :]
-                    put(targets[f], i + width, y + width, SUBLANES, value)
-    for side, begin in enumerate((0, width + size_x)):
-        for f in range(6):
+
+    def lay_out(f):
+        for i in range(size_x):
+            for y in range(0, size_y, SUBLANES):
+                value = blocks[f, i, y : y + SUBLANES, :]
+                put(targets[f], i + width, y + width, SUBLANES, value)
+        for side, begin in enumerate((0, width + size_x)):
             for i in range(width):
                 for y in range(0, size_y, SUBLANES):
                     value = sides_x[side, f, i, y : y + SUBLANES, :]
                     put(targets[f], begin + i, y + width, SUBLANES, value)
 
+    for copy in copies[:4]:
+        copy.wait()
+    lay_out(4)
+    lay_out(5)
+    sends = kept_copies(((even, even_out), (odd, odd_out), (cells, cells_out)), size_y, more)
+    for send in sends[3:]:
+        send.start()
+
     prepare, sweep = row_work(cells, coefs, relax, forcing, rate)
 
     def prepare_row(y, carry):
@@ -708,16 +731,23 @@
 
     first, last = width + 1, width + size_y - 1
     lax.fori_loop(first, last, prepare_row, 0, unroll=2)
+    for copy in copies[4:]:
+        copy.wait()
+    for f in range(4):
+        lay_out(f)
+    early, late = (sends[1:3], sends[:1]) if SWEEPS % 2 == 0 else (sends[:1], sends[1:3])
     for step in range(SWEEPS):
         old, new = (odd, even) if step % 2 else (even, odd)
+        if step == SWEEPS - 1:
+            for send in early:
+                send.start()
 
         def sweep_row(y, carry, old=old, new=new):
             sweep(y, old, new)
             return carry
 
         lax.fori_loop(first + step, last - step, sweep_row, 0, unroll=2)
-    sends = kept_copies(((even, even_out), (odd, odd_out), (cells, cells_out)), size_y, done)
-    for send in sends:
+    for send in late:
         send.start()
     for send in sends:
         send.wait()
@@ -746,6 +776,7 @@
             pltpu.VMEM(block, f32),
             pltpu.VMEM(block, f32),
             pltpu.SemaphoreType.DMA((6,)),
+            pltpu.SemaphoreType.DMA((5,)),
         ],
         compiler_params=vmem_limit(40),
         cost_estimate=cost(25),
@@ -766,24 +797,27 @@
     for copy in (*halos, *kept[3:], *kept[:3]):
         copy.start()
     targets = [even.at[n] for n in range(4)] + [cells.at[n] for n in range(2)]
-    for target in targets:
-        for x in (*range(width), *range(width + size_x, size_x + 2 * width)):
-            for y in (0, width + size_y):
-                put(target, x, y, width, jnp.zeros((width, size_z), f32))
-    for up, halo, copy, begin in (
-        (True, from_low, halos[0], 0),
-        (False, from_high, halos[1], width + size_y),
-    ):
+
+    def lay_out(chosen):
+        for f in chosen:
+            for x in (*range(width), *range(width + size_x, size_x + 2 * width)):
+                for y in (0, width + size_y):
+                    put(targets[f], x, y, width, jnp.zeros((width, size_z), f32))
+            rows = slice(f * width, (f + 1) * width)
+            for halo, begin in ((from_low, 0), (from_high, width + size_y)):
+                for i in range(size_x):
+                    put(targets[f], i + width, begin, width, halo[i, rows, :])
+        for up, halo in ((True, from_low), (False, from_high)):
+            for f, side, far_x, far_y, plane, row in corner_rows(up, size_x)[0]:
+                if f in chosen:
+                    x = width + size_x - 1 + far_x if side else width - far_x
+                    y = width - far_y if up else width + size_y - 1 + far_y
+                    put(targets[f], x, y, 1, halo[plane, row : row + 1, :])
+
+    for copy in halos:
         copy.wait()
-        for f, target in enumerate(targets):
-            rows = slice(f * width, (f + 1) * width)
-            for i in range(size_x):
-                put(target, i + width, begin, width, halo[i, rows, :])
-        for f, side, far_x, far_y, plane, row in corner_rows(up, size_x)[0]:
-            x = width + size_x - 1 + far_x if side else width - far_x
-            y = width - far_y if up else width + size_y - 1 + far_y
-            put(targets[f], x, y, 1, halo[plane, row : row + 1, :])
-    for copy in kept:
+    lay_out((4, 5))
+    for copy in kept[3:]:
         copy.wait()
 
     prepare, sweep = row_work(cells, coefs, relax, forcing, rate)
@@ -794,6 +828,9 @@
         return carry
 
     lax.fori_loop(0, 2 * width - 1, prepare_rows, 0)
+    lay_out((0, 1, 2, 3))
+    for copy in kept[:3]:
+        copy.wait()
     for step in range(SWEEPS):
         old, new = (odd, even) if step % 2 else (even, odd)
 

time: 94.3 us -> 93.6 us (level)
  starting transfers between devices: 39.3 us -> 37.1 us
  waiting for transfers between devices: 2.96 us -> 5.14 us
    all_to_all x1, starting transfers between devices: 14.8 us -> 12.6 us  [per_device(): gathered = lax.all_to_all(moments, 'mark', 0, 0, tiled=True)]
    ppermute x4, waiting for transfers between devices: 0.77 us -> 2.95 us  [shift(): return lax.ppermute(value, axis, pairs)]
where the time goes in v5:
time: 93.6 us; the launch traced here: 93.1 us
  Pallas kernels  48.7 us (52%)
  starting transfers between devices  37.1 us (40%)
  waiting for transfers between devices  5.14 us (5%)
  local copies, waits for them, and re-layouts  1.48 us (2%)
    all_to_all x1, starting transfers between devices, per_device(): gathered = lax.all_to_all(moments, 'mark', 0, 0, tiled=True)  12.6 us
    ppermute x4, starting transfers between devices, shift(): return lax.ppermute(value, axis, pairs)  12.3 us
    pallas_call x1, Pallas kernels, marker_work(): pl.pallas_call(marker_body, out_shape=(jax.ShapeDtypeStruct((owners, part...  12.1 us
    pallas_call x1, Pallas kernels, inner_sweeps(): pl.pallas_call(inner_body, out_shape=tuple((jax.ShapeDtypeStruct(shape, f...  10.3 us
    pallas_call x1, Pallas kernels, edge_sweeps(): pl.pallas_call(edge_body, out_shape=(jax.ShapeDtypeStruct((3, size_x, siz...  8.06 us
    pallas_call x1, Pallas kernels, settle(): pl.pallas_call(settle_body, out_shape=(shape, shape), in_specs=[pl.BlockS...  7.08 us
    all_to_all x1, starting transfers between devices, per_device(): asked = lax.all_to_all(block_brick, 'mark', 0, 0, tiled=True)  6.18 us
    all_to_all x1, starting transfers between devices, per_device(): bricks = lax.all_to_all(picked, 'mark', 0, 0, tiled=True)  6 us
  transfers between devices with their start and end apart: 7, of which 2 were waited for; matrix products, arithmetic and copies ran while one was open for 0% of the time, Pallas kernels for 45%

profile of v5, /device:TPU:18, one launch (start us, length us, event | category | flops | bytes accessed | tf_op | source)
XLA Modules:
  0.0 93.1 jit_solution(11958214396092081399)
XLA Ops:
  0.6 6.2 %all-to-all-start = ((s32[8,1,48]{2,1,0:T(1,128)}), s32[8,1,48]{2,1,0:T(1,128)S(1)}, u32[]{:S(2)}, u32[]{:S(2)}) async-start(s32[8,1,48]{2,1,0:T(1,128)} %bitcast.8), calls=%async_computation | async-start | bytes 8192 | tf_op jit(solution)/shard_map/all_to_all | solution.py:912
  6.8 2.2 %pack_x.1 = (f32[6,4,16,256]{3,2,1,0:T(8,128)}, f32[6,4,16,256]{3,2,1,0:T(8,128)}) custom-call(f32[3,32,16,256]{3,2,1,0:T(8,128)} %vel.5, f32[3,32,16,256]{3,2,1,0:T(8,128)} %vel.5, f32[32,16,256]{2,1,0:T(8,128)} %pres.3, f32[32,16,256]{2,1,0:T(8,128)} %pres.3, f32[32,16,256]{2,1,0:T(8,128)} %visc_in.1, f32[32,16,256]{2,1,0:T(8,128)} %visc_in.1, ...), custom_call_target="tpu_custom_call" | custom-call | flops 2300000000 | tf_op jit(solution)/shard_map/pack_x/pallas_call | solution.py:485
  9.0 1.9 %collective-permute-start = (f32[6,4,16,256]{3,2,1,0:T(8,128)}, f32[6,4,16,256]{3,2,1,0:T(8,128)S(1)}, u32[]{:S(2)}, u32[]{:S(2)}) collective-permute-start(f32[6,4,16,256]{3,2,1,0:T(8,128)} %get-tuple-element.18), channel_id=1, source_target_pairs={{0,8},{8,16},{16,24},{1,9},{9,17},{17,25},{2,10},{10,18},{18,26},{... | collective-permute-start | bytes 1179656 | tf_op jit(solution)/shard_map/ppermute | solution.py:898
  10.9 3.6 %collective-permute-start.1 = (f32[6,4,16,256]{3,2,1,0:T(8,128)}, f32[6,4,16,256]{3,2,1,0:T(8,128)S(1)}, u32[]{:S(2)}, u32[]{:S(2)}) collective-permute-start(f32[6,4,16,256]{3,2,1,0:T(8,128)} %get-tuple-element.19), channel_id=1, source_target_pairs={{8,0},{16,8},{24,16},{9,1},{17,9},{25,17},{10,2},{18,10},{26,18},{... | collective-permute-start | bytes 1179656 | tf_op jit(solution)/shard_map/ppermute | solution.py:898
  14.5 0.0 all-to-all-done
  14.6 5.9 %pick_bricks.1 = f32[8,3,48,128]{3,2,1,0:T(8,128)} custom-call(s32[8,48]{1,0:T(8,128)S(1)} %bitcast.6, f32[3,32,16,256]{3,2,1,0:T(8,128)S(1)} %copy-done), custom_call_target="tpu_custom_call" | custom-call | flops 28750000128 | tf_op jit(solution)/shard_map/pick_bricks/pallas_call | solution.py:86
  20.5 6.0 %all-to-all-start.1 = ((f32[8,3,48,128]{3,2,1,0:T(8,128)}), f32[8,3,48,128]{3,2,1,0:T(8,128)}, u32[]{:S(2)}, u32[]{:S(2)}) async-start(f32[8,3,48,128]{3,2,1,0:T(8,128)} %pick_bricks.1), calls=%async_computation.1 | async-start | bytes 1179648 | tf_op jit(solution)/shard_map/all_to_all | solution.py:920
  26.5 0.0 collective-permute-done.low_x
  26.5 0.0 copy-start.2
  26.5 0.0 collective-permute-done.1.high_x
  26.5 0.7 copy-done.2
  27.3 0.7 copy-done.3
  28.0 3.0 %pack_y.1 = (f32[34,24,256]{2,1,0:T(8,128)S(1)}, f32[32,24,256]{2,1,0:T(8,128)S(1)}) custom-call(f32[3,32,16,256]{3,2,1,0:T(8,128)} %vel.5, f32[32,16,256]{2,1,0:T(8,128)} %pres.3, f32[32,16,256]{2,1,0:T(8,128)} %visc_in.1, f32[32,16,256]{2,1,0:T(8,128)} %dens_in.1, f32[6,4,16,256]{3,2,1,0:T(8,128)} %copy-done.2, f32[6,4,16,256]{3,2,1,0:T(8,128)} %copy-done.3), custom_call_target="tpu_custom_call" | custom-call | flops 17250000896 | tf_op jit(solution)/shard_map/pack_y/pallas_call | solution.py:539
  31.0 3.4 %collective-permute-start.2 = (f32[34,24,256]{2,1,0:T(8,128)S(1)}, f32[34,24,256]{2,1,0:T(8,128)S(1)}, u32[]{:S(2)}, u32[]{:S(2)}) collective-permute-start(f32[34,24,256]{2,1,0:T(8,128)S(1)} %get-tuple-element.20.refs_6_), channel_id=1, source_target_pairs={{0,1},{1,2},{2,3},{3,4},{4,5},{5,6},{6,7},{8,9},{9,10},{10,11},{11... | collective-permute-start | bytes 2506760 | tf_op jit(solution)/shard_map/ppermute | solution.py:898
  34.4 3.4 %collective-permute-start.3 = (f32[32,24,256]{2,1,0:T(8,128)S(1)}, f32[32,24,256]{2,1,0:T(8,128)S(1)}, u32[]{:S(2)}, u32[]{:S(2)}) collective-permute-start(f32[32,24,256]{2,1,0:T(8,128)S(1)} %get-tuple-element.25), channel_id=1, source_target_pairs={{1,0},{2,1},{3,2},{4,3},{5,4},{6,5},{7,6},{9,8},{10,9},{11,10},{12... | collective-permute-start | bytes 2359304 | tf_op jit(solution)/shard_map/ppermute | solution.py:898
  37.8 2.2 %all-to-all-done.1.refs_5_ = f32[8,3,48,128]{3,2,1,0:T(8,128)} async-done(((f32[8,3,48,128]{3,2,1,0:T(8,128)}), f32[8,3,48,128]{3,2,1,0:T(8,128)}, u32[]{:S(2)}, u32[]{:S(2)}) %all-to-all-start.1) | async-done | bytes 589856 | tf_op jit(solution)/shard_map/all_to_all | solution.py:920
  40.0 12.1 %marker_work.1 = (f32[8,6,8,256]{3,2,1,0:T(8,128)}, f32[8,3,48,128]{3,2,1,0:T(8,128)}) custom-call(s32[1,8]{1,0:T(1,128)S(1)} %copy-done.1, bf16[2,2,128,256]{3,2,1,0:T(8,128)(2,1)} %constant.4.clone.refs_0_, bf16[512,512]{1,0:T(8,128)(2,1)} %constant.5.clone.refs_1_, f32[8,3,6,8,256]{4,3,2,1,0:T(8,128)} %bitcast.9, f32[8,6,8,256]{3,2,1,0:T(8,128)} %bitcast.10, ...), custom_call_target="tpu_custom_call" | custom-call | flops 28750000128 | tf_op jit(solution)/shard_map/marker_work/pallas_call | solution.py:329
  52.1 12.6 %all-to-all-start.2 = ((f32[8,3,48,128]{3,2,1,0:T(8,128)}), f32[8,3,48,128]{3,2,1,0:T(8,128)}, u32[]{:S(2)}, u32[]{:S(2)}) async-start(f32[8,3,48,128]{3,2,1,0:T(8,128)} %get-tuple-element.21._), calls=%async_computation.2 | async-start | bytes 1179648 | tf_op jit(solution)/shard_map/all_to_all | solution.py:924
  64.7 10.3 %inner_sweeps.1 = (f32[4,5,2,192,128]{4,3,2,1,0:T(8,128)S(1)}, f32[4,5,2,192,128]{4,3,2,1,0:T(8,128)S(1)}, f32[2,5,2,192,128]{4,3,2,1,0:T(8,128)S(1)}) custom-call(f32[3,32,16,256]{3,2,1,0:T(8,128)} %vel.5, f32[32,16,256]{2,1,0:T(8,128)} %pres.3, f32[32,16,256]{2,1,0:T(8,128)} %visc_in.1, f32[32,16,256]{2,1,0:T(8,128)} %dens_in.1, ...), custom_call_target="tpu_custom_call" | custom-call | flops 28750000128 | tf_op jit(solution)/shard_map/inner_sweeps/pallas_call | solution.py:763
  75.0 2.9 %collective-permute-done.3.high_y = f32[32,24,256]{2,1,0:T(8,128)S(1)} collective-permute-done((f32[32,24,256]{2,1,0:T(8,128)S(1)}, f32[32,24,256]{2,1,0:T(8,128)S(1)}, u32[]{:S(2)}, u32[]{:S(2)}) %collective-permute-start.3) | collective-permute-done | bytes 786464 | tf_op jit(solution)/shard_map/ppermute | solution.py:898
  77.9 0.0 collective-permute-done.2.low_y
  77.9 8.1 %edge_sweeps.1 = (f32[3,32,16,256]{3,2,1,0:T(8,128)}, f32[32,16,256]{2,1,0:T(8,128)}) custom-call(f32[4,5,2,192,128]{4,3,2,1,0:T(8,128)S(1)} %get-tuple-element.22.even_in, f32[4,5,2,192,128]{4,3,2,1,0:T(8,128)S(1)} %get-tuple-element.23.odd_in, f32[2,5,2,192,128]{4,3,2,1,0:T(8,128)S(1)} %get-tuple-element.24.cells_in, ...), custom_call_target="tpu_custom_call" | custom-call | flops 1150000000 | tf_op jit(solution)/shard_map/edge_sweeps/pallas_call | solution.py:867
  86.0 0.0 all-to-all-done.2.moments_in
  86.0 7.1 %settle.1 = (f32[32,16,256]{2,1,0:T(8,128)}, f32[32,16,256]{2,1,0:T(8,128)}) custom-call(s32[8,48]{1,0:T(8,128)S(1)} %bitcast.7, f32[8,3,48,128]{3,2,1,0:T(8,128)} %all-to-all-done.2.moments_in, f32[32,16,256]{2,1,0:T(8,128)} %visc_in.1, f32[32,16,256]{2,1,0:T(8,128)} %dens_in.1), custom_call_target="tpu_custom_call" | custom-call | flops 8049999872 | tf_op jit(solution)/shard_map/settle/pallas_call | solution.py:442
  (5 shorter events, 0.0 us)
Async XLA Ops:
  0.6 13.9 %all-to-all-start = ((s32[8,1,48]{2,1,0:T(1,128)}), s32[8,1,48]{2,1,0:T(1,128)S(1)}, u32[]{:S(2)}, u32[]{:S(2)}) async-start(s32[8,1,48]{2,1,0:T(1,128)} %bitcast.8), calls=%async_computation | async-start | bytes 8192 | tf_op jit(solution)/shard_map/all_to_all | solution.py:912
  6.8 7.8 %copy-start = (f32[3,32,16,256]{3,2,1,0:T(8,128)S(1)}, f32[3,32,16,256]{3,2,1,0:T(8,128)}, u32[]{:S(2)}) copy-start(f32[3,32,16,256]{3,2,1,0:T(8,128)} %vel.5) | copy-start | bytes 4718596
  9.0 17.5 %collective-permute-start = (f32[6,4,16,256]{3,2,1,0:T(8,128)}, f32[6,4,16,256]{3,2,1,0:T(8,128)S(1)}, u32[]{:S(2)}, u32[]{:S(2)}) collective-permute-start(f32[6,4,16,256]{3,2,1,0:T(8,128)} %get-tuple-element.18), channel_id=1, source_target_pairs={{0,8},{8,16},{16,24},{1,9},{9,17},{17,25},{2,10},{10,18},{18,26},{... | collective-permute-start | bytes 1179656 | tf_op jit(solution)/shard_map/ppermute | solution.py:898
  10.9 15.6 %collective-permute-start.1 = (f32[6,4,16,256]{3,2,1,0:T(8,128)}, f32[6,4,16,256]{3,2,1,0:T(8,128)S(1)}, u32[]{:S(2)}, u32[]{:S(2)}) collective-permute-start(f32[6,4,16,256]{3,2,1,0:T(8,128)} %get-tuple-element.19), channel_id=1, source_target_pairs={{8,0},{16,8},{24,16},{9,1},{17,9},{25,17},{10,2},{18,10},{26,18},{... | collective-permute-start | bytes 1179656 | tf_op jit(solution)/shard_map/ppermute | solution.py:898
  20.5 19.5 %all-to-all-start.1 = ((f32[8,3,48,128]{3,2,1,0:T(8,128)}), f32[8,3,48,128]{3,2,1,0:T(8,128)}, u32[]{:S(2)}, u32[]{:S(2)}) async-start(f32[8,3,48,128]{3,2,1,0:T(8,128)} %pick_bricks.1), calls=%async_computation.1 | async-start | bytes 1179648 | tf_op jit(solution)/shard_map/all_to_all | solution.py:920
  26.5 13.5 %copy-start.1 = (s32[1,8]{1,0:T(1,128)S(1)}, s32[1,8]{1,0:T(1,128)}, u32[]{:S(2)}) copy-start(s32[1,8]{1,0:T(1,128)} %counts.1) | copy-start | bytes 100
  26.5 0.7 copy-start.2
  27.3 0.7 copy-start.3
  31.0 46.9 %collective-permute-start.2 = (f32[34,24,256]{2,1,0:T(8,128)S(1)}, f32[34,24,256]{2,1,0:T(8,128)S(1)}, u32[]{:S(2)}, u32[]{:S(2)}) collective-permute-start(f32[34,24,256]{2,1,0:T(8,128)S(1)} %get-tuple-element.20.refs_6_), channel_id=1, source_target_pairs={{0,1},{1,2},{2,3},{3,4},{4,5},{5,6},{6,7},{8,9},{9,10},{10,11},{11... | collective-permute-start | bytes 2506760 | tf_op jit(solution)/shard_map/ppermute | solution.py:898
  34.4 43.5 %collective-permute-start.3 = (f32[32,24,256]{2,1,0:T(8,128)S(1)}, f32[32,24,256]{2,1,0:T(8,128)S(1)}, u32[]{:S(2)}, u32[]{:S(2)}) collective-permute-start(f32[32,24,256]{2,1,0:T(8,128)S(1)} %get-tuple-element.25), channel_id=1, source_target_pairs={{1,0},{2,1},{3,2},{4,3},{5,4},{6,5},{7,6},{9,8},{10,9},{11,10},{12... | collective-permute-start | bytes 2359304 | tf_op jit(solution)/shard_map/ppermute | solution.py:898
  52.1 33.9 %all-to-all-start.2 = ((f32[8,3,48,128]{3,2,1,0:T(8,128)}), f32[8,3,48,128]{3,2,1,0:T(8,128)}, u32[]{:S(2)}, u32[]{:S(2)}) async-start(f32[8,3,48,128]{3,2,1,0:T(8,128)} %get-tuple-element.21._), calls=%async_computation.2 | async-start | bytes 1179648 | tf_op jit(solution)/shard_map/all_to_all | solution.py:924

commit v6 on v5

--- a/solution.py
+++ b/solution.py
@@ -275,8 +275,14 @@
 
 
 def marker_body(counts, *refs):
-    ins, outs, scratch = refs[:6], refs[7:9], refs[9:]
-    listed, sums, *flat = scratch
+    sources, targets, scratch = refs[:6], refs[7:9], refs[9:]
+    ins, outs, (got, sent, listed, sums, *flat) = scratch[:6], scratch[6:8], scratch[8:]
+    fetches = [
+        pltpu.make_async_copy(there, here, got.at[n])
+        for n, (there, here) in enumerate(zip(sources, ins))
+    ]
+    for fetch in fetches:
+        fetch.start()
     held = 2 * TOGETHER
     buffers = [flat[n * held : (n + 1) * held] for n in range(len(flat) // held)]
     visc_out, moments_out = outs
@@ -307,7 +313,17 @@
         marker_groups(taken, counts, ins, outs, buffers, sums)
         return carry
 
+    for fetch in fetches:
+        fetch.wait()
     lax.fori_loop(0, (number + TOGETHER - 1) // TOGETHER, step, 0)
+    sends = [
+        pltpu.make_async_copy(here, there, sent.at[n])
+        for n, (here, there) in enumerate(zip(outs, targets))
+    ]
+    for send in sends:
+        send.start()
+    for send in sends:
+        send.wait()
 
 
 def marker_work(counts, positions, start_visc, marker_dens, bricks, after):
@@ -315,7 +331,16 @@
     groups, parts = slots // GROUP, slots // HALF
     spread, gather = permutations()
     width = 4 * BZ * HALF
-    whole = pl.BlockSpec(memory_space=pltpu.VMEM)
+    anywhere = pl.BlockSpec(memory_space=pl.ANY)
+    fetched = (
+        spread,
+        gather,
+        positions.reshape(owners, 3, parts, HALF, markers),
+        start_visc.reshape(owners, parts, HALF, markers),
+        marker_dens.reshape(owners, parts, HALF, markers),
+        bricks,
+    )
+    shapes = ((owners, parts, HALF, markers), (owners, groups, ROWS, LANES))
     buffers = (
         pltpu.VMEM((ROWS, width), f32),
         pltpu.VMEM((ROWS * HALF, width), bf16),
@@ -328,15 +353,14 @@
     )
     visc, moments = pl.pallas_call(
         marker_body,
-        out_shape=(
-            jax.ShapeDtypeStruct((owners, parts, HALF, markers), f32),
-            jax.ShapeDtypeStruct((owners, groups, ROWS, LANES), f32),
-        ),
-        in_specs=[pl.BlockSpec(memory_space=pltpu.SMEM)]
-        + [whole] * 6
-        + [pl.BlockSpec(memory_space=pl.ANY)],
-        out_specs=(whole, whole),
-        scratch_shapes=[
+        out_shape=tuple(jax.ShapeDtypeStruct(shape, f32) for shape in shapes),
+        in_specs=[pl.BlockSpec(memory_space=pltpu.SMEM)] + [anywhere] * 7,
+        out_specs=(anywhere, anywhere),
+        scratch_shapes=[pltpu.VMEM(array.shape, array.dtype) for array in fetched]
+        + [pltpu.VMEM(shape, f32) for shape in shapes]
+        + [
+            pltpu.SemaphoreType.DMA((len(fetched),)),
+            pltpu.SemaphoreType.DMA((len(shapes),)),
             pltpu.SMEM((2 * (owners * groups + TOGETHER),), jnp.int32),
             pltpu.VMEM((32 * TOGETHER, 2 * BY * BZ * HALF), f32),
         ]
@@ -344,18 +368,7 @@
         compiler_params=vmem_limit(40),
         cost_estimate=cost(25),
         name="marker_work",
-    )(
-        counts,
-        *in_hbm(
-            spread,
-            gather,
-            positions.reshape(owners, 3, parts, HALF, markers),
-            start_visc.reshape(owners, parts, HALF, markers),
-            marker_dens.reshape(owners, parts, HALF, markers),
-            bricks,
-        ),
-        after,
-    )
+    )(counts, *in_hbm(*fetched), after)
     return visc.reshape(owners, slots, markers), moments
 
 
@@ -552,7 +565,7 @@
         compiler_params=vmem_limit(24),
         cost_estimate=cost(15),
         name="pack_y",
-    )(*in_hbm(velocity, pressure, cell_visc, cell_dens, low_x, high_x))
+    )(*in_hbm(velocity, pressure, cell_visc, cell_dens), low_x, high_x)
 
 
 def place(per, x, y, rows):

time: 93.6 us -> 93.3 us (level)
  waiting for transfers between devices: 5.14 us -> 8.28 us
  starting transfers between devices: 37.1 us -> 35 us
  local copies, waits for them, and re-layouts: 1.48 us -> 0.02 us
    all_to_all x1, starting transfers between devices: 12.6 us -> 10.5 us  [per_device(): gathered = lax.all_to_all(moments, 'mark', 0, 0, tiled=True)]
    ppermute x4, waiting for transfers between devices: 2.95 us -> 4.66 us  [shift(): return lax.ppermute(value, axis, pairs)]
    unnamed x8, local copies, waits for them, and re-layouts: 1.48 us -> 0.02 us
    all_to_all x1, waiting for transfers between devices: 2.19 us -> 3.61 us  [per_device(): bricks = lax.all_to_all(picked, 'mark', 0, 0, tiled=True)]
where the time goes in v6:
time: 93.3 us; the launch traced here: 92.8 us
  Pallas kernels  48.8 us (52%)
  starting transfers between devices  35 us (38%)
  waiting for transfers between devices  8.28 us (9%)
    ppermute x4, starting transfers between devices, shift(): return lax.ppermute(value, axis, pairs)  12.3 us
    pallas_call x1, Pallas kernels, marker_work(): pl.pallas_call(marker_body, out_shape=tuple((jax.ShapeDtypeStruct(shape,...  12.2 us
    all_to_all x1, starting transfers between devices, per_device(): gathered = lax.all_to_all(moments, 'mark', 0, 0, tiled=True)  10.5 us
    pallas_call x1, Pallas kernels, inner_sweeps(): pl.pallas_call(inner_body, out_shape=tuple((jax.ShapeDtypeStruct(shape, f...  10.3 us
    pallas_call x1, Pallas kernels, edge_sweeps(): pl.pallas_call(edge_body, out_shape=(jax.ShapeDtypeStruct((3, size_x, siz...  8.06 us
    pallas_call x1, Pallas kernels, settle(): pl.pallas_call(settle_body, out_shape=(shape, shape), in_specs=[pl.BlockS...  7.08 us
    all_to_all x1, starting transfers between devices, per_device(): asked = lax.all_to_all(block_brick, 'mark', 0, 0, tiled=True)  6.18 us
    all_to_all x1, starting transfers between devices, per_device(): bricks = lax.all_to_all(picked, 'mark', 0, 0, tiled=True)  6 us
  transfers between devices with their start and end apart: 7, of which 2 were waited for; matrix products, arithmetic and copies ran while one was open for 0% of the time, Pallas kernels for 45%

profile of v6, /device:TPU:18, one launch (start us, length us, event | category | flops | bytes accessed | tf_op | source)
XLA Modules:
  0.0 92.8 jit_solution(8628239408708431427)
XLA Ops:
  0.6 6.2 %all-to-all-start = ((s32[8,1,48]{2,1,0:T(1,128)}), s32[8,1,48]{2,1,0:T(1,128)S(1)}, u32[]{:S(2)}, u32[]{:S(2)}) async-start(s32[8,1,48]{2,1,0:T(1,128)} %bitcast.8), calls=%async_computation | async-start | bytes 8192 | tf_op jit(solution)/shard_map/all_to_all | solution.py:925
  6.8 2.2 %pack_x.1 = (f32[6,4,16,256]{3,2,1,0:T(8,128)}, f32[6,4,16,256]{3,2,1,0:T(8,128)}) custom-call(f32[3,32,16,256]{3,2,1,0:T(8,128)} %vel.5, f32[3,32,16,256]{3,2,1,0:T(8,128)} %vel.5, f32[32,16,256]{2,1,0:T(8,128)} %pres.3, f32[32,16,256]{2,1,0:T(8,128)} %pres.3, f32[32,16,256]{2,1,0:T(8,128)} %visc_in.1, f32[32,16,256]{2,1,0:T(8,128)} %visc_in.1, ...), custom_call_target="tpu_custom_call" | custom-call | flops 2300000000 | tf_op jit(solution)/shard_map/pack_x/pallas_call | solution.py:498
  9.0 1.9 %collective-permute-start = (f32[6,4,16,256]{3,2,1,0:T(8,128)}, f32[6,4,16,256]{3,2,1,0:T(8,128)S(1)}, u32[]{:S(2)}, u32[]{:S(2)}) collective-permute-start(f32[6,4,16,256]{3,2,1,0:T(8,128)} %get-tuple-element.18), channel_id=1, source_target_pairs={{0,8},{8,16},{16,24},{1,9},{9,17},{17,25},{2,10},{10,18},{18,26},{... | collective-permute-start | bytes 1179656 | tf_op jit(solution)/shard_map/ppermute | solution.py:911
  10.9 3.6 %collective-permute-start.1 = (f32[6,4,16,256]{3,2,1,0:T(8,128)}, f32[6,4,16,256]{3,2,1,0:T(8,128)S(1)}, u32[]{:S(2)}, u32[]{:S(2)}) collective-permute-start(f32[6,4,16,256]{3,2,1,0:T(8,128)} %get-tuple-element.19), channel_id=1, source_target_pairs={{8,0},{16,8},{24,16},{9,1},{17,9},{25,17},{10,2},{18,10},{26,18},{... | collective-permute-start | bytes 1179656 | tf_op jit(solution)/shard_map/ppermute | solution.py:911
  14.5 0.0 all-to-all-done
  14.6 0.0 copy-done
  14.6 5.9 %pick_bricks.1 = f32[8,3,48,128]{3,2,1,0:T(8,128)} custom-call(s32[8,48]{1,0:T(8,128)S(1)} %bitcast.6, f32[3,32,16,256]{3,2,1,0:T(8,128)S(1)} %copy-done), custom_call_target="tpu_custom_call" | custom-call | flops 28750000128 | tf_op jit(solution)/shard_map/pick_bricks/pallas_call | solution.py:86
  20.5 6.0 %all-to-all-start.1 = ((f32[8,3,48,128]{3,2,1,0:T(8,128)}), f32[8,3,48,128]{3,2,1,0:T(8,128)}, u32[]{:S(2)}, u32[]{:S(2)}) async-start(f32[8,3,48,128]{3,2,1,0:T(8,128)} %pick_bricks.1), calls=%async_computation.1 | async-start | bytes 1179648 | tf_op jit(solution)/shard_map/all_to_all | solution.py:933
  26.5 0.0 collective-permute-done.low_x
  26.5 0.0 copy-start.1
  26.5 0.0 collective-permute-done.1.high_x
  26.5 0.0 copy-start.2
  26.5 3.0 %pack_y.1 = (f32[34,24,256]{2,1,0:T(8,128)S(1)}, f32[32,24,256]{2,1,0:T(8,128)S(1)}) custom-call(f32[3,32,16,256]{3,2,1,0:T(8,128)} %vel.5, f32[32,16,256]{2,1,0:T(8,128)} %pres.3, f32[32,16,256]{2,1,0:T(8,128)} %visc_in.1, f32[32,16,256]{2,1,0:T(8,128)} %dens_in.1, f32[6,4,16,256]{3,2,1,0:T(8,128)S(1)} %collective-permute-done.low_x, ...), custom_call_target="tpu_custom_call" | custom-call | flops 17250000896 | tf_op jit(solution)/shard_map/pack_y/pallas_call | solution.py:552
  29.6 3.4 %collective-permute-start.2 = (f32[34,24,256]{2,1,0:T(8,128)S(1)}, f32[34,24,256]{2,1,0:T(8,128)S(1)}, u32[]{:S(2)}, u32[]{:S(2)}) collective-permute-start(f32[34,24,256]{2,1,0:T(8,128)S(1)} %get-tuple-element.20.refs_6_), channel_id=1, source_target_pairs={{0,1},{1,2},{2,3},{3,4},{4,5},{5,6},{6,7},{8,9},{9,10},{10,11},{11... | collective-permute-start | bytes 2506760 | tf_op jit(solution)/shard_map/ppermute | solution.py:911
  33.0 3.4 %collective-permute-start.3 = (f32[32,24,256]{2,1,0:T(8,128)S(1)}, f32[32,24,256]{2,1,0:T(8,128)S(1)}, u32[]{:S(2)}, u32[]{:S(2)}) collective-permute-start(f32[32,24,256]{2,1,0:T(8,128)S(1)} %get-tuple-element.25), channel_id=1, source_target_pairs={{1,0},{2,1},{3,2},{4,3},{5,4},{6,5},{7,6},{9,8},{10,9},{11,10},{12... | collective-permute-start | bytes 2359304 | tf_op jit(solution)/shard_map/ppermute | solution.py:911
  36.4 3.6 %all-to-all-done.1.refs_5_ = f32[8,3,48,128]{3,2,1,0:T(8,128)} async-done(((f32[8,3,48,128]{3,2,1,0:T(8,128)}), f32[8,3,48,128]{3,2,1,0:T(8,128)}, u32[]{:S(2)}, u32[]{:S(2)}) %all-to-all-start.1) | async-done | bytes 589856 | tf_op jit(solution)/shard_map/all_to_all | solution.py:933
  40.0 12.2 %marker_work.1 = (f32[8,6,8,256]{3,2,1,0:T(8,128)}, f32[8,3,48,128]{3,2,1,0:T(8,128)}) custom-call(s32[1,8]{1,0:T(1,128)S(1)} %copy-done.3, bf16[2,2,128,256]{3,2,1,0:T(8,128)(2,1)} %constant.4.clone.refs_0_, bf16[512,512]{1,0:T(8,128)(2,1)} %constant.5.clone.refs_1_, f32[8,3,6,8,256]{4,3,2,1,0:T(8,128)} %bitcast.9, f32[8,6,8,256]{3,2,1,0:T(8,128)} %bitcast.10, ...), custom_call_target="tpu_custom_call" | custom-call | flops 28750000128 | tf_op jit(solution)/shard_map/marker_work/pallas_call | solution.py:354
  52.2 10.5 %all-to-all-start.2 = ((f32[8,3,48,128]{3,2,1,0:T(8,128)}), f32[8,3,48,128]{3,2,1,0:T(8,128)}, u32[]{:S(2)}, u32[]{:S(2)}) async-start(f32[8,3,48,128]{3,2,1,0:T(8,128)} %get-tuple-element.21._), calls=%async_computation.2 | async-start | bytes 1179648 | tf_op jit(solution)/shard_map/all_to_all | solution.py:937
  62.7 10.3 %inner_sweeps.1 = (f32[4,5,2,192,128]{4,3,2,1,0:T(8,128)S(1)}, f32[4,5,2,192,128]{4,3,2,1,0:T(8,128)S(1)}, f32[2,5,2,192,128]{4,3,2,1,0:T(8,128)S(1)}) custom-call(f32[3,32,16,256]{3,2,1,0:T(8,128)} %vel.5, f32[32,16,256]{2,1,0:T(8,128)} %pres.3, f32[32,16,256]{2,1,0:T(8,128)} %visc_in.1, f32[32,16,256]{2,1,0:T(8,128)} %dens_in.1, ...), custom_call_target="tpu_custom_call" | custom-call | flops 28750000128 | tf_op jit(solution)/shard_map/inner_sweeps/pallas_call | solution.py:776
  73.0 4.7 %collective-permute-done.3.high_y = f32[32,24,256]{2,1,0:T(8,128)S(1)} collective-permute-done((f32[32,24,256]{2,1,0:T(8,128)S(1)}, f32[32,24,256]{2,1,0:T(8,128)S(1)}, u32[]{:S(2)}, u32[]{:S(2)}) %collective-permute-start.3) | collective-permute-done | bytes 786464 | tf_op jit(solution)/shard_map/ppermute | solution.py:911
  77.6 0.0 collective-permute-done.2.low_y
  77.6 8.1 %edge_sweeps.1 = (f32[3,32,16,256]{3,2,1,0:T(8,128)}, f32[32,16,256]{2,1,0:T(8,128)}) custom-call(f32[4,5,2,192,128]{4,3,2,1,0:T(8,128)S(1)} %get-tuple-element.22.even_in, f32[4,5,2,192,128]{4,3,2,1,0:T(8,128)S(1)} %get-tuple-element.23.odd_in, f32[2,5,2,192,128]{4,3,2,1,0:T(8,128)S(1)} %get-tuple-element.24.cells_in, ...), custom_call_target="tpu_custom_call" | custom-call | flops 1150000000 | tf_op jit(solution)/shard_map/edge_sweeps/pallas_call | solution.py:880
  85.7 0.0 all-to-all-done.2.moments_in
  85.7 7.1 %settle.1 = (f32[32,16,256]{2,1,0:T(8,128)}, f32[32,16,256]{2,1,0:T(8,128)}) custom-call(s32[8,48]{1,0:T(8,128)S(1)} %bitcast.7, f32[8,3,48,128]{3,2,1,0:T(8,128)} %all-to-all-done.2.moments_in, f32[32,16,256]{2,1,0:T(8,128)} %visc_in.1, f32[32,16,256]{2,1,0:T(8,128)} %dens_in.1), custom_call_target="tpu_custom_call" | custom-call | flops 8049999872 | tf_op jit(solution)/shard_map/settle/pallas_call | solution.py:455
  (5 shorter events, 0.0 us)
Async XLA Ops:
  0.6 13.9 %all-to-all-start = ((s32[8,1,48]{2,1,0:T(1,128)}), s32[8,1,48]{2,1,0:T(1,128)S(1)}, u32[]{:S(2)}, u32[]{:S(2)}) async-start(s32[8,1,48]{2,1,0:T(1,128)} %bitcast.8), calls=%async_computation | async-start | bytes 8192 | tf_op jit(solution)/shard_map/all_to_all | solution.py:925
  6.8 7.8 %copy-start = (f32[3,32,16,256]{3,2,1,0:T(8,128)S(1)}, f32[3,32,16,256]{3,2,1,0:T(8,128)}, u32[]{:S(2)}) copy-start(f32[3,32,16,256]{3,2,1,0:T(8,128)} %vel.5) | copy-start | bytes 4718596
  9.0 17.5 %collective-permute-start = (f32[6,4,16,256]{3,2,1,0:T(8,128)}, f32[6,4,16,256]{3,2,1,0:T(8,128)S(1)}, u32[]{:S(2)}, u32[]{:S(2)}) collective-permute-start(f32[6,4,16,256]{3,2,1,0:T(8,128)} %get-tuple-element.18), channel_id=1, source_target_pairs={{0,8},{8,16},{16,24},{1,9},{9,17},{17,25},{2,10},{10,18},{18,26},{... | collective-permute-start | bytes 1179656 | tf_op jit(solution)/shard_map/ppermute | solution.py:911
  10.9 15.6 %collective-permute-start.1 = (f32[6,4,16,256]{3,2,1,0:T(8,128)}, f32[6,4,16,256]{3,2,1,0:T(8,128)S(1)}, u32[]{:S(2)}, u32[]{:S(2)}) collective-permute-start(f32[6,4,16,256]{3,2,1,0:T(8,128)} %get-tuple-element.19), channel_id=1, source_target_pairs={{8,0},{16,8},{24,16},{9,1},{17,9},{25,17},{10,2},{18,10},{26,18},{... | collective-permute-start | bytes 1179656 | tf_op jit(solution)/shard_map/ppermute | solution.py:911
  20.5 19.5 %all-to-all-start.1 = ((f32[8,3,48,128]{3,2,1,0:T(8,128)}), f32[8,3,48,128]{3,2,1,0:T(8,128)}, u32[]{:S(2)}, u32[]{:S(2)}) async-start(f32[8,3,48,128]{3,2,1,0:T(8,128)} %pick_bricks.1), calls=%async_computation.1 | async-start | bytes 1179648 | tf_op jit(solution)/shard_map/all_to_all | solution.py:933
  26.5 13.5 %copy-start.3 = (s32[1,8]{1,0:T(1,128)S(1)}, s32[1,8]{1,0:T(1,128)}, u32[]{:S(2)}) copy-start(s32[1,8]{1,0:T(1,128)} %counts.1) | copy-start | bytes 100
  26.5 3.1 %copy-start.1 = (f32[6,4,16,256]{3,2,1,0:T(8,128)}, f32[6,4,16,256]{3,2,1,0:T(8,128)S(1)}, u32[]{:S(2)}) copy-start(f32[6,4,16,256]{3,2,1,0:T(8,128)S(1)} %collective-permute-done.low_x) | copy-start | bytes 1179652
  26.5 3.1 %copy-start.2 = (f32[6,4,16,256]{3,2,1,0:T(8,128)}, f32[6,4,16,256]{3,2,1,0:T(8,128)S(1)}, u32[]{:S(2)}) copy-start(f32[6,4,16,256]{3,2,1,0:T(8,128)S(1)} %collective-permute-done.1.high_x) | copy-start | bytes 1179652
  29.6 48.0 %collective-permute-start.2 = (f32[34,24,256]{2,1,0:T(8,128)S(1)}, f32[34,24,256]{2,1,0:T(8,128)S(1)}, u32[]{:S(2)}, u32[]{:S(2)}) collective-permute-start(f32[34,24,256]{2,1,0:T(8,128)S(1)} %get-tuple-element.20.refs_6_), channel_id=1, source_target_pairs={{0,1},{1,2},{2,3},{3,4},{4,5},{5,6},{6,7},{8,9},{9,10},{10,11},{11... | collective-permute-start | bytes 2506760 | tf_op jit(solution)/shard_map/ppermute | solution.py:911
  33.0 44.6 %collective-permute-start.3 = (f32[32,24,256]{2,1,0:T(8,128)S(1)}, f32[32,24,256]{2,1,0:T(8,128)S(1)}, u32[]{:S(2)}, u32[]{:S(2)}) collective-permute-start(f32[32,24,256]{2,1,0:T(8,128)S(1)} %get-tuple-element.25), channel_id=1, source_target_pairs={{1,0},{2,1},{3,2},{4,3},{5,4},{6,5},{7,6},{9,8},{10,9},{11,10},{12... | collective-permute-start | bytes 2359304 | tf_op jit(solution)/shard_map/ppermute | solution.py:911
  52.2 33.5 %all-to-all-start.2 = ((f32[8,3,48,128]{3,2,1,0:T(8,128)}), f32[8,3,48,128]{3,2,1,0:T(8,128)}, u32[]{:S(2)}, u32[]{:S(2)}) async-start(f32[8,3,48,128]{3,2,1,0:T(8,128)} %get-tuple-element.21._), calls=%async_computation.2 | async-start | bytes 1179648 | tf_op jit(solution)/shard_map/all_to_all | solution.py:937

commit v7 on v6

--- a/solution.py
+++ b/solution.py
@@ -43,7 +43,7 @@
     return lax.shift_right_logical(brick, GROUP.bit_length() - 1), (brick & (GROUP - 1)) * BZ
 
 
-def pick_body(asked, vel, out, table):
+def pick_body(asked, vel, far, out, table, sent):
     size_x, size_y, size_z = vel.shape[1:]
     bricks_y, halves = size_y // BY, size_z // LANES
 
@@ -66,17 +66,32 @@
     groups = out.shape[1]
     lane_slot = lax.broadcasted_iota(jnp.int32, (ROWS, LANES), 1) // BZ
 
-    def one_group(step, carry):
-        device, group = step // groups, step % groups
+    def one_group(device, group):
         packed = jnp.zeros((ROWS, LANES), f32)
         for slot in range(GROUP):
             place, lane = place_of(asked[device, group * GROUP + slot])
             rolled = pltpu.roll(table[place], (BZ * slot - lane) & (LANES - 1), 1)
             packed = jnp.where(lane_slot == slot, rolled, packed)
         out[device, group] = packed
+
+    def send(device):
+        return pltpu.make_async_copy(out.at[device], far.at[device], sent.at[device])
+
+    def one_device(device, carry):
+        def each(group, inner):
+            one_group(device, group)
+            return inner
+
+        lax.fori_loop(0, groups, each, 0)
+        send(device).start()
         return carry
 
-    lax.fori_loop(0, out.shape[0] * groups, one_group, 0)
+    def drain(device, carry):
+        send(device).wait()
+        return carry
+
+    lax.fori_loop(0, out.shape[0], one_device, 0)
+    lax.fori_loop(0, out.shape[0], drain, 0)
 
 
 def pick_bricks(asked, velocity):
@@ -90,8 +105,12 @@
             pl.BlockSpec(memory_space=pltpu.SMEM),
             pl.BlockSpec(memory_space=pltpu.VMEM),
         ],
-        out_specs=pl.BlockSpec(memory_space=pltpu.VMEM),
-        scratch_shapes=[pltpu.VMEM((places, ROWS, LANES), f32)],
+        out_specs=pl.BlockSpec(memory_space=pl.ANY),
+        scratch_shapes=[
+            pltpu.VMEM((devices, slots // GROUP, ROWS, LANES), f32),
+            pltpu.VMEM((places, ROWS, LANES), f32),
+            pltpu.SemaphoreType.DMA((devices,)),
+        ],
         compiler_params=vmem_limit(24),
         cost_estimate=cost(25),
         name="pick_bricks",
@@ -634,12 +653,12 @@
                 up_z(here),
                 down_z(here),
             ]
-            links = [0.5 * (here + other) for other in near]
+            links = [here + other for other in near]
             scale = jnp.where(here > 0.0, RELAX / add_all(links), 0.0)
             for n in range(6):
                 coefs[n, plane, tile(y), :] = links[n] * scale
-            relax[plane, tile(y), :] = scale
-            forcing[plane, tile(y), :] = take(dens, plane, y) * (-GRAVITY * scale)
+            relax[plane, tile(y), :] = 2.0 * scale
+            forcing[plane, tile(y), :] = take(dens, plane, y) * (-2.0 * GRAVITY * scale)
             rate[plane, tile(y), :] = PRESSURE_RATE * here
 
     def sweep(y, old, new):
@@ -852,7 +871,7 @@
             sweep(width + size_y - 1 - step + n, old, new)
             return carry
 
-        lax.fori_loop(0, width, sweep_rows, 0)
+        lax.fori_loop(0, width, sweep_rows, 0, unroll=2)
 
     final = odd if SWEEPS % 2 else even
     outs = [vel_out.at[0], vel_out.at[1], vel_out.at[2], pres_out]

time: 93.3 us -> 92.7 us (level)
  starting transfers between devices: 35 us -> 33 us
  Pallas kernels: 48.8 us -> 50.2 us
    pallas_call x1, Pallas kernels: 12.2 us -> 14.4 us  [marker_work(): pl.pallas_call(marker_body, out_shape=tuple((jax.ShapeDtypeStruct(shape,...]
    all_to_all x1, starting transfers between devices: 10.5 us -> 8.56 us  [per_device(): gathered = lax.all_to_all(moments, 'mark', 0, 0, tiled=True)]
  transfers between devices with their start and end apart: 7 -> 7, of which waited for: 2 -> 2; matrix products, arithmetic and copies ran while one was open for 0% -> 0% of each run, Pallas kernels for 45% -> 47%
where the time goes in v7:
time: 92.7 us; the launch traced here: 92.1 us
  Pallas kernels  50.2 us (54%)
  starting transfers between devices  33 us (36%)
  waiting for transfers between devices  8.11 us (9%)
    pallas_call x1, Pallas kernels, marker_work(): pl.pallas_call(marker_body, out_shape=tuple((jax.ShapeDtypeStruct(shape,...  14.4 us
    ppermute x4, starting transfers between devices, shift(): return lax.ppermute(value, axis, pairs)  12.3 us
    pallas_call x1, Pallas kernels, inner_sweeps(): pl.pallas_call(inner_body, out_shape=tuple((jax.ShapeDtypeStruct(shape, f...  10.2 us
    all_to_all x1, starting transfers between devices, per_device(): gathered = lax.all_to_all(moments, 'mark', 0, 0, tiled=True)  8.56 us
    pallas_call x1, Pallas kernels, edge_sweeps(): pl.pallas_call(edge_body, out_shape=(jax.ShapeDtypeStruct((3, size_x, siz...  7.62 us
    pallas_call x1, Pallas kernels, settle(): pl.pallas_call(settle_body, out_shape=(shape, shape), in_specs=[pl.BlockS...  7.08 us
    all_to_all x1, starting transfers between devices, per_device(): asked = lax.all_to_all(block_brick, 'mark', 0, 0, tiled=True)  6.18 us
    all_to_all x1, starting transfers between devices, per_device(): bricks = lax.all_to_all(picked, 'mark', 0, 0, tiled=True)  6.01 us
  transfers between devices with their start and end apart: 7, of which 2 were waited for; matrix products, arithmetic and copies ran while one was open for 0% of the time, Pallas kernels for 47%

profile of v7, /device:TPU:18, one launch (start us, length us, event | category | flops | bytes accessed | tf_op | source)
XLA Modules:
  0.0 92.1 jit_solution(3212080807470662470)
XLA Ops:
  0.6 6.2 %all-to-all-start = ((s32[8,1,48]{2,1,0:T(1,128)}), s32[8,1,48]{2,1,0:T(1,128)S(1)}, u32[]{:S(2)}, u32[]{:S(2)}) async-start(s32[8,1,48]{2,1,0:T(1,128)} %bitcast.8), calls=%async_computation | async-start | bytes 8192 | tf_op jit(solution)/shard_map/all_to_all | solution.py:944
  6.8 2.2 %pack_x.1 = (f32[6,4,16,256]{3,2,1,0:T(8,128)}, f32[6,4,16,256]{3,2,1,0:T(8,128)}) custom-call(f32[3,32,16,256]{3,2,1,0:T(8,128)} %vel.5, f32[3,32,16,256]{3,2,1,0:T(8,128)} %vel.5, f32[32,16,256]{2,1,0:T(8,128)} %pres.3, f32[32,16,256]{2,1,0:T(8,128)} %pres.3, f32[32,16,256]{2,1,0:T(8,128)} %visc_in.1, f32[32,16,256]{2,1,0:T(8,128)} %visc_in.1, ...), custom_call_target="tpu_custom_call" | custom-call | flops 2300000000 | tf_op jit(solution)/shard_map/pack_x/pallas_call | solution.py:517
  9.0 1.9 %collective-permute-start = (f32[6,4,16,256]{3,2,1,0:T(8,128)}, f32[6,4,16,256]{3,2,1,0:T(8,128)S(1)}, u32[]{:S(2)}, u32[]{:S(2)}) collective-permute-start(f32[6,4,16,256]{3,2,1,0:T(8,128)} %get-tuple-element.18), channel_id=1, source_target_pairs={{0,8},{8,16},{16,24},{1,9},{9,17},{17,25},{2,10},{10,18},{18,26},{... | collective-permute-start | bytes 1179656 | tf_op jit(solution)/shard_map/ppermute | solution.py:930
  10.9 3.6 %collective-permute-start.1 = (f32[6,4,16,256]{3,2,1,0:T(8,128)}, f32[6,4,16,256]{3,2,1,0:T(8,128)S(1)}, u32[]{:S(2)}, u32[]{:S(2)}) collective-permute-start(f32[6,4,16,256]{3,2,1,0:T(8,128)} %get-tuple-element.19), channel_id=1, source_target_pairs={{8,0},{16,8},{24,16},{9,1},{17,9},{25,17},{10,2},{18,10},{26,18},{... | collective-permute-start | bytes 1179656 | tf_op jit(solution)/shard_map/ppermute | solution.py:930
  14.5 0.0 all-to-all-done
  14.6 0.0 copy-done
  14.6 5.7 %pick_bricks.1 = f32[8,3,48,128]{3,2,1,0:T(8,128)} custom-call(s32[8,48]{1,0:T(8,128)S(1)} %bitcast.6, f32[3,32,16,256]{3,2,1,0:T(8,128)S(1)} %copy-done), custom_call_target="tpu_custom_call" | custom-call | flops 28750000128 | tf_op jit(solution)/shard_map/pick_bricks/pallas_call | solution.py:101
  20.3 6.0 %all-to-all-start.1 = ((f32[8,3,48,128]{3,2,1,0:T(8,128)}), f32[8,3,48,128]{3,2,1,0:T(8,128)}, u32[]{:S(2)}, u32[]{:S(2)}) async-start(f32[8,3,48,128]{3,2,1,0:T(8,128)} %pick_bricks.1), calls=%async_computation.1 | async-start | bytes 1179648 | tf_op jit(solution)/shard_map/all_to_all | solution.py:952
  26.3 0.0 collective-permute-done.low_x
  26.3 0.0 copy-start.1
  26.3 0.0 collective-permute-done.1.high_x
  26.3 0.0 copy-start.2
  26.3 3.0 %pack_y.1 = (f32[34,24,256]{2,1,0:T(8,128)S(1)}, f32[32,24,256]{2,1,0:T(8,128)S(1)}) custom-call(f32[3,32,16,256]{3,2,1,0:T(8,128)} %vel.5, f32[32,16,256]{2,1,0:T(8,128)} %pres.3, f32[32,16,256]{2,1,0:T(8,128)} %visc_in.1, f32[32,16,256]{2,1,0:T(8,128)} %dens_in.1, f32[6,4,16,256]{3,2,1,0:T(8,128)S(1)} %collective-permute-done.low_x, ...), custom_call_target="tpu_custom_call" | custom-call | flops 17250000896 | tf_op jit(solution)/shard_map/pack_y/pallas_call | solution.py:571
  29.4 3.4 %collective-permute-start.2 = (f32[34,24,256]{2,1,0:T(8,128)S(1)}, f32[34,24,256]{2,1,0:T(8,128)S(1)}, u32[]{:S(2)}, u32[]{:S(2)}) collective-permute-start(f32[34,24,256]{2,1,0:T(8,128)S(1)} %get-tuple-element.20.refs_6_), channel_id=1, source_target_pairs={{0,1},{1,2},{2,3},{3,4},{4,5},{5,6},{6,7},{8,9},{9,10},{10,11},{11... | collective-permute-start | bytes 2506760 | tf_op jit(solution)/shard_map/ppermute | solution.py:930
  32.8 3.4 %collective-permute-start.3 = (f32[32,24,256]{2,1,0:T(8,128)S(1)}, f32[32,24,256]{2,1,0:T(8,128)S(1)}, u32[]{:S(2)}, u32[]{:S(2)}) collective-permute-start(f32[32,24,256]{2,1,0:T(8,128)S(1)} %get-tuple-element.25), channel_id=1, source_target_pairs={{1,0},{2,1},{3,2},{4,3},{5,4},{6,5},{7,6},{9,8},{10,9},{11,10},{12... | collective-permute-start | bytes 2359304 | tf_op jit(solution)/shard_map/ppermute | solution.py:930
  36.1 3.6 %all-to-all-done.1.refs_5_ = f32[8,3,48,128]{3,2,1,0:T(8,128)} async-done(((f32[8,3,48,128]{3,2,1,0:T(8,128)}), f32[8,3,48,128]{3,2,1,0:T(8,128)}, u32[]{:S(2)}, u32[]{:S(2)}) %all-to-all-start.1) | async-done | bytes 589856 | tf_op jit(solution)/shard_map/all_to_all | solution.py:952
  39.8 14.4 %marker_work.1 = (f32[8,6,8,256]{3,2,1,0:T(8,128)}, f32[8,3,48,128]{3,2,1,0:T(8,128)}) custom-call(s32[1,8]{1,0:T(1,128)S(1)} %copy-done.3, bf16[2,2,128,256]{3,2,1,0:T(8,128)(2,1)} %constant.4.clone.refs_0_, bf16[512,512]{1,0:T(8,128)(2,1)} %constant.5.clone.refs_1_, f32[8,3,6,8,256]{4,3,2,1,0:T(8,128)} %bitcast.9, f32[8,6,8,256]{3,2,1,0:T(8,128)} %bitcast.10, ...), custom_call_target="tpu_custom_call" | custom-call | flops 28750000128 | tf_op jit(solution)/shard_map/marker_work/pallas_call | solution.py:373
  54.1 8.6 %all-to-all-start.2 = ((f32[8,3,48,128]{3,2,1,0:T(8,128)}), f32[8,3,48,128]{3,2,1,0:T(8,128)}, u32[]{:S(2)}, u32[]{:S(2)}) async-start(f32[8,3,48,128]{3,2,1,0:T(8,128)} %get-tuple-element.21._), calls=%async_computation.2 | async-start | bytes 1179648 | tf_op jit(solution)/shard_map/all_to_all | solution.py:956
  62.7 10.2 %inner_sweeps.1 = (f32[4,5,2,192,128]{4,3,2,1,0:T(8,128)S(1)}, f32[4,5,2,192,128]{4,3,2,1,0:T(8,128)S(1)}, f32[2,5,2,192,128]{4,3,2,1,0:T(8,128)S(1)}) custom-call(f32[3,32,16,256]{3,2,1,0:T(8,128)} %vel.5, f32[32,16,256]{2,1,0:T(8,128)} %pres.3, f32[32,16,256]{2,1,0:T(8,128)} %visc_in.1, f32[32,16,256]{2,1,0:T(8,128)} %dens_in.1, ...), custom_call_target="tpu_custom_call" | custom-call | flops 28750000128 | tf_op jit(solution)/shard_map/inner_sweeps/pallas_call | solution.py:795
  72.9 4.5 %collective-permute-done.3.high_y = f32[32,24,256]{2,1,0:T(8,128)S(1)} collective-permute-done((f32[32,24,256]{2,1,0:T(8,128)S(1)}, f32[32,24,256]{2,1,0:T(8,128)S(1)}, u32[]{:S(2)}, u32[]{:S(2)}) %collective-permute-start.3) | collective-permute-done | bytes 786464 | tf_op jit(solution)/shard_map/ppermute | solution.py:930
  77.4 0.0 collective-permute-done.2.low_y
  77.4 7.6 %edge_sweeps.1 = (f32[3,32,16,256]{3,2,1,0:T(8,128)}, f32[32,16,256]{2,1,0:T(8,128)}) custom-call(f32[4,5,2,192,128]{4,3,2,1,0:T(8,128)S(1)} %get-tuple-element.22.even_in, f32[4,5,2,192,128]{4,3,2,1,0:T(8,128)S(1)} %get-tuple-element.23.odd_in, f32[2,5,2,192,128]{4,3,2,1,0:T(8,128)S(1)} %get-tuple-element.24.cells_in, ...), custom_call_target="tpu_custom_call" | custom-call | flops 1150000000 | tf_op jit(solution)/shard_map/edge_sweeps/pallas_call | solution.py:899
  85.0 0.0 all-to-all-done.2.moments_in
  85.0 7.1 %settle.1 = (f32[32,16,256]{2,1,0:T(8,128)}, f32[32,16,256]{2,1,0:T(8,128)}) custom-call(s32[8,48]{1,0:T(8,128)S(1)} %bitcast.7, f32[8,3,48,128]{3,2,1,0:T(8,128)} %all-to-all-done.2.moments_in, f32[32,16,256]{2,1,0:T(8,128)} %visc_in.1, f32[32,16,256]{2,1,0:T(8,128)} %dens_in.1), custom_call_target="tpu_custom_call" | custom-call | flops 8049999872 | tf_op jit(solution)/shard_map/settle/pallas_call | solution.py:474
  (5 shorter events, 0.0 us)
Async XLA Ops:
  0.6 13.9 %all-to-all-start = ((s32[8,1,48]{2,1,0:T(1,128)}), s32[8,1,48]{2,1,0:T(1,128)S(1)}, u32[]{:S(2)}, u32[]{:S(2)}) async-start(s32[8,1,48]{2,1,0:T(1,128)} %bitcast.8), calls=%async_computation | async-start | bytes 8192 | tf_op jit(solution)/shard_map/all_to_all | solution.py:944
  6.8 7.8 %copy-start = (f32[3,32,16,256]{3,2,1,0:T(8,128)S(1)}, f32[3,32,16,256]{3,2,1,0:T(8,128)}, u32[]{:S(2)}) copy-start(f32[3,32,16,256]{3,2,1,0:T(8,128)} %vel.5) | copy-start | bytes 4718596
  9.0 17.3 %collective-permute-start = (f32[6,4,16,256]{3,2,1,0:T(8,128)}, f32[6,4,16,256]{3,2,1,0:T(8,128)S(1)}, u32[]{:S(2)}, u32[]{:S(2)}) collective-permute-start(f32[6,4,16,256]{3,2,1,0:T(8,128)} %get-tuple-element.18), channel_id=1, source_target_pairs={{0,8},{8,16},{16,24},{1,9},{9,17},{17,25},{2,10},{10,18},{18,26},{... | collective-permute-start | bytes 1179656 | tf_op jit(solution)/shard_map/ppermute | solution.py:930
  10.9 15.4 %collective-permute-start.1 = (f32[6,4,16,256]{3,2,1,0:T(8,128)}, f32[6,4,16,256]{3,2,1,0:T(8,128)S(1)}, u32[]{:S(2)}, u32[]{:S(2)}) collective-permute-start(f32[6,4,16,256]{3,2,1,0:T(8,128)} %get-tuple-element.19), channel_id=1, source_target_pairs={{8,0},{16,8},{24,16},{9,1},{17,9},{25,17},{10,2},{18,10},{26,18},{... | collective-permute-start | bytes 1179656 | tf_op jit(solution)/shard_map/ppermute | solution.py:930
  20.3 19.5 %all-to-all-start.1 = ((f32[8,3,48,128]{3,2,1,0:T(8,128)}), f32[8,3,48,128]{3,2,1,0:T(8,128)}, u32[]{:S(2)}, u32[]{:S(2)}) async-start(f32[8,3,48,128]{3,2,1,0:T(8,128)} %pick_bricks.1), calls=%async_computation.1 | async-start | bytes 1179648 | tf_op jit(solution)/shard_map/all_to_all | solution.py:952
  26.3 13.5 %copy-start.3 = (s32[1,8]{1,0:T(1,128)S(1)}, s32[1,8]{1,0:T(1,128)}, u32[]{:S(2)}) copy-start(s32[1,8]{1,0:T(1,128)} %counts.1) | copy-start | bytes 100
  26.3 3.1 %copy-start.1 = (f32[6,4,16,256]{3,2,1,0:T(8,128)}, f32[6,4,16,256]{3,2,1,0:T(8,128)S(1)}, u32[]{:S(2)}) copy-start(f32[6,4,16,256]{3,2,1,0:T(8,128)S(1)} %collective-permute-done.low_x) | copy-start | bytes 1179652
  26.3 3.1 %copy-start.2 = (f32[6,4,16,256]{3,2,1,0:T(8,128)}, f32[6,4,16,256]{3,2,1,0:T(8,128)S(1)}, u32[]{:S(2)}) copy-start(f32[6,4,16,256]{3,2,1,0:T(8,128)S(1)} %collective-permute-done.1.high_x) | copy-start | bytes 1179652
  29.4 48.0 %collective-permute-start.2 = (f32[34,24,256]{2,1,0:T(8,128)S(1)}, f32[34,24,256]{2,1,0:T(8,128)S(1)}, u32[]{:S(2)}, u32[]{:S(2)}) collective-permute-start(f32[34,24,256]{2,1,0:T(8,128)S(1)} %get-tuple-element.20.refs_6_), channel_id=1, source_target_pairs={{0,1},{1,2},{2,3},{3,4},{4,5},{5,6},{6,7},{8,9},{9,10},{10,11},{11... | collective-permute-start | bytes 2506760 | tf_op jit(solution)/shard_map/ppermute | solution.py:930
  32.8 44.6 %collective-permute-start.3 = (f32[32,24,256]{2,1,0:T(8,128)S(1)}, f32[32,24,256]{2,1,0:T(8,128)S(1)}, u32[]{:S(2)}, u32[]{:S(2)}) collective-permute-start(f32[32,24,256]{2,1,0:T(8,128)S(1)} %get-tuple-element.25), channel_id=1, source_target_pairs={{1,0},{2,1},{3,2},{4,3},{5,4},{6,5},{7,6},{9,8},{10,9},{11,10},{12... | collective-permute-start | bytes 2359304 | tf_op jit(solution)/shard_map/ppermute | solution.py:930
  54.1 30.9 %all-to-all-start.2 = ((f32[8,3,48,128]{3,2,1,0:T(8,128)}), f32[8,3,48,128]{3,2,1,0:T(8,128)}, u32[]{:S(2)}, u32[]{:S(2)}) async-start(f32[8,3,48,128]{3,2,1,0:T(8,128)} %get-tuple-element.21._), calls=%async_computation.2 | async-start | bytes 1179648 | tf_op jit(solution)/shard_map/all_to_all | solution.py:956
